TPU v7x, 128 devices: a whole 4x4x4 slice. The times are simulated.
128 devices in a mesh: ctx: 16 (over y_hi, z, core), wsh: 8 (over y_lo, x).
Axes of the slice: x: 4, y: 4 (y_hi: 2, y_lo: 2; y = y_hi * 2 + y_lo), z: 4, core: 2. Of those that a mesh axis runs over, the one named last changes fastest.
Arguments:
- tokens: bfloat16 [8, 2048, 768], P('wsh', 'ctx'), may hold values from -6 to 6
- gain_attn: float32 [768], replicated, may hold values from 0.1 to 1.9
- w_qkv: bfloat16 [768, 2304], replicated, may hold values from -0.21875 to 0.21875
- rel_bias: float32 [32, 12], replicated, may hold values from -4 to 4
- w_attn_out: bfloat16 [768, 768], replicated, may hold values from -2.5 to 2.5
- gain_ffn: float32 [768], replicated, may hold values from 0.1 to 1.9
- w_router: bfloat16 [768, 32], replicated, may hold values from -0.15625 to 0.15625
- w_in: bfloat16 [32, 768, 3072], P('ctx', None, 'wsh'), may hold values from -0.21875 to 0.21875
- w_out: bfloat16 [32, 3072, 768], P('ctx', 'wsh'), may hold values from -0.109375 to 0.109375
- routes: int32 [8, 2048, 2], P('wsh', 'ctx'), may hold values from 0 to 31, all different within a row; in each aligned block of 128 rows (0 to 127, 128 to 255, ..., all dimensions but the last counted through in order) at most 16 rows name the same one
- pair_order: int32 [16], replicated, may hold values from 0 to 15, each once
- bucket_table: int32 [2048], replicated, may hold values from 0 to 31, as said below
- cotangent: bfloat16 [8, 2048, 768], P('wsh', 'ctx'), may hold values from -6 to 6
Outputs:
- layer_out: bfloat16 [8, 2048, 768], P('wsh', 'ctx')
- grad_tokens: float32 [8, 2048, 768], P('wsh', 'ctx')
- grad_gain_attn: float32 [768], replicated
- grad_w_qkv: float32 [768, 2304], replicated
- grad_rel_bias: float32 [32, 12], replicated
- grad_w_attn_out: float32 [768, 768], replicated
- grad_gain_ffn: float32 [768], replicated
- grad_w_router: float32 [768, 32], replicated
- grad_w_in: float32 [32, 768, 3072], P('ctx', None, 'wsh')
- grad_w_out: float32 [32, 3072, 768], P('ctx', 'wsh')
Inputs may be any that keep to these rules, and one draw needn't show every extreme that they name: `routes`: each row names two different experts; among the rows of one device no expert is named more than 16 times, a bound that some block reaches. `pair_order`: each index appears once. `bucket_table`: never falls as the distance grows; equals the distance below 16 and is 31 at the largest distance.
All inputs are finite; a program needn't handle non-finite values.
Results may differ from a plain program's by a relative error of at most 0.017.
Values may be sent and summed in bfloat16 or wider, within the bound.
No kernel may reach another device: no remote copies, remote signals or barrier semaphores. Data moves between devices by JAX's collectives and lax.ppermute only.
A program may use at most 192 MiB of HBM per device.

v0:
```python
import functools

import jax
import jax.numpy as jnp
from jax import lax
from jax.experimental import pallas as pl
from jax.experimental.pallas import tpu as pltpu
from jax.sharding import Mesh
from jax.sharding import PartitionSpec as P

BF = jnp.bfloat16
F32 = jnp.float32
EPSILON = 1e-06
HIGHEST = lax.Precision.HIGHEST
MASKED = -1e30
ROWS = (((0,), (0,)), ((), ()))
COLS = (((1,), (1,)), ((), ()))
LANES = 128
VMEM_LIMIT = 44 * 1024 * 1024
SPLIT = (2, 4, 2, 2, 4)
EVERY = ("ya", "z", "core", "yb", "x")
CTX = ("ya", "z", "core")
WSH = ("yb", "x")
SAME_CORE = ("ya", "z")
CHIPS = ("ya", "z", "yb", "x")
EXPERT_AXES = ("ya", "z", "core", "yb")
SWAP = ((0, 1), (1, 0))


def norm_scale(values):
    return lax.rsqrt(jnp.mean(values * values, axis=-1, keepdims=True) + EPSILON)


def norm_backward(values, scale_vector, gain_vector, upstream):
    weighted = upstream * gain_vector
    inner_mean = jnp.mean(weighted * values, axis=-1, keepdims=True)
    grad_input = (
        scale_vector * weighted - values * scale_vector * scale_vector * scale_vector * inner_mean
    )
    grad_gain = jnp.sum(upstream * values * scale_vector, axis=0)
    return (grad_input, grad_gain)


def contract_rows(left_matrix, right_matrix):
    return lax.dot_general(left_matrix, right_matrix, ROWS, preferred_element_type=F32)


def contract_cols(left_matrix, right_matrix):
    return lax.dot_general(left_matrix, right_matrix, COLS, preferred_element_type=F32)


def exchange(array, axes):
    return lax.all_to_all(array, axes, split_axis=0, concat_axis=0, tiled=True)


def spread(array, axes):
    return exchange(jnp.broadcast_to(array[None], (lax.axis_size(axes), *array.shape)), axes)


def sum_halves(kept, given):
    rows, columns = kept.shape
    chips = lax.axis_size(CHIPS)
    got = lax.ppermute(given, "core", SWAP)
    half = (kept.astype(F32) + got.astype(F32)).astype(BF).reshape(chips, rows // chips, columns)
    share = jnp.sum(exchange(half, CHIPS).astype(F32), axis=0).astype(BF)
    mine = spread(share, CHIPS).reshape(rows, columns)
    return mine, lax.ppermute(mine, "core", SWAP)


def shear(tile, rows):
    while rows > 8:
        half = rows // 2
        tile = pltpu.roll(tile[:half], half, axis=1) + tile[half:]
        rows = half
    total = tile[rows - 1 : rows]
    for row in range(rows - 1):
        total = total + pltpu.roll(tile[row : row + 1], rows - 1 - row, axis=1)
    return total


def head_lanes(array, head):
    lanes = lax.broadcasted_iota(jnp.int32, array.shape, 1) // (LANES // 2)
    return jnp.where(lanes == head, array.astype(F32), 0.0)


def attend_kernel(q_ref, k_ref, v_ref, window_ref, out_ref, prob_ref):
    half, seq = q_ref.shape[0] // 2, k_ref.shape[0]
    window = seq + 2 * half
    total_out = None
    for head in range(2):
        q = (head_lanes(q_ref[...], head) * (LANES // 2) ** -0.5).astype(BF)
        raw = lax.dot_general(q, k_ref[...], COLS, preferred_element_type=F32)
        parts = []
        for part in range(2):
            row = 2 * head + part
            tile = jnp.broadcast_to(window_ref[row : row + 1, :], (half, window))
            tile = pltpu.roll(tile, window - half + 1, axis=1, stride=1, stride_axis=0)
            parts.append(raw[part * half : (part + 1) * half] + tile[:, :seq])
        scores = jnp.concatenate(parts, axis=0)
        exps = jnp.exp(scores - jnp.max(scores, axis=1, keepdims=True))
        prob = (exps * (1.0 / jnp.sum(exps, axis=1, keepdims=True))).astype(BF)
        prob_ref[head] = prob
        out = head_lanes(jnp.dot(prob, v_ref[...], preferred_element_type=F32), head)
        total_out = out if total_out is None else total_out + out
    out_ref[...] = total_out.astype(BF)


def attend(queries, key_value, windows):
    rows, width = queries.shape
    seq = key_value.shape[0]
    pairs = width // LANES
    work = rows * seq * width
    return pl.pallas_call(
        attend_kernel,
        grid=(pairs,),
        in_specs=[
            pl.BlockSpec((rows, LANES), lambda h: (0, h)),
            pl.BlockSpec((seq, LANES), lambda h: (0, h)),
            pl.BlockSpec((seq, LANES), lambda h: (0, pairs + h)),
            pl.BlockSpec((None, 4, windows.shape[2]), lambda h: (h, 0, 0)),
        ],
        out_specs=[
            pl.BlockSpec((rows, LANES), lambda h: (0, h)),
            pl.BlockSpec((2, rows, seq), lambda h: (h, 0, 0)),
        ],
        out_shape=[
            jax.ShapeDtypeStruct((rows, width), BF),
            jax.ShapeDtypeStruct((2 * pairs, rows, seq), BF),
        ],
        compiler_params=pltpu.CompilerParams(vmem_limit_bytes=VMEM_LIMIT),
        cost_estimate=pl.CostEstimate(
            flops=8 * work,
            bytes_accessed=4 * seq * width + 4 * pairs * rows * seq,
            transcendentals=2 * pairs * rows * seq,
        ),
        name="attend",
    )(queries, key_value, key_value, windows)


def attend_back_kernel(
    prob_ref, q_ref, k_ref, v_ref, grad_ref, dq_ref, dkv_ref, diag_ref, dv_kept
):
    half, seq = q_ref.shape[0] // 2, k_ref.shape[0]

    @pl.when(pl.program_id(1) == 0)
    def _():
        factor = (LANES // 2) ** -0.5
        query_grad = None
        qs, score_grads, grads, probs = [], [], [], []
        for head in range(2):
            q = (head_lanes(q_ref[...], head) * factor).astype(BF)
            grad = head_lanes(grad_ref[...], head).astype(BF)
            prob = prob_ref[head]
            wide = prob.astype(F32)
            prob_grad = lax.dot_general(grad, v_ref[...], COLS, preferred_element_type=F32)
            inner = jnp.sum(wide * prob_grad, axis=1, keepdims=True)
            score_grad = wide * (prob_grad - inner)
            for part in range(2):
                row = 2 * head + part
                tile = score_grad[part * half : (part + 1) * half]
                tile = jnp.concatenate([tile, jnp.zeros((half, 2 * half), F32)], axis=1)
                diag_ref[row : row + 1, :] = shear(tile, half)
            score_grad = score_grad.astype(BF)
            out = jnp.dot(score_grad, k_ref[...], preferred_element_type=F32) * factor
            out = head_lanes(out, head)
            query_grad = out if query_grad is None else query_grad + out
            qs.append(q)
            score_grads.append(score_grad)
            grads.append(grad)
            probs.append(prob)
        dq_ref[...] = query_grad.astype(BF)
        joined = functools.partial(jnp.concatenate, axis=0)
        dk = lax.dot_general(joined(score_grads), joined(qs), ROWS, preferred_element_type=F32)
        dkv_ref[...] = dk.astype(BF)
        dv = lax.dot_general(joined(probs), joined(grads), ROWS, preferred_element_type=F32)
        dv_kept[...] = dv.astype(BF)

    @pl.when(pl.program_id(1) == 1)
    def _():
        dkv_ref[...] = dv_kept[...]


def attend_back(prob, queries, key_value, attended_grad):
    rows, width = queries.shape
    seq = key_value.shape[0]
    pairs = width // LANES
    window = seq + rows
    return pl.pallas_call(
        attend_back_kernel,
        grid=(pairs, 2),
        in_specs=[
            pl.BlockSpec((2, rows, seq), lambda h, j: (h, 0, 0)),
            pl.BlockSpec((rows, LANES), lambda h, j: (0, h)),
            pl.BlockSpec((seq, LANES), lambda h, j: (0, h)),
            pl.BlockSpec((seq, LANES), lambda h, j: (0, pairs + h)),
            pl.BlockSpec((rows, LANES), lambda h, j: (0, h)),
        ],
        out_specs=[
            pl.BlockSpec((rows, LANES), lambda h, j: (0, h)),
            pl.BlockSpec((seq, LANES), lambda h, j: (0, h + pairs * j)),
            pl.BlockSpec((None, 4, window), lambda h, j: (h, 0, 0)),
        ],
        scratch_shapes=[pltpu.VMEM((seq, LANES), BF)],
        out_shape=[
            jax.ShapeDtypeStruct((rows, width), BF),
            jax.ShapeDtypeStruct((seq, 2 * width), BF),
            jax.ShapeDtypeStruct((pairs, 4, window), F32),
        ],
        compiler_params=pltpu.CompilerParams(vmem_limit_bytes=VMEM_LIMIT),
        cost_estimate=pl.CostEstimate(
            flops=16 * rows * seq * width,
            bytes_accessed=8 * seq * width + 4 * pairs * rows * seq,
            transcendentals=0,
        ),
        name="attend_back",
    )(prob, queries, key_value, key_value, attended_grad)


def key_value_kernel(place_ref, near_ref, far_ref, gain_ref, wk_ref, wv_ref, normed_ref, kv_ref, *, half):
    tile = normed_ref.shape[0] // half
    near_blocks = near_ref.shape[0] // half
    rows = []
    for block in range(tile):
        source = place_ref[pl.program_id(0) * tile + block]
        at = pl.ds(pl.multiple_of(lax.rem(source, near_blocks) * half, half), half)
        rows.append(jnp.where(source < near_blocks, near_ref[at].astype(F32), far_ref[at].astype(F32)))
    inputs = jnp.concatenate(rows, axis=0)
    normed = (inputs * norm_scale(inputs) * gain_ref[...]).astype(BF)
    normed_ref[...] = normed
    width = normed.shape[1]
    kv_ref[:, :width] = jnp.dot(normed, wk_ref[...], preferred_element_type=F32).astype(BF)
    kv_ref[:, width:] = jnp.dot(normed, wv_ref[...], preferred_element_type=F32).astype(BF)


def keys_and_values(place, near, far, gain, w_qkv, half):
    near_rows, width = near.shape
    seq = 2 * near_rows
    tile = 4 * half
    return pl.pallas_call(
        functools.partial(key_value_kernel, half=half),
        grid_spec=pltpu.PrefetchScalarGridSpec(
            num_scalar_prefetch=1,
            grid=(seq // tile,),
            in_specs=[
                pl.BlockSpec((near_rows, width), lambda r, p: (0, 0)),
                pl.BlockSpec((near_rows, width), lambda r, p: (0, 0)),
                pl.BlockSpec((1, width), lambda r, p: (0, 0)),
                pl.BlockSpec((width, width), lambda r, p: (0, 1)),
                pl.BlockSpec((width, width), lambda r, p: (0, 2)),
            ],
            out_specs=[
                pl.BlockSpec((tile, width), lambda r, p: (r, 0)),
                pl.BlockSpec((tile, 2 * width), lambda r, p: (r, 0)),
            ],
        ),
        out_shape=[
            jax.ShapeDtypeStruct((seq, width), BF),
            jax.ShapeDtypeStruct((seq, 2 * width), BF),
        ],
        compiler_params=pltpu.CompilerParams(vmem_limit_bytes=VMEM_LIMIT),
        cost_estimate=pl.CostEstimate(
            flops=4 * seq * width * width, bytes_accessed=8 * seq * width, transcendentals=seq
        ),
        name="keys_and_values",
    )(place, near, far, gain[None], w_qkv, w_qkv)


def normed_grad_kernel(position_ref, dkv_ref, wk_ref, wv_ref, out_ref, *, half):
    tile = out_ref.shape[0] // half
    rows = []
    for block in range(tile):
        source = position_ref[pl.program_id(0) * tile + block]
        rows.append(dkv_ref[pl.ds(pl.multiple_of(source * half, half), half)])
    grads = jnp.concatenate(rows, axis=0)
    width = out_ref.shape[1]
    out = lax.dot_general(grads[:, :width], wk_ref[...], COLS, preferred_element_type=F32)
    out += lax.dot_general(grads[:, width:], wv_ref[...], COLS, preferred_element_type=F32)
    out_ref[...] = out.astype(BF)


def normed_grads(position, key_value_grad, w_qkv, half):
    seq, width = key_value_grad.shape[0], w_qkv.shape[0]
    rows = position.shape[0] * half
    tile = 4 * half
    return pl.pallas_call(
        functools.partial(normed_grad_kernel, half=half),
        grid_spec=pltpu.PrefetchScalarGridSpec(
            num_scalar_prefetch=1,
            grid=(rows // tile,),
            in_specs=[
                pl.BlockSpec((seq, 2 * width), lambda r, p: (0, 0)),
                pl.BlockSpec((width, width), lambda r, p: (0, 1)),
                pl.BlockSpec((width, width), lambda r, p: (0, 2)),
            ],
            out_specs=pl.BlockSpec((tile, width), lambda r, p: (r, 0)),
        ),
        out_shape=jax.ShapeDtypeStruct((rows, width), BF),
        compiler_params=pltpu.CompilerParams(vmem_limit_bytes=VMEM_LIMIT),
        cost_estimate=pl.CostEstimate(
            flops=4 * rows * width * width, bytes_accessed=8 * rows * width, transcendentals=0
        ),
        name="normed_grads",
    )(position, key_value_grad, w_qkv, w_qkv)


def weight_grad_kernel(
    core_ref, dq_ref, normed_ref, dkv_ref, all_normed_ref, extra_ref, kept_ref, given_ref, total
):
    step = pl.program_id(0)
    tiles = normed_ref.shape[1] // dq_ref.shape[1]

    @pl.when(step < tiles)
    def _():
        total[...] = lax.dot_general(
            dq_ref[...], normed_ref[...], ROWS, preferred_element_type=F32
        )

    @pl.when((step >= tiles) & (step < 3 * tiles))
    def _():
        total[...] = lax.dot_general(
            dkv_ref[...], all_normed_ref[...], ROWS, preferred_element_type=F32
        )

    @pl.when(step == 3 * tiles)
    def _():
        total[...] = extra_ref[...]

    side = kept_ref.shape[1]
    left, right = total[:, :side].astype(BF), total[:, side:].astype(BF)

    @pl.when(core_ref[0] == 0)
    def _():
        kept_ref[...] = left
        given_ref[...] = right

    @pl.when(core_ref[0] != 0)
    def _():
        kept_ref[...] = right
        given_ref[...] = left


def weight_grads(core, query_grad, normed_one, key_value_grad, all_normed, extra):
    rows, width = normed_one.shape
    seq = all_normed.shape[0]
    tile = extra.shape[0]
    tiles = width // tile
    out_spec = pl.BlockSpec((tile, width // 2), lambda t, p: (t, 0))
    out_shape = jax.ShapeDtypeStruct((3 * width + tile, width // 2), BF)
    return pl.pallas_call(
        weight_grad_kernel,
        grid_spec=pltpu.PrefetchScalarGridSpec(
            num_scalar_prefetch=1,
            grid=(3 * tiles + 1,),
            in_specs=[
                pl.BlockSpec((rows, tile), lambda t, p: (0, jnp.minimum(t, tiles - 1))),
                pl.BlockSpec((rows, width), lambda t, p: (0, 0)),
                pl.BlockSpec((seq, tile), lambda t, p: (0, jnp.clip(t - tiles, 0, 2 * tiles - 1))),
                pl.BlockSpec((seq, width), lambda t, p: (0, 0)),
                pl.BlockSpec((tile, width), lambda t, p: (0, 0)),
            ],
            out_specs=[out_spec, out_spec],
            scratch_shapes=[pltpu.VMEM((tile, width), F32)],
        ),
        out_shape=[out_shape, out_shape],
        compiler_params=pltpu.CompilerParams(vmem_limit_bytes=VMEM_LIMIT),
        cost_estimate=pl.CostEstimate(
            flops=4 * seq * width * width, bytes_accessed=10 * seq * width, transcendentals=0
        ),
        name="weight_grads",
    )(core, query_grad, normed_one, key_value_grad, all_normed, extra)


def whole_grad_kernel(core_ref, mine_ref, other_ref, weight_ref, grad_ref, product_ref):
    side, tile = mine_ref.shape[1], mine_ref.shape[0]
    width = 2 * side
    first = pl.multiple_of(core_ref[0] * side, side)
    grad_ref[pl.ds(first, side), :] = mine_ref[...].astype(F32).T
    grad_ref[pl.ds(pl.multiple_of(side - first, side), side), :] = other_ref[...].astype(F32).T
    product = jnp.sum(grad_ref[...] * weight_ref[...].astype(F32), axis=1, keepdims=True)
    product = jnp.broadcast_to(product, (width, LANES))

    @pl.when(pl.program_id(0) == 0)
    def _():
        product_ref[...] = product

    @pl.when(pl.program_id(0) > 0)
    def _():
        product_ref[...] += product


def whole_grad(core, mine, other, weight):
    width, columns = weight.shape
    side = mine.shape[1]
    tile = 2 * LANES
    half_spec = pl.BlockSpec((tile, side), lambda t, p: (t, 0))
    whole_spec = pl.BlockSpec((width, tile), lambda t, p: (0, t))
    return pl.pallas_call(
        whole_grad_kernel,
        grid_spec=pltpu.PrefetchScalarGridSpec(
            num_scalar_prefetch=1,
            grid=(columns // tile,),
            in_specs=[half_spec, half_spec, whole_spec],
            out_specs=[whole_spec, pl.BlockSpec((width, LANES), lambda t, p: (0, 0))],
        ),
        out_shape=[
            jax.ShapeDtypeStruct((width, columns), F32),
            jax.ShapeDtypeStruct((width, LANES), F32),
        ],
        compiler_params=pltpu.CompilerParams(vmem_limit_bytes=VMEM_LIMIT),
        cost_estimate=pl.CostEstimate(
            flops=2 * width * columns, bytes_accessed=8 * width * columns, transcendentals=0
        ),
        name="whole_grad",
    )(core, mine, other, weight)


def expert_kernel(
    x_ref, cot_ref, in_ref, out_ref, back_ref, act_ref, pre_grad_ref, ret_sum, dx_sum
):
    part = pl.program_id(1)
    width = cot_ref.shape[-1]
    rows = x_ref.shape[0] * x_ref.shape[1]
    x, slot_grad = expert_rows(x_ref, cot_ref)
    weight_in, weight_out = in_ref[...], out_ref[...]
    pre = jnp.dot(x, weight_in, preferred_element_type=F32)
    act_grad = lax.dot_general(slot_grad, weight_out, COLS, preferred_element_type=F32)
    cumulative = 0.5 * (1.0 + lax.erf(pre * 0.7071067811865476))
    activated = (pre * cumulative).astype(BF)
    slope = cumulative + pre * (jnp.exp(-0.5 * pre * pre) * 0.3989422804014327)
    pre_grad = (act_grad * slope).astype(BF)
    act_ref[...] = activated
    pre_grad_ref[...] = pre_grad
    returned = jnp.dot(activated, weight_out, preferred_element_type=F32)
    input_grad = lax.dot_general(pre_grad, weight_in, COLS, preferred_element_type=F32)

    @pl.when(part == 0)
    def _():
        ret_sum[...] = returned
        dx_sum[...] = input_grad

    @pl.when(part > 0)
    def _():
        ret_sum[...] += returned
        dx_sum[...] += input_grad

    @pl.when(part == pl.num_programs(1) - 1)
    def _():
        shape = cot_ref.shape
        back_ref[:, :, :width] = ret_sum[...].astype(BF).reshape(shape)
        back_ref[:, :, width:] = dx_sum[...].astype(BF).reshape(shape)


def expert_rows(x_ref, cot_ref):
    width = cot_ref.shape[-1]
    rows = x_ref.shape[0] * x_ref.shape[1]
    rows_in = x_ref[...].reshape(rows, x_ref.shape[2])
    gate = jnp.sum(rows_in[:, width:].astype(F32), axis=1, keepdims=True)
    slot_grad = (cot_ref[...].reshape(rows, width).astype(F32) * gate).astype(BF)
    return rows_in[:, :width], slot_grad


def expert_grad_kernel(x_ref, cot_ref, act_ref, pre_grad_ref, grad_in_ref, grad_out_ref):
    x, slot_grad = expert_rows(x_ref, cot_ref)
    grad_in = lax.dot_general(x, pre_grad_ref[...], ROWS, preferred_element_type=F32)
    grad_out = lax.dot_general(act_ref[...], slot_grad, ROWS, preferred_element_type=F32)
    grad_in_ref[...] = grad_in.astype(BF)
    grad_out_ref[...] = grad_out.astype(BF)


def run_experts(x_rows, cot_rows, weight_in, weight_out):
    devices, experts, slots, width = cot_rows.shape
    wide = x_rows.shape[3]
    parts, _, _, hidden = weight_in.shape
    rows = devices * slots

    def row_spec(columns):
        return pl.BlockSpec((devices, None, slots, columns), lambda e, w: (0, e, 0, 0))

    def part_spec(tall, columns):
        return pl.BlockSpec((None, None, tall, columns), lambda e, w: (w, e, 0, 0))

    in_spec, out_spec = part_spec(width, hidden), part_spec(hidden, width)
    hidden_spec = part_spec(rows, hidden)
    hidden_shape = jax.ShapeDtypeStruct((parts, experts, rows, hidden), BF)
    work = experts * rows * width * parts * hidden
    params = pltpu.CompilerParams(vmem_limit_bytes=VMEM_LIMIT)
    back, activated, pre_grad = pl.pallas_call(
        expert_kernel,
        grid=(experts, parts),
        in_specs=[row_spec(wide), row_spec(width), in_spec, out_spec],
        out_specs=[row_spec(2 * width), hidden_spec, hidden_spec],
        out_shape=[
            jax.ShapeDtypeStruct((devices, experts, slots, 2 * width), BF),
            hidden_shape,
            hidden_shape,
        ],
        scratch_shapes=[pltpu.VMEM((rows, width), F32), pltpu.VMEM((rows, width), F32)],
        compiler_params=params,
        cost_estimate=pl.CostEstimate(
            flops=8 * work,
            bytes_accessed=8 * experts * rows * width + 8 * parts * experts * width * hidden,
            transcendentals=2 * experts * rows * parts * hidden,
        ),
        name="experts",
    )(x_rows, cot_rows, weight_in, weight_out)
    grads = pl.pallas_call(
        expert_grad_kernel,
        grid=(experts, parts),
        in_specs=[row_spec(wide), row_spec(width), hidden_spec, hidden_spec],
        out_specs=[in_spec, out_spec],
        out_shape=[
            jax.ShapeDtypeStruct(weight_in.shape, BF),
            jax.ShapeDtypeStruct(weight_out.shape, BF),
        ],
        compiler_params=params,
        cost_estimate=pl.CostEstimate(
            flops=4 * work,
            bytes_accessed=8 * experts * rows * width + 4 * parts * experts * width * hidden,
            transcendentals=0,
        ),
        name="expert_grads",
    )(x_rows, cot_rows, activated, pre_grad)
    return back, *grads


def on_device(
    tokens,
    gain_attn,
    w_qkv,
    rel_bias,
    w_attn_out,
    gain_ffn,
    w_router,
    w_in,
    w_out,
    routes,
    pair_order,
    bucket_table,
    cotangent,
):
    tok_rows = tokens.shape[1]
    model_width = tokens.shape[2]
    head_count = rel_bias.shape[1]
    bucket_count = rel_bias.shape[0]
    ctx_count = lax.axis_size(CTX)
    half = tok_rows // 2
    blocks = 2 * ctx_count
    seq = half * blocks
    window = seq + 2 * half
    head_pairs = head_count // 2
    local_experts = w_in.shape[0]
    experts = w_router.shape[1]
    capacity = 4 * tok_rows // experts
    device_slots = local_experts * capacity
    expert_devices = lax.axis_size(EXPERT_AXES)
    copies = expert_devices // ctx_count

    near_tokens = spread(tokens[0], SAME_CORE)
    far_tokens = lax.ppermute(near_tokens, "core", SWAP)
    near_tokens = near_tokens.reshape(seq // 2, model_width)
    far_tokens = far_tokens.reshape(seq // 2, model_width)
    whole_in = lax.all_gather(w_in, "x", axis=0)
    whole_out = lax.all_gather(w_out, "x", axis=0)

    chosen = routes[0].T
    expert_ids = jnp.arange(experts, dtype=jnp.int32)
    flat_expert = chosen.reshape(2 * tok_rows)
    member = flat_expert[:, None] == expert_ids[None, :]
    picks = jnp.arange(2 * tok_rows, dtype=jnp.int32)
    before = (picks[:, None] > picks[None, :]).astype(BF)
    counts = jnp.dot(before, member.astype(BF), preferred_element_type=F32)
    slot_rank = jnp.sum(jnp.where(member, counts, 0.0), axis=1).astype(jnp.int32)
    owner_index = flat_expert // local_experts
    slot_of = (flat_expert % local_experts) * capacity + slot_rank
    slot_ids = jnp.arange(expert_devices * device_slots, dtype=jnp.int32)
    slot_hot = (owner_index[:, None] == (slot_ids // (copies * device_slots))[None, :]) & (
        slot_of[:, None] == (slot_ids % device_slots)[None, :]
    )
    slot_table = slot_hot.astype(BF)
    token_table = slot_table[:tok_rows] + slot_table[tok_rows:]

    def to_experts(table, rows):
        slots = contract_rows(table, rows).astype(BF)
        arrived = exchange(slots.reshape(expert_devices, device_slots, rows.shape[1]), EXPERT_AXES)
        return arrived.reshape(expert_devices, local_experts, capacity, rows.shape[1])

    cot_rows = to_experts(token_table, cotangent[0])

    ctx_ids = jnp.arange(ctx_count, dtype=jnp.int32)
    my_core = lax.axis_index("core")
    near = (ctx_ids % 2) == my_core
    lies = 2 * (jnp.where(near, 0, ctx_count // 2) + ctx_ids // 2)
    block_ids = jnp.arange(blocks, dtype=jnp.int32)[:, None]
    place = jnp.sum(
        jnp.where(pair_order[None, :] == block_ids, lies[None, :], 0)
        + jnp.where(blocks - 1 - pair_order[None, :] == block_ids, lies[None, :] + 1, 0),
        axis=1,
        dtype=jnp.int32,
    )
    positions = jnp.sum(
        jnp.where(
            2 * (block_ids // 2) == lies[None, :],
            jnp.where(block_ids % 2 == 0, pair_order[None, :], blocks - 1 - pair_order[None, :]),
            0,
        ),
        axis=1,
        dtype=jnp.int32,
    )
    my_pair = jnp.sum(jnp.where(ctx_ids == lax.axis_index(CTX), pair_order, 0))
    reversed_table = jnp.pad(bucket_table[::-1], (0, window - half), constant_values=-1)
    diagonal_bucket = jnp.stack(
        [
            lax.dynamic_slice(reversed_table, (seq - half - block * half,), (window,))
            for block in (my_pair, blocks - 1 - my_pair)
        ]
    ).reshape(1, 2 * window)
    bucket_ids = jnp.arange(bucket_count, dtype=jnp.int32)
    bucket_hot = (diagonal_bucket == bucket_ids[:, None]).astype(F32)
    windows = lax.dot_general(rel_bias, bucket_hot, ROWS, precision=HIGHEST)
    windows = jnp.where(diagonal_bucket >= 0, windows, MASKED)
    windows = windows.reshape(head_pairs, 4, window)

    inputs = tokens[0].astype(F32)
    scale_one = norm_scale(inputs)
    normed_one = (inputs * scale_one * gain_attn).astype(BF)
    w_q = w_qkv[:, :model_width]
    queries = jnp.dot(normed_one, w_q, preferred_element_type=F32).astype(BF)
    all_normed, key_value = keys_and_values(
        place, near_tokens, far_tokens, gain_attn, w_qkv, half
    )
    attended, probabilities = attend(queries, key_value, windows)
    residual_one = inputs + jnp.dot(attended, w_attn_out, preferred_element_type=F32)
    scale_two = norm_scale(residual_one)
    normed_two = (residual_one * scale_two * gain_ffn).astype(BF)

    router_logits = jnp.dot(normed_two, w_router, preferred_element_type=F32)
    chosen_hot = (chosen[:, :, None] == expert_ids[None, None, :]).astype(F32)
    picked_logits = jnp.sum(chosen_hot * router_logits[None], axis=2)
    logit_peak = jnp.max(picked_logits, axis=0, keepdims=True)
    gate_exp = jnp.exp(picked_logits - logit_peak)
    gate_weights = (gate_exp / jnp.sum(gate_exp, axis=0, keepdims=True))[:, :, None]

    flat_gate = gate_weights.reshape(2 * tok_rows, 1)
    gate_high = flat_gate.astype(BF).astype(F32)
    lane_ids = jnp.arange(LANES, dtype=jnp.int32)[None, :]
    gate_lanes = jnp.where(lane_ids == 0, gate_high, 0.0)
    gate_lanes = jnp.where(lane_ids == 1, flat_gate - gate_high, gate_lanes).astype(BF)
    pick_rows = jnp.concatenate([normed_two, normed_two], axis=0)
    x_rows = to_experts(slot_table, jnp.concatenate([pick_rows, gate_lanes], axis=1))
    back, part_in, part_out = run_experts(x_rows, cot_rows, whole_in, whole_out)
    grad_w_in = lax.psum_scatter(part_in, "x", scatter_dimension=0).astype(F32)
    grad_w_out = lax.psum_scatter(part_out, "x", scatter_dimension=0).astype(F32)
    back = exchange(back.reshape(expert_devices, device_slots, 2 * model_width), EXPERT_AXES)
    back = back.reshape(expert_devices * device_slots, 2 * model_width)
    picked = jnp.dot(slot_table, back[:, :model_width], preferred_element_type=F32)
    picked = picked.reshape(2, tok_rows, model_width)
    expert_part = jnp.dot(token_table, back[:, model_width:], preferred_element_type=F32)
    mixture = jnp.sum(gate_weights * picked, axis=0)
    layer_out = (residual_one + mixture).astype(BF)[None]

    upstream = cotangent[0].astype(F32)
    gate_grad = jnp.sum(picked * upstream[None], axis=2, keepdims=True)
    inner_mean = jnp.sum(gate_weights * gate_grad, axis=0, keepdims=True)
    pick_grad = gate_weights * (gate_grad - inner_mean)
    logit_grad = jnp.sum(pick_grad * chosen_hot, axis=0)
    grad_w_router = lax.dot_general(normed_two.astype(F32), logit_grad, ROWS, precision=HIGHEST)
    router_back = lax.dot_general(logit_grad, w_router.astype(F32), COLS, precision=HIGHEST)
    normed_two_grad = expert_part + router_back
    norm_part, grad_gain_ffn = norm_backward(residual_one, scale_two, gain_ffn, normed_two_grad)
    mixed_grad = upstream + norm_part
    branch_grad = mixed_grad.astype(BF)
    grad_w_attn_out = contract_rows(attended, branch_grad)

    core = jnp.reshape(my_core, (1,)).astype(jnp.int32)
    side = model_width // 2
    chips = lax.axis_size(CHIPS)
    small = jnp.concatenate([grad_w_attn_out, grad_w_router.T, grad_gain_ffn[None]], axis=0)
    spare = -small.shape[0] % (16 * chips)
    small = jnp.pad(small, ((0, spare), (0, 0))).astype(BF)
    left, right = small[:, :side], small[:, side:]
    first = my_core == 0
    mine, other = sum_halves(jnp.where(first, left, right), jnp.where(first, right, left))
    left, right = jnp.where(first, mine, other), jnp.where(first, other, mine)
    small = jnp.concatenate([left, right], axis=1).astype(F32)
    sum_w_attn_out = small[:model_width]
    sum_w_router = small[model_width : model_width + experts].T
    sum_gain_ffn = small[model_width + experts]

    attended_grad = contract_cols(branch_grad, w_attn_out).astype(BF)
    query_grad, key_value_grad, diagonals = attend_back(
        probabilities, queries, key_value, attended_grad
    )
    diagonals = diagonals.reshape(head_count, 2 * window)
    grad_rel_bias = lax.dot_general(bucket_hot, diagonals, COLS, precision=HIGHEST)
    biases = bucket_count * head_count
    bias_row = jnp.pad(grad_rel_bias.reshape(1, biases), ((0, 0), (0, side - biases)))
    bias_row = jnp.concatenate([bias_row, bias_row], axis=1)
    extra = jnp.pad(bias_row, ((0, 2 * LANES - 1), (0, 0)))
    kept, given = weight_grads(core, query_grad, normed_one, key_value_grad, all_normed, extra)
    key_value_grad, kept, given = lax.optimization_barrier((key_value_grad, kept, given))
    mine, other = sum_halves(kept, given)
    sum_w_qkv, products = whole_grad(core, mine, other, w_qkv)
    sum_gain_attn = products[:, 0] / gain_attn
    sum_rel_bias = mine[3 * model_width, :biases].astype(F32).reshape(bucket_count, head_count)
    far_grad = normed_grads(positions[blocks // 2 :], key_value_grad, w_qkv, half)
    near_grad = normed_grads(positions[: blocks // 2], key_value_grad, w_qkv, half)
    near_grad = near_grad.astype(F32) + lax.ppermute(far_grad, "core", SWAP).astype(F32)
    near_grad = near_grad.astype(BF).reshape(ctx_count // 2, tok_rows, model_width)
    normed_one_grad = jnp.sum(exchange(near_grad, SAME_CORE).astype(F32), axis=0)
    normed_one_grad = normed_one_grad + contract_cols(query_grad, w_q)
    input_norm_grad, _ = norm_backward(inputs, scale_one, gain_attn, normed_one_grad)
    grad_tokens = (mixed_grad + input_norm_grad)[None]
    return (
        layer_out,
        grad_tokens,
        sum_gain_attn,
        sum_w_qkv,
        sum_rel_bias,
        sum_w_attn_out,
        sum_gain_ffn,
        sum_w_router,
        grad_w_in,
        grad_w_out,
    )


def solution(mesh):
    split_mesh = Mesh(mesh.devices.reshape(SPLIT), EVERY)
    in_specs = (
        P(WSH, CTX, None),
        P(),
        P(),
        P(),
        P(),
        P(),
        P(),
        P(CTX, None, WSH),
        P(CTX, WSH, None),
        P(WSH, CTX, None),
        P(),
        P(),
        P(WSH, CTX, None),
    )
    out_specs = (
        P(WSH, CTX, None),
        P(WSH, CTX, None),
        P(),
        P(),
        P(),
        P(),
        P(),
        P(),
        P(CTX, None, WSH),
        P(CTX, WSH, None),
    )
    return jax.shard_map(
        on_device, mesh=split_mesh, in_specs=in_specs, out_specs=out_specs, check_vma=False
    )
```

profile of v0, /device:TPU:1, one launch (start us, length us, event | category | flops | bytes accessed | tf_op | source)
XLA Modules:
  0.0 450.0 jit_solution(10535767826944083731)
XLA Ops:
  10.1 8.6 %all-to-all-start = ((bf16[8,128,768]{2,1,0:T(8,128)(2,1)}), bf16[8,128,768]{2,1,0:T(8,128)(2,1)S(1)}, u32[]{:S(2)}, u32[]{:S(2)}) async-start(bf16[8,128,768]{2,1,0:T(8,128)(2,1)} %broadcast_in_dim.168), calls=%async_computation | async-start | bytes 3145728 | tf_op jit(solution)/shard_map/all_to_all | solution.py:53
  24.8 14.5 %all-to-all-done = bf16[8,128,768]{2,1,0:T(8,128)(2,1)S(1)} async-done(((bf16[8,128,768]{2,1,0:T(8,128)(2,1)}), bf16[8,128,768]{2,1,0:T(8,128)(2,1)S(1)}, u32[]{:S(2)}, u32[]{:S(2)}) %all-to-all-start) | async-done | bytes 1572896 | tf_op jit(solution)/shard_map/all_to_all | solution.py:53
  39.2 6.4 %all-to-all-start.2 = ((bf16[32,32,768]{2,1,0:T(8,128)(2,1)}), bf16[32,32,768]{2,1,0:T(8,128)(2,1)}, u32[]{:S(2)}, u32[]{:S(2)}) async-start(bf16[32,32,768]{2,1,0:T(8,128)(2,1)} %bitcast.97), calls=%async_computation.2 | async-start | bytes 3145728 | tf_op jit(solution)/shard_map/all_to_all | solution.py:53
  53.9 10.4 %keys_and_values.1 = (bf16[2048,768]{1,0:T(8,128)(2,1)S(1)}, bf16[2048,1536]{1,0:T(8,128)(2,1)}) custom-call(s32[32]{0:T(128)S(1)} %get-tuple-element.91.place_ref, bf16[1024,768]{1,0:T(8,128)(2,1)S(1)} %bitcast.94, bf16[1024,768]{1,0:T(8,128)(2,1)} %bitcast.2.far_ref, f32[1,768]{1,0:T(1,128)S(1)} %broadcast_in_dim.169.gain_ref, ...), custom_call_target="tpu_custom_call" | custom-call | flops 4831838208 | bytes 12582912 | tf_op jit(solution)/shard_map/keys_and_values/pallas_call | solution.py:239
  65.9 11.3 %attend.1 = (bf16[128,768]{1,0:T(8,128)(2,1)S(1)}, bf16[12,128,2048]{2,1,0:T(8,128)(2,1)S(1)}) custom-call(bf16[128,768]{1,0:T(8,128)(2,1)S(1)} %convolution_convert_fusion.4.q_ref, bf16[2048,1536]{1,0:T(8,128)(2,1)} %get-tuple-element.29.k_ref.v_ref, bf16[2048,1536]{1,0:T(8,128)(2,1)} %get-tuple-element.29.k_ref.v_ref, f32[6,4,2176]{2,1,0:T(4,128)S(1)} %reshape.433.window_ref), custom_call_target="tpu_custom_call" | custom-call | flops 1610612736 | bytes 12582912 | tf_op jit(solution)/shard_map/attend/pallas_call | solution.py:113
  83.8 31.8 %all_to_all.45 = bf16[32,32,896]{2,1,0:T(8,128)(2,1)S(1)} all-to-all(bf16[32,32,896]{2,1,0:T(8,128)(2,1)} %bitcast.102), channel_id=1, replica_groups=mesh['ya'=2,'z'=4,'core'=2,'yb'=2,'x'=4] {'ya','z','core','yb'}, dimensions={0} | all-to-all | bytes 3670016 | tf_op jit(solution)/shard_map/all_to_all | solution.py:53
  120.2 20.0 %experts.1 = (bf16[32,2,16,1536]{3,2,1,0:T(8,128)(2,1)S(1)}, bf16[4,2,512,384]{3,2,1,0:T(8,128)(2,1)S(1)}, bf16[4,2,512,384]{3,2,1,0:T(8,128)(2,1)}) custom-call(bf16[32,2,16,896]{3,2,1,0:T(8,128)(2,1)S(1)} %bitcast.92, bf16[32,2,16,768]{3,2,1,0:T(8,128)(2,1)} %bitcast.14.cot_ref, bf16[4,2,768,384]{3,2,1,0:T(8,128)(2,1)} %bitcast.106, ...), custom_call_target="tpu_custom_call" | custom-call | flops 9663676416 | bytes 25165824 | tf_op jit(solution)/shard_map/experts/pallas_call | solution.py:487
  143.8 10.2 %expert_grads.1 = (bf16[4,2,768,384]{3,2,1,0:T(8,128)(2,1)}, bf16[4,2,384,768]{3,2,1,0:T(8,128)(2,1)}) custom-call(bf16[32,2,16,896]{3,2,1,0:T(8,128)(2,1)S(1)} %bitcast.93, bf16[32,2,16,768]{3,2,1,0:T(8,128)(2,1)} %bitcast.14.cot_ref, bf16[4,2,512,384]{3,2,1,0:T(8,128)(2,1)S(1)} %get-tuple-element.44.act_ref, bf16[4,2,512,384]{3,2,1,0:T(8,128)(2,1)S(1)} %copy-done.14), custom_call_target="tpu_custom_call" | custom-call | flops 4831838208 | bytes 15728640 | tf_op jit(solution)/shard_map/expert_grads/pallas_call | solution.py:506
  154.0 7.9 %all-to-all-start.3 = ((bf16[32,32,1536]{2,1,0:T(8,128)(2,1)}), bf16[32,32,1536]{2,1,0:T(8,128)(2,1)}, u32[]{:S(2)}, u32[]{:S(2)}) async-start(bf16[32,32,1536]{2,1,0:T(8,128)(2,1)} %bitcast.91), calls=%async_computation.3 | async-start | bytes 6291456 | tf_op jit(solution)/shard_map/all_to_all | solution.py:53
  162.2 39.2 %all-to-all-done.3 = bf16[32,32,1536]{2,1,0:T(8,128)(2,1)} async-done(((bf16[32,32,1536]{2,1,0:T(8,128)(2,1)}), bf16[32,32,1536]{2,1,0:T(8,128)(2,1)}, u32[]{:S(2)}, u32[]{:S(2)}) %all-to-all-start.3) | async-done | bytes 3145760 | tf_op jit(solution)/shard_map/all_to_all | solution.py:53
  208.1 25.1 %attend_back.1 = (bf16[128,768]{1,0:T(8,128)(2,1)S(1)}, bf16[2048,1536]{1,0:T(8,128)(2,1)S(1)}, f32[6,4,2176]{2,1,0:T(4,128)S(1)}) custom-call(bf16[12,128,2048]{2,1,0:T(8,128)(2,1)} %copy-done.6, bf16[128,768]{1,0:T(8,128)(2,1)S(1)} %convolution_convert_fusion.4.q_ref, bf16[2048,1536]{1,0:T(8,128)(2,1)} %get-tuple-element.29.k_ref.v_ref, ...), custom_call_target="tpu_custom_call" | custom-call | flops 3221225472 | bytes 18874368 | tf_op jit(solution)/shard_map/attend_back/pallas_call | solution.py:188
  240.6 10.9 %weight_grads.1 = (bf16[2560,384]{1,0:T(8,128)(2,1)S(1)}, bf16[2560,384]{1,0:T(8,128)(2,1)}) custom-call(s32[1]{0:T(128)} %bitcast.23.core_ref, bf16[128,768]{1,0:T(8,128)(2,1)S(1)} %copy-done.11, bf16[128,768]{1,0:T(8,128)(2,1)S(1)} %copy-done.9, bf16[2048,1536]{1,0:T(8,128)(2,1)} %copy-done.5, bf16[2048,768]{1,0:T(8,128)(2,1)S(1)} %copy-done.13, ...), custom_call_target="tpu_custom_call" | custom-call | flops 4831838208 | bytes 15728640 | tf_op jit(solution)/shard_map/weight_grads/pallas_call | solution.py:349
  261.4 9.6 %all-to-all-start.7 = ((bf16[64,16,384]{2,1,0:T(8,128)(2,1)}), bf16[64,16,384]{2,1,0:T(8,128)(2,1)S(1)}, u32[]{:S(2)}, u32[]{:S(2)}) async-start(bf16[64,16,384]{2,1,0:T(8,128)(2,1)} %bitcast.101), calls=%async_computation.7 | async-start | bytes 1572864 | tf_op jit(solution)/shard_map/all_to_all | solution.py:53
  271.1 24.0 %all-to-all-done.7 = bf16[64,16,384]{2,1,0:T(8,128)(2,1)S(1)} async-done(((bf16[64,16,384]{2,1,0:T(8,128)(2,1)}), bf16[64,16,384]{2,1,0:T(8,128)(2,1)S(1)}, u32[]{:S(2)}, u32[]{:S(2)}) %all-to-all-start.7) | async-done | bytes 786464 | tf_op jit(solution)/shard_map/all_to_all | solution.py:53
  296.2 4.7 %all-to-all-start.8 = ((bf16[64,16,384]{2,1,0:T(8,128)(2,1)}), bf16[64,16,384]{2,1,0:T(8,128)(2,1)S(1)}, u32[]{:S(2)}, u32[]{:S(2)}) async-start(bf16[64,16,384]{2,1,0:T(8,128)(2,1)} %broadcast_in_dim.183), calls=%async_computation.8 | async-start | bytes 1572864 | tf_op jit(solution)/shard_map/all_to_all | solution.py:53
  304.3 20.5 %all-to-all-done.8 = bf16[64,16,384]{2,1,0:T(8,128)(2,1)S(1)} async-done(((bf16[64,16,384]{2,1,0:T(8,128)(2,1)}), bf16[64,16,384]{2,1,0:T(8,128)(2,1)S(1)}, u32[]{:S(2)}, u32[]{:S(2)}) %all-to-all-start.8) | async-done | bytes 786464 | tf_op jit(solution)/shard_map/all_to_all | solution.py:53
  325.7 4.9 %all-to-all-start.5 = ((bf16[64,40,384]{2,1,0:T(8,128)(2,1)}), bf16[64,40,384]{2,1,0:T(8,128)(2,1)S(1)}, u32[]{:S(2)}, u32[]{:S(2)}) async-start(bf16[64,40,384]{2,1,0:T(8,128)(2,1)} %bitcast.95), calls=%async_computation.5 | async-start | bytes 3932160 | tf_op jit(solution)/shard_map/all_to_all | solution.py:53
  332.6 6.6 %normed_grads.3 = bf16[1024,768]{1,0:T(8,128)(2,1)S(1)} custom-call(s32[16]{0:T(128)S(1)} %get-tuple-element.103.position_ref, bf16[2048,1536]{1,0:T(8,128)(2,1)} %copy-done.5, bf16[768,2304]{1,0:T(8,128)(2,1)S(1)} %copy-done.3, bf16[768,2304]{1,0:T(8,128)(2,1)S(1)} %copy-done.3), custom_call_target="tpu_custom_call" | custom-call | flops 2415919104 | bytes 6291456 | tf_op jit(solution)/shard_map/normed_grads/pallas_call | solution.py:285
  342.3 6.6 %normed_grads.2 = bf16[1024,768]{1,0:T(8,128)(2,1)S(1)} custom-call(s32[16]{0:T(128)S(1)} %get-tuple-element.102.position_ref, bf16[2048,1536]{1,0:T(8,128)(2,1)} %copy-done.5, bf16[768,2304]{1,0:T(8,128)(2,1)S(1)} %copy-done.3, bf16[768,2304]{1,0:T(8,128)(2,1)S(1)} %copy-done.3), custom_call_target="tpu_custom_call" | custom-call | flops 2415919104 | bytes 6291456 | tf_op jit(solution)/shard_map/normed_grads/pallas_call | solution.py:285
  350.5 6.7 %all-to-all-done.5 = bf16[64,40,384]{2,1,0:T(8,128)(2,1)S(1)} async-done(((bf16[64,40,384]{2,1,0:T(8,128)(2,1)}), bf16[64,40,384]{2,1,0:T(8,128)(2,1)S(1)}, u32[]{:S(2)}, u32[]{:S(2)}) %all-to-all-start.5) | async-done | bytes 1966112 | tf_op jit(solution)/shard_map/all_to_all | solution.py:53
  361.8 17.4 %all-to-all-done.4 = bf16[8,128,768]{2,1,0:T(8,128)(2,1)} async-done(((bf16[8,128,768]{2,1,0:T(8,128)(2,1)}), bf16[8,128,768]{2,1,0:T(8,128)(2,1)}, u32[]{:S(2)}, u32[]{:S(2)}) %all-to-all-start.4) | async-done | bytes 1572896 | tf_op jit(solution)/shard_map/all_to_all | solution.py:53
  380.6 9.8 %all-to-all-start.6 = ((bf16[64,40,384]{2,1,0:T(8,128)(2,1)}), bf16[64,40,384]{2,1,0:T(8,128)(2,1)S(1)}, u32[]{:S(2)}, u32[]{:S(2)}) async-start(bf16[64,40,384]{2,1,0:T(8,128)(2,1)} %broadcast_in_dim.181), calls=%async_computation.6 | async-start | bytes 3932160 | tf_op jit(solution)/shard_map/all_to_all | solution.py:53
  393.2 24.8 %all-to-all-done.6 = bf16[64,40,384]{2,1,0:T(8,128)(2,1)S(1)} async-done(((bf16[64,40,384]{2,1,0:T(8,128)(2,1)}), bf16[64,40,384]{2,1,0:T(8,128)(2,1)S(1)}, u32[]{:S(2)}, u32[]{:S(2)}) %all-to-all-start.6) | async-done | bytes 1966112 | tf_op jit(solution)/shard_map/all_to_all | solution.py:53
  434.1 8.6 %whole_grad.1 = (f32[768,2304]{1,0:T(8,128)}, f32[768,128]{1,0:T(8,128)S(1)}) custom-call(s32[1]{0:T(128)} %bitcast.23.core_ref, bf16[2560,384]{1,0:T(8,128)(2,1)S(1)} %bitcast.90, bf16[2560,384]{1,0:T(8,128)(2,1)} %collective-permute-done.3.other_ref, bf16[768,2304]{1,0:T(8,128)(2,1)S(1)} %copy-done.4), custom_call_target="tpu_custom_call" | custom-call | flops 3538944 | bytes 14155776 | tf_op jit(solution)/shard_map/whole_grad/pallas_call | solution.py:397
  (207 shorter events, 93.5 us)
Async XLA Ops:
  7.2 72.7 %copy-start = (bf16[768,768]{1,0:T(8,128)(2,1)S(1)}, bf16[768,768]{1,0:T(8,128)(2,1)}, u32[]{:S(2)}) copy-start(bf16[768,768]{1,0:T(8,128)(2,1)} %param.17) | copy-start | bytes 3538948
  7.2 108.4 %all-gather.5.cloned.1.call-start = ((), (), s32[]{:S(2)}) async-start(), calls=%async_computation.13 | async-start | bytes 5898240 | tf_op jit(solution)/shard_map/all_gather | solution.py:562
  10.1 29.1 %all-to-all-start = ((bf16[8,128,768]{2,1,0:T(8,128)(2,1)}), bf16[8,128,768]{2,1,0:T(8,128)(2,1)S(1)}, u32[]{:S(2)}, u32[]{:S(2)}) async-start(bf16[8,128,768]{2,1,0:T(8,128)(2,1)} %broadcast_in_dim.168), calls=%async_computation | async-start | bytes 3145728 | tf_op jit(solution)/shard_map/all_to_all | solution.py:53
  18.8 101.5 %all-gather.7.cloned.1.call-start = ((), (), s32[]{:S(2)}) async-start(), calls=%async_computation.14 | async-start | bytes 5898240 | tf_op jit(solution)/shard_map/all_gather | solution.py:563
  39.2 44.5 %all-to-all-start.2 = ((bf16[32,32,768]{2,1,0:T(8,128)(2,1)}), bf16[32,32,768]{2,1,0:T(8,128)(2,1)}, u32[]{:S(2)}, u32[]{:S(2)}) async-start(bf16[32,32,768]{2,1,0:T(8,128)(2,1)} %bitcast.97), calls=%async_computation.2 | async-start | bytes 3145728 | tf_op jit(solution)/shard_map/all_to_all | solution.py:53
  45.6 382.6 %reduce-scatter.3.cloned.1.call-start = ((), (), s32[]{:S(2)}) async-start(), calls=%async_computation.11 | async-start | bytes 5898240 | tf_op jit(solution)/shard_map/reduce_scatter | solution.py:651
  45.7 6.2 %collective-permute-start = (bf16[8,128,768]{2,1,0:T(8,128)(2,1)S(1)}, bf16[8,128,768]{2,1,0:T(8,128)(2,1)}, u32[]{:S(2)}, u32[]{:S(2)}) collective-permute-start(bf16[8,128,768]{2,1,0:T(8,128)(2,1)S(1)} %all-to-all-done), channel_id=1, source_target_pairs={{0,8},{8,0},{1,9},{9,1},{2,10},{10,2},{3,11},{11,3},{4,12},{12,4},... | collective-permute-start | bytes 4718600 | tf_op jit(solution)/shard_map/ppermute | solution.py:559
  154.0 47.4 %all-to-all-start.3 = ((bf16[32,32,1536]{2,1,0:T(8,128)(2,1)}), bf16[32,32,1536]{2,1,0:T(8,128)(2,1)}, u32[]{:S(2)}, u32[]{:S(2)}) async-start(bf16[32,32,1536]{2,1,0:T(8,128)(2,1)} %bitcast.91), calls=%async_computation.3 | async-start | bytes 6291456 | tf_op jit(solution)/shard_map/all_to_all | solution.py:53
  161.9 269.2 %reduce-scatter.5.cloned.1.call-start = ((), (), s32[]{:S(2)}) async-start(), calls=%async_computation.12 | async-start | bytes 5898240 | tf_op jit(solution)/shard_map/reduce_scatter | solution.py:652
  208.1 28.0 %copy-start.32 = (s32[4352]{0:T(1024)S(1)}, s32[4352]{0:T(1024)}, u32[]{:S(2)}) copy-start(s32[4352]{0:T(1024)} %copy-done.31) | copy-start | bytes 52228
  251.5 49.4 %collective-permute-start.2 = (bf16[2560,384]{1,0:T(8,128)(2,1)}, bf16[2560,384]{1,0:T(8,128)(2,1)}, u32[]{:S(2)}, u32[]{:S(2)}) collective-permute-start(bf16[2560,384]{1,0:T(8,128)(2,1)} %get-tuple-element.41), channel_id=1, source_target_pairs={{0,8},{8,0},{1,9},{9,1},{2,10},{10,2},{3,11},{11,3},{4,12},{12,4},... | collective-permute-start | bytes 5898248 | tf_op jit(solution)/shard_map/ppermute | solution.py:63
  256.2 2.5 collective-permute-start.4
  261.4 33.7 %all-to-all-start.7 = ((bf16[64,16,384]{2,1,0:T(8,128)(2,1)}), bf16[64,16,384]{2,1,0:T(8,128)(2,1)S(1)}, u32[]{:S(2)}, u32[]{:S(2)}) async-start(bf16[64,16,384]{2,1,0:T(8,128)(2,1)} %bitcast.101), calls=%async_computation.7 | async-start | bytes 1572864 | tf_op jit(solution)/shard_map/all_to_all | solution.py:53
  296.2 28.6 %all-to-all-start.8 = ((bf16[64,16,384]{2,1,0:T(8,128)(2,1)}), bf16[64,16,384]{2,1,0:T(8,128)(2,1)S(1)}, u32[]{:S(2)}, u32[]{:S(2)}) async-start(bf16[64,16,384]{2,1,0:T(8,128)(2,1)} %broadcast_in_dim.183), calls=%async_computation.8 | async-start | bytes 1572864 | tf_op jit(solution)/shard_map/all_to_all | solution.py:53
  325.7 31.5 %all-to-all-start.5 = ((bf16[64,40,384]{2,1,0:T(8,128)(2,1)}), bf16[64,40,384]{2,1,0:T(8,128)(2,1)S(1)}, u32[]{:S(2)}, u32[]{:S(2)}) async-start(bf16[64,40,384]{2,1,0:T(8,128)(2,1)} %bitcast.95), calls=%async_computation.5 | async-start | bytes 3932160 | tf_op jit(solution)/shard_map/all_to_all | solution.py:53
  339.3 9.7 %collective-permute-start.1 = (bf16[1024,768]{1,0:T(8,128)(2,1)S(1)}, bf16[1024,768]{1,0:T(8,128)(2,1)S(1)}, u32[]{:S(2)}, u32[]{:S(2)}) collective-permute-start(bf16[1024,768]{1,0:T(8,128)(2,1)S(1)} %normed_grads.3), channel_id=1, source_target_pairs={{0,8},{8,0},{1,9},{9,1},{2,10},{10,2},{3,11},{11,3},{4,12},{12,4},... | collective-permute-start | bytes 4718600 | tf_op jit(solution)/shard_map/ppermute | solution.py:707
  357.2 22.0 %all-to-all-start.4 = ((bf16[8,128,768]{2,1,0:T(8,128)(2,1)}), bf16[8,128,768]{2,1,0:T(8,128)(2,1)}, u32[]{:S(2)}, u32[]{:S(2)}) async-start(bf16[8,128,768]{2,1,0:T(8,128)(2,1)} %bitcast.98), calls=%async_computation.4 | async-start | bytes 3145728 | tf_op jit(solution)/shard_map/all_to_all | solution.py:53
  380.6 37.4 %all-to-all-start.6 = ((bf16[64,40,384]{2,1,0:T(8,128)(2,1)}), bf16[64,40,384]{2,1,0:T(8,128)(2,1)S(1)}, u32[]{:S(2)}, u32[]{:S(2)}) async-start(bf16[64,40,384]{2,1,0:T(8,128)(2,1)} %broadcast_in_dim.181), calls=%async_computation.6 | async-start | bytes 3932160 | tf_op jit(solution)/shard_map/all_to_all | solution.py:53
  390.4 29.8 %copy-start.17 = (bf16[1,128,768]{2,1,0:T(8,128)(2,1)S(1)}, bf16[1,128,768]{2,1,0:T(8,128)(2,1)}, u32[]{:S(2)}) copy-start(bf16[1,128,768]{2,1,0:T(8,128)(2,1)} %param.13) | copy-start | bytes 589828
  390.5 29.8 %copy-start.35 = (f32[768]{0:T(1024)S(1)}, f32[768]{0:T(1024)}, u32[]{:S(2)}) copy-start(f32[768]{0:T(1024)} %param.14) | copy-start | bytes 9220
  390.5 31.7 %copy-start.20 = (f32[128,768]{1,0:T(8,128)S(1)}, f32[128,768]{1,0:T(8,128)}, u32[]{:S(2)}) copy-start(f32[128,768]{1,0:T(8,128)} %copy-done.18) | copy-start | bytes 1179652
  390.5 31.7 %copy-start.46 = (f32[128]{0:T(128)S(1)}, f32[128]{0:T(128)}, u32[]{:S(2)}) copy-start(f32[128]{0:T(128)} %copy-done.45) | copy-start | bytes 1540
  390.5 32.6 %collective-permute-start.5 = (bf16[1024,384]{1,0:T(8,128)(2,1)}, bf16[1024,384]{1,0:T(8,128)(2,1)}, u32[]{:S(2)}, u32[]{:S(2)}) collective-permute-start(bf16[1024,384]{1,0:T(8,128)(2,1)} %bitcast.100), channel_id=1, source_target_pairs={{0,8},{8,0},{1,9},{9,1},{2,10},{10,2},{3,11},{11,3},{4,12},{12,4},... | collective-permute-start | bytes 2359304 | tf_op jit(solution)/shard_map/ppermute | solution.py:67
  418.0 16.1 %collective-permute-start.3 = (bf16[2560,384]{1,0:T(8,128)(2,1)S(1)}, bf16[2560,384]{1,0:T(8,128)(2,1)}, u32[]{:S(2)}, u32[]{:S(2)}) collective-permute-start(bf16[2560,384]{1,0:T(8,128)(2,1)S(1)} %bitcast.88), channel_id=1, source_target_pairs={{0,8},{8,0},{1,9},{9,1},{2,10},{10,2},{3,11},{11,3},{4,12},{12,4},... | collective-permute-start | bytes 5898248 | tf_op jit(solution)/shard_map/ppermute | solution.py:67
  (44 other events, 282.8 us)
Sparse Core Ops, SparseCore 0:
  9.7 55.7 all-gather.4
  67.2 53.0 all-gather.6
  154.1 51.5 reduce-scatter.2
  256.4 68.6 reduce-scatter.4
where the time goes:
time: 452 us; the launch traced here: 450 us
  waiting for transfers between devices  156 us (35%)
  Pallas kernels  110 us (24%)
  starting transfers between devices  64.6 us (14%)
  blocking collectives  31.8 us (7%)
  local copies, waits for them, and re-layouts  30.3 us (7%)
  other arithmetic  26.3 us (6%)
  matrix products  15.9 us (4%)
  between operations  15.9 us (4%)
    all_to_all x8, waiting for transfers between devices, exchange(): return lax.all_to_all(array, axes, split_axis=0, concat_axis=0, tiled=True)  147 us
    all_to_all x8, starting transfers between devices, exchange(): return lax.all_to_all(array, axes, split_axis=0, concat_axis=0, tiled=True)  56.3 us
    all_to_all x1, blocking collectives, exchange(): return lax.all_to_all(array, axes, split_axis=0, concat_axis=0, tiled=True)  31.8 us
    pallas_call x1, Pallas kernels, attend_back(): pl.pallas_call(attend_back_kernel, grid=(pairs, 2), in_specs=[pl.BlockSpe...  25.1 us
    unnamed x101, local copies, waits for them, and re-layouts  22.4 us
    pallas_call x1, Pallas kernels, run_experts(): pl.pallas_call(expert_kernel, grid=(experts, parts), in_specs=[row_spec(w...  20 us
    pallas_call x2, Pallas kernels, normed_grads(): pl.pallas_call(functools.partial(normed_grad_kernel, half=half), grid_spe...  13.3 us
    pallas_call x1, Pallas kernels, attend(): pl.pallas_call(attend_kernel, grid=(pairs,), in_specs=[pl.BlockSpec((rows...  11.3 us
  transfers between devices with their start and end apart: 18, of which 9 were waited for; matrix products, arithmetic and copies ran while one was open for 11% of the time, Pallas kernels for 16%

commit v1 on v0

v1 whole, which is shorter than its diff:
```python
import functools

import jax
import jax.numpy as jnp
from jax import lax
from jax.experimental import pallas as pl
from jax.experimental.pallas import tpu as pltpu
from jax.sharding import Mesh
from jax.sharding import PartitionSpec as P

BF = jnp.bfloat16
F32 = jnp.float32
EPSILON = 1e-06
HIGHEST = lax.Precision.HIGHEST
MASKED = -1e30
ROWS = (((0,), (0,)), ((), ()))
COLS = (((1,), (1,)), ((), ()))
LANES = 128
VMEM_LIMIT = 58 * 1024 * 1024
SPLIT = (2, 4, 2, 2, 4)
EVERY = ("ya", "z", "core", "yb", "x")
CTX = ("ya", "z", "core")
WSH = ("yb", "x")
SAME_CORE = ("ya", "z")
CHIPS = ("ya", "z", "yb", "x")
EXPERT_AXES = ("ya", "z", "core", "yb")
SWAP = ((0, 1), (1, 0))


def norm_scale(values):
    return lax.rsqrt(jnp.mean(values * values, axis=-1, keepdims=True) + EPSILON)


def norm_backward(values, scale_vector, gain_vector, upstream):
    weighted = upstream * gain_vector
    inner_mean = jnp.mean(weighted * values, axis=-1, keepdims=True)
    grad_input = (
        scale_vector * weighted - values * scale_vector * scale_vector * scale_vector * inner_mean
    )
    grad_gain = jnp.sum(upstream * values * scale_vector, axis=0)
    return (grad_input, grad_gain)


def contract_rows(left_matrix, right_matrix):
    return lax.dot_general(left_matrix, right_matrix, ROWS, preferred_element_type=F32)


def contract_cols(left_matrix, right_matrix):
    return lax.dot_general(left_matrix, right_matrix, COLS, preferred_element_type=F32)


def exchange(array, axes):
    return lax.all_to_all(array, axes, split_axis=0, concat_axis=0, tiled=True)


def spread(array, axes):
    return exchange(jnp.broadcast_to(array[None], (lax.axis_size(axes), *array.shape)), axes)


def half_share(kept, given):
    rows, columns = kept.shape
    chips = lax.axis_size(CHIPS)
    got = lax.ppermute(given, "core", SWAP)
    half = (kept.astype(F32) + got.astype(F32)).astype(BF).reshape(chips, rows // chips, columns)
    return jnp.sum(exchange(half, CHIPS).astype(F32), axis=0).astype(BF)


def shear(tiles):
    count, rows, columns = tiles.shape
    while rows > 8:
        half = rows // 2
        moved = pltpu.roll(tiles[:, :half].reshape(count * half, columns), half, axis=1)
        tiles = moved.reshape(count, half, columns) + tiles[:, half:]
        rows = half
    flat = tiles.reshape(count * rows, columns)
    row_ids = lax.broadcasted_iota(jnp.int32, flat.shape, 0)
    step = rows // 2
    while step:
        flat = jnp.where(row_ids // step % 2 == 0, pltpu.roll(flat, step, axis=1), flat)
        step //= 2
    return jnp.sum(flat.reshape(count, rows, columns), axis=1)


def split_heads(array, factor):
    lanes = lax.broadcasted_iota(jnp.int32, array.shape, 1) // (LANES // 2)
    wide = array.astype(F32) * factor
    parts = [jnp.where(lanes == head, wide, 0.0).astype(BF) for head in range(2)]
    return jnp.concatenate(parts, axis=0)


def join_heads(array):
    rows = array.shape[0] // 2
    lanes = lax.broadcasted_iota(jnp.int32, (rows, LANES), 1) // (LANES // 2)
    return jnp.where(lanes == 0, array[:rows], array[rows:]).astype(BF)


def attend_kernel(q_ref, kv_ref, window_ref, out_ref, prob_ref):
    half, seq = q_ref.shape[0] // 2, kv_ref.shape[1]
    window = seq + 2 * half
    q = split_heads(q_ref[...], (LANES // 2) ** -0.5)
    raw = contract_cols(q, kv_ref[0])
    tiles = jnp.broadcast_to(window_ref[...][:, None], (4, half, window))
    tiles = [
        pltpu.roll(tiles[part], window - half + 1, axis=1, stride=1, stride_axis=0)[:, :seq]
        for part in range(4)
    ]
    scores = raw + jnp.concatenate(tiles, axis=0)
    exps = jnp.exp(scores - jnp.max(scores, axis=1, keepdims=True))
    prob = (exps * (1.0 / jnp.sum(exps, axis=1, keepdims=True))).astype(BF)
    prob_ref[...] = prob.reshape(prob_ref.shape)
    out_ref[...] = join_heads(jnp.dot(prob, kv_ref[1], preferred_element_type=F32))


def attend(queries, key_value, windows):
    rows, width = queries.shape
    pairs, seq = key_value.shape[1:3]
    work = rows * seq * width
    return pl.pallas_call(
        attend_kernel,
        grid=(pairs,),
        in_specs=[
            pl.BlockSpec((rows, LANES), lambda h: (0, h)),
            pl.BlockSpec((2, None, seq, LANES), lambda h: (0, h, 0, 0)),
            pl.BlockSpec((None, 4, windows.shape[2]), lambda h: (h, 0, 0)),
        ],
        out_specs=[
            pl.BlockSpec((rows, LANES), lambda h: (0, h)),
            pl.BlockSpec((2, rows, seq), lambda h: (h, 0, 0)),
        ],
        out_shape=[
            jax.ShapeDtypeStruct((rows, width), BF),
            jax.ShapeDtypeStruct((2 * pairs, rows, seq), BF),
        ],
        compiler_params=pltpu.CompilerParams(vmem_limit_bytes=VMEM_LIMIT),
        cost_estimate=pl.CostEstimate(
            flops=8 * work,
            bytes_accessed=4 * seq * width + 4 * pairs * rows * seq,
            transcendentals=2 * pairs * rows * seq,
        ),
        name="attend",
    )(queries, key_value, windows)


def attend_back_kernel(prob_ref, q_ref, kv_ref, grad_ref, dq_ref, dkv_ref, diag_ref):
    half, seq = q_ref.shape[0] // 2, kv_ref.shape[1]
    factor = (LANES // 2) ** -0.5
    rows = 4 * half
    q = split_heads(q_ref[...], factor)
    grad = split_heads(grad_ref[...], 1.0)
    prob = prob_ref[...].reshape(rows, seq)
    wide = prob.astype(F32)
    prob_grad = contract_cols(grad, kv_ref[1])
    inner = jnp.sum(wide * prob_grad, axis=1, keepdims=True)
    score_grad = wide * (prob_grad - inner)
    tiles = jnp.concatenate([score_grad, jnp.zeros((rows, 2 * half), F32)], axis=1)
    diag_ref[...] = shear(tiles.reshape(4, half, seq + 2 * half))
    score_grad = score_grad.astype(BF)
    query_grad = jnp.dot(score_grad, kv_ref[0], preferred_element_type=F32) * factor
    dq_ref[...] = join_heads(query_grad)
    dkv_ref[0] = contract_rows(q, score_grad).T.astype(BF)
    dkv_ref[1] = contract_rows(grad, prob).T.astype(BF)


def attend_back(prob, queries, key_value, attended_grad):
    rows, width = queries.shape
    pairs, seq = key_value.shape[1:3]
    window = seq + rows
    row_spec = pl.BlockSpec((rows, LANES), lambda h: (0, h))
    kv_spec = pl.BlockSpec((2, None, seq, LANES), lambda h: (0, h, 0, 0))
    return pl.pallas_call(
        attend_back_kernel,
        grid=(pairs,),
        in_specs=[
            pl.BlockSpec((2, rows, seq), lambda h: (h, 0, 0)),
            row_spec,
            kv_spec,
            row_spec,
        ],
        out_specs=[
            row_spec,
            kv_spec,
            pl.BlockSpec((None, 4, window), lambda h: (h, 0, 0)),
        ],
        out_shape=[
            jax.ShapeDtypeStruct((rows, width), BF),
            jax.ShapeDtypeStruct(key_value.shape, BF),
            jax.ShapeDtypeStruct((pairs, 4, window), F32),
        ],
        compiler_params=pltpu.CompilerParams(vmem_limit_bytes=VMEM_LIMIT),
        cost_estimate=pl.CostEstimate(
            flops=16 * rows * seq * width,
            bytes_accessed=8 * seq * width + 4 * pairs * rows * seq,
            transcendentals=0,
        ),
        name="attend_back",
    )(prob, queries, key_value, attended_grad)


def key_value_kernel(place_ref, near_ref, far_ref, gain_ref, wk_ref, wv_ref, normed_ref, kv_ref, *, half):
    tile = normed_ref.shape[0] // half
    near_blocks = near_ref.shape[0] // half
    rows = []
    for block in range(tile):
        source = place_ref[pl.program_id(0) * tile + block]
        at = pl.ds(pl.multiple_of(lax.rem(source, near_blocks) * half, half), half)
        rows.append(jnp.where(source < near_blocks, near_ref[at].astype(F32), far_ref[at].astype(F32)))
    inputs = jnp.concatenate(rows, axis=0)
    normed = (inputs * norm_scale(inputs) * gain_ref[...]).astype(BF)
    normed_ref[...] = normed
    for part, weight_ref in enumerate((wk_ref, wv_ref)):
        out = jnp.dot(normed, weight_ref[...], preferred_element_type=F32).astype(BF)
        for pair in range(kv_ref.shape[1]):
            kv_ref[part, pair] = out[:, pair * LANES : (pair + 1) * LANES]


def keys_and_values(place, near, far, gain, w_qkv, half):
    near_rows, width = near.shape
    seq = 2 * near_rows
    tile = 8 * half
    return pl.pallas_call(
        functools.partial(key_value_kernel, half=half),
        grid_spec=pltpu.PrefetchScalarGridSpec(
            num_scalar_prefetch=1,
            grid=(seq // tile,),
            in_specs=[
                pl.BlockSpec((near_rows, width), lambda r, p: (0, 0)),
                pl.BlockSpec((near_rows, width), lambda r, p: (0, 0)),
                pl.BlockSpec((1, width), lambda r, p: (0, 0)),
                pl.BlockSpec((width, width), lambda r, p: (0, 1)),
                pl.BlockSpec((width, width), lambda r, p: (0, 2)),
            ],
            out_specs=[
                pl.BlockSpec((tile, width), lambda r, p: (r, 0)),
                pl.BlockSpec((2, width // LANES, tile, LANES), lambda r, p: (0, 0, r, 0)),
            ],
        ),
        out_shape=[
            jax.ShapeDtypeStruct((seq, width), BF),
            jax.ShapeDtypeStruct((2, width // LANES, seq, LANES), BF),
        ],
        compiler_params=pltpu.CompilerParams(vmem_limit_bytes=VMEM_LIMIT),
        cost_estimate=pl.CostEstimate(
            flops=4 * seq * width * width, bytes_accessed=8 * seq * width, transcendentals=seq
        ),
        name="keys_and_values",
    )(place, near, far, gain[None], w_qkv, w_qkv)


def normed_grad_kernel(position_ref, dkv_ref, wk_ref, wv_ref, out_ref, *, half):
    tile = out_ref.shape[0] // half
    out = 0.0
    for part, weight_ref in enumerate((wk_ref, wv_ref)):
        rows = []
        for block in range(tile):
            source = position_ref[pl.program_id(0) * tile + block]
            at = pl.ds(pl.multiple_of(source * half, half), half)
            pairs = [dkv_ref[part, pair, at] for pair in range(dkv_ref.shape[1])]
            rows.append(jnp.concatenate(pairs, axis=1))
        out += contract_cols(jnp.concatenate(rows, axis=0), weight_ref[...])
    out_ref[...] = out.astype(BF)


def normed_grads(position, key_value_grad, w_qkv, half):
    width = w_qkv.shape[0]
    rows = position.shape[0] * half
    tile = 8 * half
    return pl.pallas_call(
        functools.partial(normed_grad_kernel, half=half),
        grid_spec=pltpu.PrefetchScalarGridSpec(
            num_scalar_prefetch=1,
            grid=(rows // tile,),
            in_specs=[
                pl.BlockSpec(key_value_grad.shape, lambda r, p: (0, 0, 0, 0)),
                pl.BlockSpec((width, width), lambda r, p: (0, 1)),
                pl.BlockSpec((width, width), lambda r, p: (0, 2)),
            ],
            out_specs=pl.BlockSpec((tile, width), lambda r, p: (r, 0)),
        ),
        out_shape=jax.ShapeDtypeStruct((rows, width), BF),
        compiler_params=pltpu.CompilerParams(vmem_limit_bytes=VMEM_LIMIT),
        cost_estimate=pl.CostEstimate(
            flops=4 * rows * width * width, bytes_accessed=8 * rows * width, transcendentals=0
        ),
        name="normed_grads",
    )(position, key_value_grad, w_qkv, w_qkv)


def weight_grad_kernel(
    core_ref,
    dq_ref,
    normed_ref,
    dkv_ref,
    all_normed_ref,
    attended_ref,
    branch_ref,
    extra_ref,
    kept_ref,
    given_ref,
):
    step = pl.program_id(0)
    side = kept_ref.shape[1]

    def give(total):
        left, right = total[:, :side].astype(BF), total[:, side:].astype(BF)
        rows = total.shape[0]

        @pl.when(core_ref[0] == 0)
        def _():
            kept_ref[:rows] = left
            given_ref[:rows] = right

        @pl.when(core_ref[0] != 0)
        def _():
            kept_ref[:rows] = right
            given_ref[:rows] = left

    @pl.when(step == 0)
    def _():
        give(contract_rows(dq_ref[...], normed_ref[...]))

    @pl.when((step == 1) | (step == 2))
    def _():
        pairs = [dkv_ref[pair] for pair in range(dkv_ref.shape[0])]
        give(contract_rows(jnp.concatenate(pairs, axis=1), all_normed_ref[...]))

    @pl.when(step == 3)
    def _():
        give(contract_rows(attended_ref[...], branch_ref[...]))

    @pl.when(step == 4)
    def _():
        give(extra_ref[...])


def weight_grads(
    core, query_grad, normed_one, key_value_grad, all_normed, attended, branch_grad, extra
):
    rows, width = normed_one.shape
    seq = all_normed.shape[0]
    total = 4 * width + extra.shape[0]
    row_spec = pl.BlockSpec((rows, width), lambda t, p: (0, 0))
    out_spec = pl.BlockSpec((width, width // 2), lambda t, p: (t, 0))
    out_shape = jax.ShapeDtypeStruct((total, width // 2), BF)
    return pl.pallas_call(
        weight_grad_kernel,
        grid_spec=pltpu.PrefetchScalarGridSpec(
            num_scalar_prefetch=1,
            grid=(5,),
            in_specs=[
                row_spec,
                row_spec,
                pl.BlockSpec(
                    (None, width // LANES, seq, LANES), lambda t, p: (jnp.clip(t - 1, 0, 1), 0, 0, 0)
                ),
                pl.BlockSpec((seq, width), lambda t, p: (0, 0)),
                row_spec,
                row_spec,
                pl.BlockSpec(extra.shape, lambda t, p: (0, 0)),
            ],
            out_specs=[out_spec, out_spec],
        ),
        out_shape=[out_shape, out_shape],
        compiler_params=pltpu.CompilerParams(vmem_limit_bytes=VMEM_LIMIT),
        cost_estimate=pl.CostEstimate(
            flops=4 * seq * width * width, bytes_accessed=10 * seq * width, transcendentals=0
        ),
        name="weight_grads",
    )(core, query_grad, normed_one, key_value_grad, all_normed, attended, branch_grad, extra)


def whole_grad_kernel(core_ref, mine_ref, other_ref, weight_ref, grad_ref, product_ref, out_ref):
    step = pl.program_id(0)
    last = pl.num_programs(0) - out_ref.shape[0] // mine_ref.shape[0]
    side, tile = mine_ref.shape[1], mine_ref.shape[0]
    width = 2 * side
    mine_at = pl.ds(pl.multiple_of(core_ref[0] * side, side), side)
    other_at = pl.ds(pl.multiple_of(side - core_ref[0] * side, side), side)

    @pl.when(step < last)
    def _():
        grad_ref[mine_at, :] = mine_ref[...].astype(F32).T
        grad_ref[other_at, :] = other_ref[...].astype(F32).T
        product = jnp.sum(grad_ref[...] * weight_ref[...].astype(F32), axis=1, keepdims=True)
        product = jnp.broadcast_to(product, (width, LANES))

        @pl.when(step == 0)
        def _():
            product_ref[...] = product

        @pl.when(step > 0)
        def _():
            product_ref[...] += product

    @pl.when(step >= last)
    def _():
        at = pl.ds(pl.multiple_of((step - last) * tile, tile), tile)

        @pl.when(core_ref[0] == 0)
        def _():
            out_ref[at, :side] = mine_ref[...].astype(F32)
            out_ref[at, side:] = other_ref[...].astype(F32)

        @pl.when(core_ref[0] != 0)
        def _():
            out_ref[at, :side] = other_ref[...].astype(F32)
            out_ref[at, side:] = mine_ref[...].astype(F32)


def whole_grad(core, mine, other, weight):
    width, columns = weight.shape
    side = mine.shape[1]
    tile = width
    count = columns // tile
    half_spec = pl.BlockSpec((tile, side), lambda t, p: (t, 0))
    whole_spec = pl.BlockSpec((width, tile), lambda t, p: (0, jnp.minimum(t, count - 1)))
    return pl.pallas_call(
        whole_grad_kernel,
        grid_spec=pltpu.PrefetchScalarGridSpec(
            num_scalar_prefetch=1,
            grid=(count + width // tile,),
            in_specs=[half_spec, half_spec, whole_spec],
            out_specs=[
                whole_spec,
                pl.BlockSpec((width, LANES), lambda t, p: (0, 0)),
                pl.BlockSpec((width, width), lambda t, p: (0, 0)),
            ],
        ),
        out_shape=[
            jax.ShapeDtypeStruct((width, columns), F32),
            jax.ShapeDtypeStruct((width, LANES), F32),
            jax.ShapeDtypeStruct((width, width), F32),
        ],
        compiler_params=pltpu.CompilerParams(vmem_limit_bytes=VMEM_LIMIT),
        cost_estimate=pl.CostEstimate(
            flops=2 * width * columns, bytes_accessed=8 * width * columns, transcendentals=0
        ),
        name="whole_grad",
    )(core, mine, other, weight)


def expert_rows(x_ref, cot_ref):
    width = cot_ref.shape[-1]
    rows = x_ref.shape[0] * x_ref.shape[1]
    rows_in = x_ref[...].reshape(rows, x_ref.shape[2])
    gate = jnp.sum(rows_in[:, width:].astype(F32), axis=1, keepdims=True)
    slot_grad = (cot_ref[...].reshape(rows, width).astype(F32) * gate).astype(BF)
    return rows_in[:, :width], slot_grad


def high_and_low(column):
    high = column.astype(BF).astype(F32)
    lanes = lax.broadcasted_iota(jnp.int32, (column.shape[0], LANES), 1)
    wide = jnp.where(lanes == 0, high, jnp.where(lanes == 1, column - high, 0.0))
    return wide.astype(BF)


def write_weight_grads(x, slot_grad, activated, pre_grad, grad_ref):
    grad_in = contract_rows(pre_grad, x).astype(BF)
    grad_out = contract_rows(activated, slot_grad).astype(BF)
    slices, hidden = grad_ref.shape[0], grad_ref.shape[1] // 2
    for index in range(slices):
        grad_ref[index, :hidden] = grad_in[index * hidden : (index + 1) * hidden]
        grad_ref[index, hidden:] = grad_out[index * hidden : (index + 1) * hidden]


def expert_kernel(
    x_ref,
    cot_ref,
    weight_ref,
    dx_ref,
    ret_ref,
    first_grad_ref,
    act_ref,
    pre_grad_ref,
    ret_sum,
    dx_sum,
):
    part = pl.program_id(1)
    width = cot_ref.shape[-1]
    x, slot_grad = expert_rows(x_ref, cot_ref)
    slices, hidden = weight_ref.shape[0], weight_ref.shape[1] // 2
    weights = [weight_ref[index] for index in range(slices)]
    weight_in = jnp.concatenate([weight[:hidden] for weight in weights], axis=0)
    weight_out = jnp.concatenate([weight[hidden:] for weight in weights], axis=0)
    pre = contract_cols(x, weight_in)
    act_grad = contract_cols(slot_grad, weight_out)
    cumulative = 0.5 * (1.0 + lax.erf(pre * 0.7071067811865476))
    activated = (pre * cumulative).astype(BF)
    slope = cumulative + pre * (jnp.exp(-0.5 * pre * pre) * 0.3989422804014327)
    pre_grad = (act_grad * slope).astype(BF)
    returned = jnp.dot(activated, weight_out, preferred_element_type=F32)
    input_grad = jnp.dot(pre_grad, weight_in, preferred_element_type=F32)

    @pl.when(pl.program_id(0) == 0)
    def _():
        write_weight_grads(x, slot_grad, activated, pre_grad, first_grad_ref)

    @pl.when(pl.program_id(0) > 0)
    def _():
        act_ref[...] = activated
        pre_grad_ref[...] = pre_grad

    @pl.when(part == 0)
    def _():
        ret_sum[...] = returned
        dx_sum[...] = input_grad

    @pl.when(part > 0)
    def _():
        ret_sum[...] += returned
        dx_sum[...] += input_grad

    @pl.when(part == pl.num_programs(1) - 1)
    def _():
        shape = cot_ref.shape
        rows = shape[0] * shape[1]
        ret = ret_sum[...]
        ret_ref[...] = ret.astype(BF).reshape(shape)
        upstream = cot_ref[...].reshape(rows, width).astype(F32)
        gate_grad = high_and_low(jnp.sum(ret * upstream, axis=1, keepdims=True))
        dx_ref[:, :, :width] = dx_sum[...].astype(BF).reshape(shape)
        dx_ref[:, :, width:] = gate_grad.reshape(shape[0], shape[1], LANES)


def expert_grad_kernel(x_ref, cot_ref, act_ref, pre_grad_ref, grad_ref):
    x, slot_grad = expert_rows(x_ref, cot_ref)
    write_weight_grads(x, slot_grad, act_ref[...], pre_grad_ref[...], grad_ref)


def run_experts(x_rows, cot_rows, weights):
    devices, experts, slots, width = cot_rows.shape
    wide = x_rows.shape[3]
    parts, _, both, _ = weights.shape
    hidden = both // 2
    rows = devices * slots
    slices = 2
    steps = parts // slices

    def row_spec(columns):
        return pl.BlockSpec((devices, None, slots, columns), lambda e, w: (0, e, 0, 0))

    later = experts - 1
    hidden_spec = pl.BlockSpec(
        (None, rows, slices * hidden),
        lambda e, w: (jnp.maximum(e - 1, 0), 0, jnp.where(e == 0, 0, w)),
    )
    hidden_shape = jax.ShapeDtypeStruct((later, rows, parts * hidden), BF)
    grad_shape = jax.ShapeDtypeStruct((parts, both, width), BF)
    work = experts * rows * width * parts * hidden
    params = pltpu.CompilerParams(vmem_limit_bytes=VMEM_LIMIT)
    input_grad, returned, first_grad, activated, pre_grad = pl.pallas_call(
        expert_kernel,
        grid=(experts, steps),
        in_specs=[
            row_spec(wide),
            row_spec(width),
            pl.BlockSpec((slices, None, both, width), lambda e, w: (w, e, 0, 0)),
        ],
        out_specs=[
            row_spec(width + LANES),
            row_spec(width),
            pl.BlockSpec(
                (slices, both, width), lambda e, w: (jnp.where(e == 0, w, steps - 1), 0, 0)
            ),
            hidden_spec,
            hidden_spec,
        ],
        out_shape=[
            jax.ShapeDtypeStruct((devices, experts, slots, width + LANES), BF),
            jax.ShapeDtypeStruct((devices, experts, slots, width), BF),
            grad_shape,
            hidden_shape,
            hidden_shape,
        ],
        scratch_shapes=[pltpu.VMEM((rows, width), F32), pltpu.VMEM((rows, width), F32)],
        compiler_params=params,
        cost_estimate=pl.CostEstimate(
            flops=10 * work,
            bytes_accessed=8 * experts * rows * width + 4 * parts * experts * width * hidden,
            transcendentals=2 * experts * rows * parts * hidden,
        ),
        name="experts",
    )(x_rows, cot_rows, weights)
    weight_grads_of = [first_grad]
    for expert in range(1, experts):

        def own_rows(columns, expert=expert):
            return pl.BlockSpec((devices, None, slots, columns), lambda w: (0, expert, 0, 0))

        own_hidden = pl.BlockSpec(
            (None, rows, slices * hidden), lambda w, expert=expert: (expert - 1, 0, w)
        )
        weight_grads_of.append(
            pl.pallas_call(
                expert_grad_kernel,
                grid=(steps,),
                in_specs=[own_rows(wide), own_rows(width), own_hidden, own_hidden],
                out_specs=pl.BlockSpec((slices, both, width), lambda w: (w, 0, 0)),
                out_shape=grad_shape,
                compiler_params=params,
                cost_estimate=pl.CostEstimate(
                    flops=4 * work // experts,
                    bytes_accessed=8 * rows * width + 4 * parts * width * hidden,
                    transcendentals=0,
                ),
                name="expert_grads",
            )(x_rows, cot_rows, activated, pre_grad)
        )
    return input_grad, returned, weight_grads_of


def on_device(
    tokens,
    gain_attn,
    w_qkv,
    rel_bias,
    w_attn_out,
    gain_ffn,
    w_router,
    w_in,
    w_out,
    routes,
    pair_order,
    bucket_table,
    cotangent,
):
    tok_rows = tokens.shape[1]
    model_width = tokens.shape[2]
    head_count = rel_bias.shape[1]
    bucket_count = rel_bias.shape[0]
    ctx_count = lax.axis_size(CTX)
    half = tok_rows // 2
    blocks = 2 * ctx_count
    seq = half * blocks
    window = seq + 2 * half
    head_pairs = head_count // 2
    local_experts = w_in.shape[0]
    experts = w_router.shape[1]
    capacity = 4 * tok_rows // experts
    device_slots = local_experts * capacity
    expert_devices = lax.axis_size(EXPERT_AXES)
    copies = expert_devices // ctx_count

    near_tokens = spread(tokens[0], SAME_CORE)
    far_tokens = lax.ppermute(near_tokens, "core", SWAP)
    near_tokens = near_tokens.reshape(seq // 2, model_width)
    far_tokens = far_tokens.reshape(seq // 2, model_width)
    weights = jnp.concatenate([w_in.transpose(0, 2, 1), w_out], axis=1)
    weights = lax.all_gather(weights, "x", axis=0)

    chosen = routes[0].T
    expert_ids = jnp.arange(experts, dtype=jnp.int32)
    flat_expert = chosen.reshape(2 * tok_rows)
    member = flat_expert[:, None] == expert_ids[None, :]
    picks = jnp.arange(2 * tok_rows, dtype=jnp.int32)
    before = (picks[:, None] > picks[None, :]).astype(BF)
    counts = jnp.dot(before, member.astype(BF), preferred_element_type=F32)
    slot_rank = jnp.sum(jnp.where(member, counts, 0.0), axis=1).astype(jnp.int32)
    owner_index = flat_expert // local_experts
    slot_of = (flat_expert % local_experts) * capacity + slot_rank
    slot_ids = jnp.arange(expert_devices * device_slots, dtype=jnp.int32)
    slot_hot = (owner_index[:, None] == (slot_ids // (copies * device_slots))[None, :]) & (
        slot_of[:, None] == (slot_ids % device_slots)[None, :]
    )
    slot_table = slot_hot.astype(BF)
    token_table = slot_table[:tok_rows] + slot_table[tok_rows:]

    def to_experts(table, rows):
        slots = contract_rows(table, rows).astype(BF)
        arrived = exchange(slots.reshape(expert_devices, device_slots, rows.shape[1]), EXPERT_AXES)
        return arrived.reshape(expert_devices, local_experts, capacity, rows.shape[1])

    cot_rows = to_experts(token_table, cotangent[0])

    ctx_ids = jnp.arange(ctx_count, dtype=jnp.int32)
    my_core = lax.axis_index("core")
    near = (ctx_ids % 2) == my_core
    lies = 2 * (jnp.where(near, 0, ctx_count // 2) + ctx_ids // 2)
    block_ids = jnp.arange(blocks, dtype=jnp.int32)[:, None]
    place = jnp.sum(
        jnp.where(pair_order[None, :] == block_ids, lies[None, :], 0)
        + jnp.where(blocks - 1 - pair_order[None, :] == block_ids, lies[None, :] + 1, 0),
        axis=1,
        dtype=jnp.int32,
    )
    positions = jnp.sum(
        jnp.where(
            2 * (block_ids // 2) == lies[None, :],
            jnp.where(block_ids % 2 == 0, pair_order[None, :], blocks - 1 - pair_order[None, :]),
            0,
        ),
        axis=1,
        dtype=jnp.int32,
    )
    my_pair = jnp.sum(jnp.where(ctx_ids == lax.axis_index(CTX), pair_order, 0))
    reversed_table = jnp.pad(bucket_table[::-1], (0, window - half), constant_values=-1)
    diagonal_bucket = jnp.stack(
        [
            lax.dynamic_slice(reversed_table, (seq - half - block * half,), (window,))
            for block in (my_pair, blocks - 1 - my_pair)
        ]
    ).reshape(1, 2 * window)
    bucket_ids = jnp.arange(bucket_count, dtype=jnp.int32)
    bucket_hot = (diagonal_bucket == bucket_ids[:, None]).astype(F32)
    windows = lax.dot_general(rel_bias, bucket_hot, ROWS, precision=HIGHEST)
    windows = jnp.where(diagonal_bucket >= 0, windows, MASKED)
    windows = windows.reshape(head_pairs, 4, window)

    inputs = tokens[0].astype(F32)
    scale_one = norm_scale(inputs)
    normed_one = (inputs * scale_one * gain_attn).astype(BF)
    w_q = w_qkv[:, :model_width]
    queries = jnp.dot(normed_one, w_q, preferred_element_type=F32).astype(BF)
    all_normed, key_value = keys_and_values(
        place, near_tokens, far_tokens, gain_attn, w_qkv, half
    )
    attended, probabilities = attend(queries, key_value, windows)
    residual_one = inputs + jnp.dot(attended, w_attn_out, preferred_element_type=F32)
    scale_two = norm_scale(residual_one)
    normed_two = (residual_one * scale_two * gain_ffn).astype(BF)

    router_logits = jnp.dot(normed_two, w_router, preferred_element_type=F32)
    chosen_hot = (chosen[:, :, None] == expert_ids[None, None, :]).astype(F32)
    picked_logits = jnp.sum(chosen_hot * router_logits[None], axis=2)
    logit_peak = jnp.max(picked_logits, axis=0, keepdims=True)
    gate_exp = jnp.exp(picked_logits - logit_peak)
    gate_weights = (gate_exp / jnp.sum(gate_exp, axis=0, keepdims=True))[:, :, None]

    flat_gate = gate_weights.reshape(2 * tok_rows, 1)
    gate_lanes = high_and_low(flat_gate)
    pick_rows = jnp.concatenate([normed_two, normed_two], axis=0)
    x_rows = to_experts(slot_table, jnp.concatenate([pick_rows, gate_lanes], axis=1))
    input_grad, returned, parts = run_experts(x_rows, cot_rows, weights)

    def from_experts(rows):
        rows = exchange(rows.reshape(expert_devices, device_slots, rows.shape[3]), EXPERT_AXES)
        return rows.reshape(expert_devices * device_slots, rows.shape[2])

    input_grad = from_experts(input_grad)
    later_parts, input_grad, returned = lax.optimization_barrier(
        (parts[1:], input_grad, returned)
    )
    shares = [
        lax.psum_scatter(part, "x", scatter_dimension=0) for part in (parts[0], *later_parts)
    ]
    expert_part = jnp.dot(
        token_table, input_grad[:, :model_width], preferred_element_type=F32
    )
    gate_grad = jnp.dot(slot_table, input_grad[:, model_width:], preferred_element_type=F32)
    gate_grad = jnp.sum(gate_grad.reshape(2, tok_rows, LANES), axis=2, keepdims=True)
    returned = from_experts(returned)

    upstream = cotangent[0].astype(F32)
    inner_mean = jnp.sum(gate_weights * gate_grad, axis=0, keepdims=True)
    pick_grad = gate_weights * (gate_grad - inner_mean)
    logit_grad = jnp.sum(pick_grad * chosen_hot, axis=0)
    grad_w_router = lax.dot_general(normed_two.astype(F32), logit_grad, ROWS, precision=HIGHEST)
    router_back = lax.dot_general(logit_grad, w_router.astype(F32), COLS, precision=HIGHEST)
    normed_two_grad = expert_part + router_back
    norm_part, grad_gain_ffn = norm_backward(residual_one, scale_two, gain_ffn, normed_two_grad)
    mixed_grad = upstream + norm_part
    branch_grad = mixed_grad.astype(BF)

    attended_grad = contract_cols(branch_grad, w_attn_out).astype(BF)
    query_grad, key_value_grad, diagonals = attend_back(
        probabilities, queries, key_value, attended_grad
    )
    query_grad, returned = lax.optimization_barrier((query_grad, returned))
    diagonals = diagonals.reshape(head_count, 2 * window)
    grad_rel_bias = lax.dot_general(bucket_hot, diagonals, COLS, precision=HIGHEST)

    core = jnp.reshape(my_core, (1,)).astype(jnp.int32)
    side = model_width // 2
    biases = bucket_count * head_count
    bias_row = jnp.pad(grad_rel_bias.reshape(1, biases), ((0, 0), (0, model_width - biases)))
    extra = jnp.concatenate([grad_w_router.T, grad_gain_ffn[None], bias_row], axis=0)
    spare = -(4 * model_width + extra.shape[0]) % (8 * lax.axis_size(CHIPS))
    extra = jnp.pad(extra, ((0, spare), (0, 0)))
    kept, given = weight_grads(
        core,
        query_grad,
        normed_one,
        key_value_grad,
        all_normed,
        attended,
        branch_grad,
        extra,
    )
    key_value_grad, kept, given, returned = lax.optimization_barrier(
        (key_value_grad, kept, given, returned)
    )
    picked = jnp.dot(slot_table, returned, preferred_element_type=F32)
    mixture = jnp.sum(gate_weights * picked.reshape(2, tok_rows, model_width), axis=0)
    layer_out = (residual_one + mixture).astype(BF)[None]
    share = half_share(kept, given)

    far_grad = normed_grads(positions[blocks // 2 :], key_value_grad, w_qkv, half)
    near_grad = normed_grads(positions[: blocks // 2], key_value_grad, w_qkv, half)
    near_grad = near_grad.astype(F32) + lax.ppermute(far_grad, "core", SWAP).astype(F32)
    near_grad = near_grad.astype(BF).reshape(2, ctx_count // 4, tok_rows, model_width)
    share, near_grad, layer_out, shares = lax.optimization_barrier(
        (share, near_grad, layer_out, shares)
    )
    my_ya, my_z = lax.axis_index("ya"), lax.axis_index("z")
    ring = lax.axis_size("z")
    along_z = 0.0
    for hop in range(ring):
        rows = lax.dynamic_index_in_dim(near_grad, (my_z + hop) % ring, axis=1, keepdims=False)
        if hop:
            rows = lax.ppermute(rows, "z", [(at, (at + hop) % ring) for at in range(ring)])
        along_z = along_z + rows.astype(F32)
    given = jnp.where(my_ya == 0, along_z[1], along_z[0]).astype(BF)
    kept = jnp.where(my_ya == 0, along_z[0], along_z[1])
    mine = spread(share, CHIPS).reshape(-1, side)
    hidden = w_in.shape[2]
    shares = jnp.stack(shares)
    grad_w_in = shares[:, :hidden].transpose(0, 2, 1).astype(F32)
    grad_w_out = shares[:, hidden:].astype(F32)
    mine, given, grad_w_in, grad_w_out = lax.optimization_barrier(
        (mine, given, grad_w_in, grad_w_out)
    )
    other = lax.ppermute(mine, "core", SWAP)
    normed_one_grad = kept + lax.ppermute(given, "ya", SWAP).astype(F32)
    normed_one_grad = normed_one_grad + contract_cols(query_grad, w_q)
    input_norm_grad, _ = norm_backward(inputs, scale_one, gain_attn, normed_one_grad)
    grad_tokens = (mixed_grad + input_norm_grad)[None]
    sum_w_qkv, products, sum_w_attn_out = whole_grad(core, mine, other, w_qkv)
    sum_gain_attn = products[:, 0] / gain_attn
    small = slice(4 * model_width, 4 * model_width + experts + 2)
    left = jnp.where(my_core == 0, mine[small], other[small])
    right = jnp.where(my_core == 0, other[small], mine[small])
    sums = jnp.concatenate([left, right], axis=1).astype(F32)
    sum_w_router, sum_gain_ffn = sums[:experts].T, sums[experts]
    sum_rel_bias = sums[experts + 1, :biases].reshape(bucket_count, head_count)
    return (
        layer_out,
        grad_tokens,
        sum_gain_attn,
        sum_w_qkv,
        sum_rel_bias,
        sum_w_attn_out,
        sum_gain_ffn,
        sum_w_router,
        grad_w_in,
        grad_w_out,
    )


def solution(mesh):
    split_mesh = Mesh(mesh.devices.reshape(SPLIT), EVERY)
    in_specs = (
        P(WSH, CTX, None),
        P(),
        P(),
        P(),
        P(),
        P(),
        P(),
        P(CTX, None, WSH),
        P(CTX, WSH, None),
        P(WSH, CTX, None),
        P(),
        P(),
        P(WSH, CTX, None),
    )
    out_specs = (
        P(WSH, CTX, None),
        P(WSH, CTX, None),
        P(),
        P(),
        P(),
        P(),
        P(),
        P(),
        P(CTX, None, WSH),
        P(CTX, WSH, None),
    )
    return jax.shard_map(
        on_device, mesh=split_mesh, in_specs=in_specs, out_specs=out_specs, check_vma=False
    )
```

time: 452 us -> 369 us (0.82)
  waiting for transfers between devices: 156 us -> 104 us
  starting transfers between devices: 64.6 us -> 49.9 us
  Pallas kernels: 110 us -> 101 us
  local copies, waits for them, and re-layouts: 30.3 us -> 21.7 us
    all_to_all x8 -> x6, waiting for transfers between devices: 147 us -> 54.1 us  [exchange(): return lax.all_to_all(array, axes, split_axis=0, concat_axis=0, tiled=True)]
    ppermute x4 -> x6, waiting for transfers between devices: 2.37 us -> 50.1 us  [the longest x3 42.2 us: on_device(): lax.ppermute(rows, 'z', [(at, (at + hop) % ring) for at in range(ring)])]
    pallas_call x3, Pallas kernels: 55.3 us -> 41 us  [the longest x1 20.6 us: run_experts(): pl.pallas_call(expert_kernel, grid=(experts, steps), in_specs=[row_spec(w...]
    all_to_all x8 -> x6, starting transfers between devices: 56.3 us -> 42.5 us  [exchange(): return lax.all_to_all(array, axes, split_axis=0, concat_axis=0, tiled=True)]
    unnamed x101 -> x105, local copies, waits for them, and re-layouts: 22.4 us -> 11.9 us
    all_gather x2 -> x1, waiting for transfers between devices: 4.63 us -> 0.01 us  [on_device(): weights = lax.all_gather(weights, 'x', axis=0)]
    convert_element_type x10 -> x7, other arithmetic: 13.9 us -> 11.5 us  [the longest x1 4.19 us: half_share(): (kept.astype(F32) + got.astype(F32)).astype(BF)]
  transfers between devices with their start and end apart: 18 -> 17, of which waited for: 9 -> 8; matrix products, arithmetic and copies ran while one was open for 11% -> 13% of each run, Pallas kernels for 16% -> 19%
where the time goes in v1:
time: 369 us; the launch traced here: 368 us
  waiting for transfers between devices  104 us (28%)
  Pallas kernels  101 us (27%)
  starting transfers between devices  49.9 us (14%)
  blocking collectives  32 us (9%)
  other arithmetic  25.8 us (7%)
  local copies, waits for them, and re-layouts  21.7 us (6%)
  matrix products  17.8 us (5%)
  between operations  15.8 us (4%)
    all_to_all x6, waiting for transfers between devices, exchange(): return lax.all_to_all(array, axes, split_axis=0, concat_axis=0, tiled=True)  54.1 us
    all_to_all x6, starting transfers between devices, exchange(): return lax.all_to_all(array, axes, split_axis=0, concat_axis=0, tiled=True)  42.5 us
    ppermute x3, waiting for transfers between devices, on_device(): lax.ppermute(rows, 'z', [(at, (at + hop) % ring) for at in range(ring)])  42.2 us
    all_to_all x1, blocking collectives, exchange(): return lax.all_to_all(array, axes, split_axis=0, concat_axis=0, tiled=True)  32 us
    pallas_call x1, Pallas kernels, run_experts(): pl.pallas_call(expert_kernel, grid=(experts, steps), in_specs=[row_spec(w...  20.6 us
    pallas_call x2, Pallas kernels, normed_grads(): pl.pallas_call(functools.partial(normed_grad_kernel, half=half), grid_spe...  15.9 us
    pallas_call x1, Pallas kernels, attend_back(): pl.pallas_call(attend_back_kernel, grid=(pairs,), in_specs=[pl.BlockSpec(...  13.8 us
    pallas_call x1, Pallas kernels, weight_grads(): pl.pallas_call(weight_grad_kernel, grid_spec=pltpu.PrefetchScalarGridSpec...  12 us
  transfers between devices with their start and end apart: 17, of which 8 were waited for; matrix products, arithmetic and copies ran while one was open for 13% of the time, Pallas kernels for 19%

profile of v1, /device:TPU:1, one launch (start us, length us, event | category | flops | bytes accessed | tf_op | source)
XLA Modules:
  0.0 367.8 jit_solution(13854837230938062237)
XLA Ops:
  13.9 8.6 %all-to-all-start = ((bf16[8,128,768]{2,1,0:T(8,128)(2,1)}), bf16[8,128,768]{2,1,0:T(8,128)(2,1)S(1)}, u32[]{:S(2)}, u32[]{:S(2)}) async-start(bf16[8,128,768]{2,1,0:T(8,128)(2,1)} %broadcast_in_dim.100), calls=%async_computation | async-start | bytes 3145728 | tf_op jit(solution)/shard_map/all_to_all | solution.py:53
  28.4 14.6 %all-to-all-done = bf16[8,128,768]{2,1,0:T(8,128)(2,1)S(1)} async-done(((bf16[8,128,768]{2,1,0:T(8,128)(2,1)}), bf16[8,128,768]{2,1,0:T(8,128)(2,1)S(1)}, u32[]{:S(2)}, u32[]{:S(2)}) %all-to-all-start) | async-done | bytes 1572896 | tf_op jit(solution)/shard_map/all_to_all | solution.py:53
  44.2 6.2 %all-to-all-start.2 = ((bf16[32,32,768]{2,1,0:T(8,128)(2,1)}), bf16[32,32,768]{2,1,0:T(8,128)(2,1)S(1)}, u32[]{:S(2)}, u32[]{:S(2)}) async-start(bf16[32,32,768]{2,1,0:T(8,128)(2,1)} %bitcast.13), calls=%async_computation.2 | async-start | bytes 3145728 | tf_op jit(solution)/shard_map/all_to_all | solution.py:53
  55.7 11.1 %keys_and_values.1 = (bf16[2048,768]{1,0:T(8,128)(2,1)}, bf16[2,6,2048,128]{3,2,1,0:T(8,128)(2,1)}) custom-call(s32[32]{0:T(128)} %get-tuple-element.123.place_ref, bf16[1024,768]{1,0:T(8,128)(2,1)} %bitcast.114, bf16[1024,768]{1,0:T(8,128)(2,1)} %bitcast.2.far_ref, f32[1,768]{1,0:T(1,128)} %broadcast_in_dim.144.gain_ref, bf16[768,2304]{1,0:T(8,128)(2,1)} %weight_ref.1, ...), custom_call_target="tpu_custom_call" | custom-call | flops 4831838208 | bytes 12582912 | tf_op jit(solution)/shard_map/keys_and_values/pallas_call | solution.py:220
  66.8 11.6 %attend.1 = (bf16[128,768]{1,0:T(8,128)(2,1)}, bf16[12,128,2048]{2,1,0:T(8,128)(2,1)}) custom-call(bf16[128,768]{1,0:T(8,128)(2,1)} %convolution_convert_fusion.3.q_ref, bf16[2,6,2048,128]{3,2,1,0:T(8,128)(2,1)} %get-tuple-element.45.kv_ref, f32[6,4,2176]{2,1,0:T(4,128)} %reshape.419.window_ref), custom_call_target="tpu_custom_call" | custom-call | flops 1610612736 | bytes 12582912 | tf_op jit(solution)/shard_map/attend/pallas_call | solution.py:118
  85.2 32.0 %all_to_all.35 = bf16[32,32,896]{2,1,0:T(8,128)(2,1)} all-to-all(bf16[32,32,896]{2,1,0:T(8,128)(2,1)} %bitcast.113), channel_id=1, replica_groups=mesh['ya'=2,'z'=4,'core'=2,'yb'=2,'x'=4] {'ya','z','core','yb'}, dimensions={0} | all-to-all | bytes 3670016 | tf_op jit(solution)/shard_map/all_to_all | solution.py:53
  117.2 20.6 %experts.1 = (bf16[32,2,16,896]{3,2,1,0:T(8,128)(2,1)}, bf16[32,2,16,768]{3,2,1,0:T(8,128)(2,1)}, bf16[4,768,768]{2,1,0:T(8,128)(2,1)}, bf16[1,512,1536]{2,1,0:T(8,128)(2,1)}, bf16[1,512,1536]{2,1,0:T(8,128)(2,1)}) custom-call(bf16[32,2,16,896]{3,2,1,0:T(8,128)(2,1)} %bitcast.104, bf16[32,2,16,768]{3,2,1,0:T(8,128)(2,1)} %bitcast.108, ...), custom_call_target="tpu_custom_call" | custom-call | flops 12079595520 | bytes 15728640 | tf_op jit(solution)/shard_map/experts/pallas_call | solution.py:551
  137.8 5.9 %all-to-all-start.3 = ((bf16[32,32,896]{2,1,0:T(8,128)(2,1)}), bf16[32,32,896]{2,1,0:T(8,128)(2,1)}, u32[]{:S(2)}, u32[]{:S(2)}) async-start(bf16[32,32,896]{2,1,0:T(8,128)(2,1)} %bitcast.112), calls=%async_computation.3 | async-start | bytes 3670016 | tf_op jit(solution)/shard_map/all_to_all | solution.py:53
  143.7 6.6 %expert_grads.1 = bf16[4,768,768]{2,1,0:T(8,128)(2,1)} custom-call(bf16[32,2,16,896]{3,2,1,0:T(8,128)(2,1)} %bitcast.105, bf16[32,2,16,768]{3,2,1,0:T(8,128)(2,1)} %bitcast.109, bf16[1,512,1536]{2,1,0:T(8,128)(2,1)} %get-tuple-element.48.act_ref, bf16[1,512,1536]{2,1,0:T(8,128)(2,1)} %get-tuple-element.49.pre_grad_ref), custom_call_target="tpu_custom_call" | custom-call | flops 2415919104 | bytes 7864320 | tf_op jit(solution)/shard_map/expert_grads/pallas_call | solution.py:594
  150.4 17.6 %all-to-all-done.3 = bf16[32,32,896]{2,1,0:T(8,128)(2,1)} async-done(((bf16[32,32,896]{2,1,0:T(8,128)(2,1)}), bf16[32,32,896]{2,1,0:T(8,128)(2,1)}, u32[]{:S(2)}, u32[]{:S(2)}) %all-to-all-start.3) | async-done | bytes 1835040 | tf_op jit(solution)/shard_map/all_to_all | solution.py:53
  168.0 5.9 %all-to-all-start.4 = ((bf16[32,32,768]{2,1,0:T(8,128)(2,1)}), bf16[32,32,768]{2,1,0:T(8,128)(2,1)S(1)}, u32[]{:S(2)}, u32[]{:S(2)}) async-start(bf16[32,32,768]{2,1,0:T(8,128)(2,1)} %bitcast.116), calls=%async_computation.4 | async-start | bytes 3145728 | tf_op jit(solution)/shard_map/all_to_all | solution.py:53
  183.6 13.8 %attend_back.1 = (bf16[128,768]{1,0:T(8,128)(2,1)}, bf16[2,6,2048,128]{3,2,1,0:T(8,128)(2,1)}, f32[6,4,2176]{2,1,0:T(4,128)}) custom-call(bf16[12,128,2048]{2,1,0:T(8,128)(2,1)} %get-tuple-element.46.prob_ref, bf16[128,768]{1,0:T(8,128)(2,1)} %convolution_convert_fusion.3.q_ref, bf16[2,6,2048,128]{3,2,1,0:T(8,128)(2,1)} %get-tuple-element.45.kv_ref, ...), custom_call_target="tpu_custom_call" | custom-call | flops 3221225472 | bytes 18874368 | tf_op jit(solution)/shard_map/attend_back/pallas_call | solution.py:170
  200.5 12.0 %weight_grads.1 = (bf16[3584,384]{1,0:T(8,128)(2,1)}, bf16[3584,384]{1,0:T(8,128)(2,1)}) custom-call(s32[1]{0:T(128)} %bitcast.20.core_ref, bf16[128,768]{1,0:T(8,128)(2,1)} %get-tuple-element.56.dq_ref, bf16[128,768]{1,0:T(8,128)(2,1)} %copy-done.17, bf16[2,6,2048,128]{3,2,1,0:T(8,128)(2,1)} %get-tuple-element.64.dkv_ref, ...), custom_call_target="tpu_custom_call" | custom-call | flops 4831838208 | bytes 15728640 | tf_op jit(solution)/shard_map/weight_grads/pallas_call | solution.py:344
  212.7 5.0 %collective-permute-done.1 = bf16[3584,384]{1,0:T(8,128)(2,1)S(1)} collective-permute-done((bf16[3584,384]{1,0:T(8,128)(2,1)}, bf16[3584,384]{1,0:T(8,128)(2,1)S(1)}, u32[]{:S(2)}, u32[]{:S(2)}) %collective-permute-start.1) | collective-permute-done | bytes 2752544 | tf_op jit(solution)/shard_map/ppermute | solution.py:63
  217.8 4.2 %add_convert_fusion = bf16[3584,384]{1,0:T(8,128)(2,1)} fusion(bf16[3584,384]{1,0:T(8,128)(2,1)S(1)} %collective-permute-done.1, bf16[3584,384]{1,0:T(8,128)(2,1)} %get-tuple-element.62), kind=kLoop, calls=%fused_computation.2 | loop fusion | flops 5505024 | bytes 8257536 | tf_op jit(solution)/shard_map/convert_element_type | solution.py:64
  221.9 10.3 %all-to-all-start.5 = ((bf16[64,56,384]{2,1,0:T(8,128)(2,1)}), bf16[64,56,384]{2,1,0:T(8,128)(2,1)}, u32[]{:S(2)}, u32[]{:S(2)}) async-start(bf16[64,56,384]{2,1,0:T(8,128)(2,1)} %bitcast.103), calls=%async_computation.5 | async-start | bytes 5505024 | tf_op jit(solution)/shard_map/all_to_all | solution.py:53
  232.9 8.0 %normed_grads.3 = bf16[1024,768]{1,0:T(8,128)(2,1)} custom-call(s32[16]{0:T(128)} %get-tuple-element.140.position_ref, bf16[2,6,2048,128]{3,2,1,0:T(8,128)(2,1)} %get-tuple-element.64.dkv_ref, bf16[768,2304]{1,0:T(8,128)(2,1)} %weight_ref.1, bf16[768,2304]{1,0:T(8,128)(2,1)} %weight_ref.1), custom_call_target="tpu_custom_call" | custom-call | flops 2415919104 | bytes 6291456 | tf_op jit(solution)/shard_map/normed_grads/pallas_call | solution.py:267
  242.4 7.9 %normed_grads.2 = bf16[1024,768]{1,0:T(8,128)(2,1)} custom-call(s32[16]{0:T(128)} %get-tuple-element.139.position_ref, bf16[2,6,2048,128]{3,2,1,0:T(8,128)(2,1)} %get-tuple-element.64.dkv_ref, bf16[768,2304]{1,0:T(8,128)(2,1)} %weight_ref.1, bf16[768,2304]{1,0:T(8,128)(2,1)} %weight_ref.1), custom_call_target="tpu_custom_call" | custom-call | flops 2415919104 | bytes 6291456 | tf_op jit(solution)/shard_map/normed_grads/pallas_call | solution.py:267
  252.8 21.9 %all-to-all-done.5 = bf16[64,56,384]{2,1,0:T(8,128)(2,1)} async-done(((bf16[64,56,384]{2,1,0:T(8,128)(2,1)}), bf16[64,56,384]{2,1,0:T(8,128)(2,1)}, u32[]{:S(2)}, u32[]{:S(2)}) %all-to-all-start.5) | async-done | bytes 2752544 | tf_op jit(solution)/shard_map/all_to_all | solution.py:53
  278.7 5.6 %all-to-all-start.6 = ((bf16[64,56,384]{2,1,0:T(8,128)(2,1)}), bf16[64,56,384]{2,1,0:T(8,128)(2,1)}, u32[]{:S(2)}, u32[]{:S(2)}) async-start(bf16[64,56,384]{2,1,0:T(8,128)(2,1)} %broadcast_in_dim.154), calls=%async_computation.8 | async-start | bytes 5505024 | tf_op jit(solution)/shard_map/all_to_all | solution.py:53
  292.5 31.9 %collective-permute-done.5 = bf16[2,128,768]{2,1,0:T(8,128)(2,1)} collective-permute-done((bf16[2,128,768]{2,1,0:T(8,128)(2,1)}, bf16[2,128,768]{2,1,0:T(8,128)(2,1)}, u32[]{:S(2)}, u32[]{:S(2)}) %collective-permute-start.5) | collective-permute-done | bytes 393248 | tf_op jit(solution)/shard_map/ppermute | solution.py:810
  324.3 4.3 %collective-permute-done.4 = bf16[2,128,768]{2,1,0:T(8,128)(2,1)} collective-permute-done((bf16[2,128,768]{2,1,0:T(8,128)(2,1)}, bf16[2,128,768]{2,1,0:T(8,128)(2,1)}, u32[]{:S(2)}, u32[]{:S(2)}) %collective-permute-start.4) | collective-permute-done | bytes 393248 | tf_op jit(solution)/shard_map/ppermute | solution.py:810
  328.6 6.0 %collective-permute-done.3 = bf16[2,128,768]{2,1,0:T(8,128)(2,1)} collective-permute-done((bf16[2,128,768]{2,1,0:T(8,128)(2,1)}, bf16[2,128,768]{2,1,0:T(8,128)(2,1)}, u32[]{:S(2)}, u32[]{:S(2)}) %collective-permute-start.3) | collective-permute-done | bytes 393248 | tf_op jit(solution)/shard_map/ppermute | solution.py:810
  349.7 9.0 %whole_grad.1 = (f32[768,2304]{1,0:T(8,128)}, f32[768,128]{1,0:T(8,128)}, f32[768,768]{1,0:T(8,128)}) custom-call(s32[1]{0:T(128)} %bitcast.20.core_ref, bf16[3584,384]{1,0:T(8,128)(2,1)} %bitcast.34.mine_ref, bf16[3584,384]{1,0:T(8,128)(2,1)} %collective-permute-done.7.other_ref, bf16[768,2304]{1,0:T(8,128)(2,1)} %weight_ref.1), custom_call_target="tpu_custom_call" | custom-call | flops 3538944 | bytes 14155776 | tf_op jit(solution)/shard_map/whole_grad/pallas_call | solution.py:416
  (204 shorter events, 71.5 us)
Async XLA Ops:
  7.2 71.2 %copy-start = (bf16[768,768]{1,0:T(8,128)(2,1)S(1)}, bf16[768,768]{1,0:T(8,128)(2,1)}, u32[]{:S(2)}) copy-start(bf16[768,768]{1,0:T(8,128)(2,1)} %param.17) | copy-start | bytes 3538948
  7.2 110.0 %all-gather.3.cloned.1.call-start = ((), (), s32[]{:S(2)}) async-start(), calls=%async_computation.11 | async-start | bytes 11796480 | tf_op jit(solution)/shard_map/all_gather | solution.py:649
  13.9 29.1 %all-to-all-start = ((bf16[8,128,768]{2,1,0:T(8,128)(2,1)}), bf16[8,128,768]{2,1,0:T(8,128)(2,1)S(1)}, u32[]{:S(2)}, u32[]{:S(2)}) async-start(bf16[8,128,768]{2,1,0:T(8,128)(2,1)} %broadcast_in_dim.100), calls=%async_computation | async-start | bytes 3145728 | tf_op jit(solution)/shard_map/all_to_all | solution.py:53
  25.4 25.4 %copy-start.13 = (s32[4352]{0:T(1024)}, s32[4352]{0:T(1024)S(1)}, u32[]{:S(2)}) copy-start(s32[4352]{0:T(1024)S(1)} %reshape.418) | copy-start | bytes 52228
  25.4 148.7 %copy-start.24 = (s32[1024]{0:T(1024)}, s32[1024]{0:T(1024)S(1)}, u32[]{:S(2)}) copy-start(s32[1024]{0:T(1024)S(1)} %get-tuple-element.149) | copy-start | bytes 12292
  25.4 148.7 %copy-start.26 = (s32[1024]{0:T(1024)}, s32[1024]{0:T(1024)S(1)}, u32[]{:S(2)}) copy-start(s32[1024]{0:T(1024)S(1)} %get-tuple-element.150) | copy-start | bytes 12292
  44.2 41.0 %all-to-all-start.2 = ((bf16[32,32,768]{2,1,0:T(8,128)(2,1)}), bf16[32,32,768]{2,1,0:T(8,128)(2,1)S(1)}, u32[]{:S(2)}, u32[]{:S(2)}) async-start(bf16[32,32,768]{2,1,0:T(8,128)(2,1)} %bitcast.13), calls=%async_computation.2 | async-start | bytes 3145728 | tf_op jit(solution)/shard_map/all_to_all | solution.py:53
  50.4 226.5 %reduce-scatter.3.cloned.1.call-start = ((), (), s32[]{:S(2)}) async-start(), calls=%async_computation.9 | async-start | bytes 5898240 | tf_op jit(solution)/shard_map/reduce_scatter | solution.py:744
  50.4 5.3 %collective-permute-start = (bf16[8,128,768]{2,1,0:T(8,128)(2,1)}, bf16[8,128,768]{2,1,0:T(8,128)(2,1)}, u32[]{:S(2)}, u32[]{:S(2)}) collective-permute-start(bf16[8,128,768]{2,1,0:T(8,128)(2,1)} %copy-done.9), channel_id=1, source_target_pairs={{0,8},{8,0},{1,9},{9,1},{2,10},{10,2},{3,11},{11,3},{4,12},{12,4},... | collective-permute-start | bytes 4718600 | tf_op jit(solution)/shard_map/ppermute | solution.py:645
  81.6 94.6 %copy-start.28 = (f32[2,128]{1,0:T(2,128)}, f32[2,128]{1,0:T(2,128)S(1)}, u32[]{:S(2)}) copy-start(f32[2,128]{1,0:T(2,128)S(1)} %get-tuple-element.127) | copy-start | bytes 3076
  85.2 32.0 %copy-start.2 = (bf16[32,32,768]{2,1,0:T(8,128)(2,1)}, bf16[32,32,768]{2,1,0:T(8,128)(2,1)S(1)}, u32[]{:S(2)}) copy-start(bf16[32,32,768]{2,1,0:T(8,128)(2,1)S(1)} %all-to-all-done.2) | copy-start | bytes 4718596
  137.8 30.2 %all-to-all-start.3 = ((bf16[32,32,896]{2,1,0:T(8,128)(2,1)}), bf16[32,32,896]{2,1,0:T(8,128)(2,1)}, u32[]{:S(2)}, u32[]{:S(2)}) async-start(bf16[32,32,896]{2,1,0:T(8,128)(2,1)} %bitcast.112), calls=%async_computation.3 | async-start | bytes 3670016 | tf_op jit(solution)/shard_map/all_to_all | solution.py:53
  150.4 23.8 %copy-start.39 = (s32[256]{0:T(256)S(1)}, s32[256]{0:T(256)}, u32[]{:S(2)}) copy-start(s32[256]{0:T(256)} %copy-done.38) | copy-start | bytes 3076
  168.0 32.5 %all-to-all-start.4 = ((bf16[32,32,768]{2,1,0:T(8,128)(2,1)}), bf16[32,32,768]{2,1,0:T(8,128)(2,1)S(1)}, u32[]{:S(2)}, u32[]{:S(2)}) async-start(bf16[32,32,768]{2,1,0:T(8,128)(2,1)} %bitcast.116), calls=%async_computation.4 | async-start | bytes 3145728 | tf_op jit(solution)/shard_map/all_to_all | solution.py:53
  173.8 103.1 %reduce-scatter.5.cloned.1.call-start = ((), (), s32[]{:S(2)}) async-start(), calls=%async_computation.10 | async-start | bytes 5898240 | tf_op jit(solution)/shard_map/reduce_scatter | solution.py:744
  212.4 5.3 %collective-permute-start.1 = (bf16[3584,384]{1,0:T(8,128)(2,1)}, bf16[3584,384]{1,0:T(8,128)(2,1)S(1)}, u32[]{:S(2)}, u32[]{:S(2)}) collective-permute-start(bf16[3584,384]{1,0:T(8,128)(2,1)} %get-tuple-element.63), channel_id=1, source_target_pairs={{0,8},{8,0},{1,9},{9,1},{2,10},{10,2},{3,11},{11,3},{4,12},{12,4},... | collective-permute-start | bytes 8257544 | tf_op jit(solution)/shard_map/ppermute | solution.py:63
  221.9 52.7 %all-to-all-start.5 = ((bf16[64,56,384]{2,1,0:T(8,128)(2,1)}), bf16[64,56,384]{2,1,0:T(8,128)(2,1)}, u32[]{:S(2)}, u32[]{:S(2)}) async-start(bf16[64,56,384]{2,1,0:T(8,128)(2,1)} %bitcast.103), calls=%async_computation.5 | async-start | bytes 5505024 | tf_op jit(solution)/shard_map/all_to_all | solution.py:53
  240.9 10.1 %collective-permute-start.2 = (bf16[1024,768]{1,0:T(8,128)(2,1)}, bf16[1024,768]{1,0:T(8,128)(2,1)S(1)}, u32[]{:S(2)}, u32[]{:S(2)}) collective-permute-start(bf16[1024,768]{1,0:T(8,128)(2,1)} %normed_grads.3), channel_id=1, source_target_pairs={{0,8},{8,0},{1,9},{9,1},{2,10},{10,2},{3,11},{11,3},{4,12},{12,4},... | collective-permute-start | bytes 4718600 | tf_op jit(solution)/shard_map/ppermute | solution.py:799
  278.7 57.4 %all-to-all-start.6 = ((bf16[64,56,384]{2,1,0:T(8,128)(2,1)}), bf16[64,56,384]{2,1,0:T(8,128)(2,1)}, u32[]{:S(2)}, u32[]{:S(2)}) async-start(bf16[64,56,384]{2,1,0:T(8,128)(2,1)} %broadcast_in_dim.154), calls=%async_computation.8 | async-start | bytes 5505024 | tf_op jit(solution)/shard_map/all_to_all | solution.py:53
  285.3 39.0 %collective-permute-start.5 = (bf16[2,128,768]{2,1,0:T(8,128)(2,1)}, bf16[2,128,768]{2,1,0:T(8,128)(2,1)}, u32[]{:S(2)}, u32[]{:S(2)}) collective-permute-start(bf16[2,128,768]{2,1,0:T(8,128)(2,1)} %get-tuple-element.133), channel_id=1, source_target_pairs={{0,48},{16,0},{32,16},{48,32},{1,49},{17,1},{33,17},{49,33},{2,50}... | collective-permute-start | bytes 1179656 | tf_op jit(solution)/shard_map/ppermute | solution.py:810
  287.5 41.1 %collective-permute-start.4 = (bf16[2,128,768]{2,1,0:T(8,128)(2,1)}, bf16[2,128,768]{2,1,0:T(8,128)(2,1)}, u32[]{:S(2)}, u32[]{:S(2)}) collective-permute-start(bf16[2,128,768]{2,1,0:T(8,128)(2,1)} %get-tuple-element.134), channel_id=1, source_target_pairs={{0,32},{16,48},{32,0},{48,16},{1,33},{17,49},{33,1},{49,17},{2,34}... | collective-permute-start | bytes 1179656 | tf_op jit(solution)/shard_map/ppermute | solution.py:810
  288.0 46.6 %collective-permute-start.3 = (bf16[2,128,768]{2,1,0:T(8,128)(2,1)}, bf16[2,128,768]{2,1,0:T(8,128)(2,1)}, u32[]{:S(2)}, u32[]{:S(2)}) collective-permute-start(bf16[2,128,768]{2,1,0:T(8,128)(2,1)} %get-tuple-element.132), channel_id=1, source_target_pairs={{0,16},{16,32},{32,48},{48,0},{1,17},{17,33},{33,49},{49,1},{2,18}... | collective-permute-start | bytes 1179656 | tf_op jit(solution)/shard_map/ppermute | solution.py:810
  336.1 11.5 %collective-permute-start.7 = (bf16[3584,384]{1,0:T(8,128)(2,1)}, bf16[3584,384]{1,0:T(8,128)(2,1)}, u32[]{:S(2)}, u32[]{:S(2)}) collective-permute-start(bf16[3584,384]{1,0:T(8,128)(2,1)} %bitcast.34.mine_ref), channel_id=1, source_target_pairs={{0,8},{8,0},{1,9},{9,1},{2,10},{10,2},{3,11},{11,3},{4,12},{12,4},... | collective-permute-start | bytes 8257544 | tf_op jit(solution)/shard_map/ppermute | solution.py:822
  336.6 8.0 %collective-permute-start.6 = (bf16[128,768]{1,0:T(8,128)(2,1)S(1)}, bf16[128,768]{1,0:T(8,128)(2,1)S(1)}, u32[]{:S(2)}, u32[]{:S(2)}) collective-permute-start(bf16[128,768]{1,0:T(8,128)(2,1)S(1)} %fusion.33), channel_id=1, source_target_pairs={{0,64},{64,0},{1,65},{65,1},{2,66},{66,2},{3,67},{67,3},{4,68},{68... | collective-permute-start | bytes 589832 | tf_op jit(solution)/shard_map/ppermute | solution.py:823
  (44 other events, 300.2 us)
Sparse Core Ops, SparseCore 0:
  11.9 95.1 all-gather.2
  137.9 49.5 reduce-scatter.2
  189.9 56.7 reduce-scatter.4

commit v2 on v1

--- a/solution.py
+++ b/solution.py
@@ -94,7 +94,7 @@
     return jnp.where(lanes == 0, array[:rows], array[rows:]).astype(BF)
 
 
-def attend_kernel(q_ref, kv_ref, window_ref, out_ref, prob_ref):
+def attend_kernel(q_ref, kv_ref, window_ref, out_ref, exps_ref, total_ref):
     half, seq = q_ref.shape[0] // 2, kv_ref.shape[1]
     window = seq + 2 * half
     q = split_heads(q_ref[...], (LANES // 2) ** -0.5)
@@ -106,9 +106,11 @@
     ]
     scores = raw + jnp.concatenate(tiles, axis=0)
     exps = jnp.exp(scores - jnp.max(scores, axis=1, keepdims=True))
-    prob = (exps * (1.0 / jnp.sum(exps, axis=1, keepdims=True))).astype(BF)
-    prob_ref[...] = prob.reshape(prob_ref.shape)
-    out_ref[...] = join_heads(jnp.dot(prob, kv_ref[1], preferred_element_type=F32))
+    inverse = 1.0 / jnp.sum(exps, axis=1, keepdims=True)
+    exps = exps.astype(BF)
+    exps_ref[...] = exps.reshape(exps_ref.shape)
+    total_ref[...] = jnp.broadcast_to(inverse, total_ref.shape)
+    out_ref[...] = join_heads(jnp.dot(exps, kv_ref[1], preferred_element_type=F32) * inverse)
 
 
 def attend(queries, key_value, windows):
@@ -126,10 +128,12 @@
         out_specs=[
             pl.BlockSpec((rows, LANES), lambda h: (0, h)),
             pl.BlockSpec((2, rows, seq), lambda h: (h, 0, 0)),
+            pl.BlockSpec((None, 2 * rows, LANES), lambda h: (h, 0, 0)),
         ],
         out_shape=[
             jax.ShapeDtypeStruct((rows, width), BF),
             jax.ShapeDtypeStruct((2 * pairs, rows, seq), BF),
+            jax.ShapeDtypeStruct((pairs, 2 * rows, LANES), F32),
         ],
         compiler_params=pltpu.CompilerParams(vmem_limit_bytes=VMEM_LIMIT),
         cost_estimate=pl.CostEstimate(
@@ -141,27 +145,33 @@
     )(queries, key_value, windows)
 
 
-def attend_back_kernel(prob_ref, q_ref, kv_ref, grad_ref, dq_ref, dkv_ref, diag_ref):
+def attend_back_kernel(
+    exps_ref, inverse_ref, q_ref, kv_ref, grad_ref, dq_ref, dkv_ref, diag_ref
+):
     half, seq = q_ref.shape[0] // 2, kv_ref.shape[1]
     factor = (LANES // 2) ** -0.5
     rows = 4 * half
     q = split_heads(q_ref[...], factor)
-    grad = split_heads(grad_ref[...], 1.0)
-    prob = prob_ref[...].reshape(rows, seq)
-    wide = prob.astype(F32)
+    inverse = inverse_ref[:, :1]
+    grad = (split_heads(grad_ref[...], 1.0).astype(F32) * inverse).astype(BF)
+    exps = exps_ref[...].reshape(rows, seq)
+    wide = exps.astype(F32)
     prob_grad = contract_cols(grad, kv_ref[1])
     inner = jnp.sum(wide * prob_grad, axis=1, keepdims=True)
-    score_grad = wide * (prob_grad - inner)
+    score_grad = wide * (prob_grad - inner * inverse)
     tiles = jnp.concatenate([score_grad, jnp.zeros((rows, 2 * half), F32)], axis=1)
-    diag_ref[...] = shear(tiles.reshape(4, half, seq + 2 * half))
+    sums = shear(tiles.reshape(4, half, seq + 2 * half))
+    for part in range(2):
+        for head in range(2):
+            diag_ref[part, head : head + 1] = sums[2 * head + part : 2 * head + part + 1]
     score_grad = score_grad.astype(BF)
     query_grad = jnp.dot(score_grad, kv_ref[0], preferred_element_type=F32) * factor
     dq_ref[...] = join_heads(query_grad)
     dkv_ref[0] = contract_rows(q, score_grad).T.astype(BF)
-    dkv_ref[1] = contract_rows(grad, prob).T.astype(BF)
-
-
-def attend_back(prob, queries, key_value, attended_grad):
+    dkv_ref[1] = contract_rows(grad, exps).T.astype(BF)
+
+
+def attend_back(exps, inverse, queries, key_value, attended_grad):
     rows, width = queries.shape
     pairs, seq = key_value.shape[1:3]
     window = seq + rows
@@ -172,6 +182,7 @@
         grid=(pairs,),
         in_specs=[
             pl.BlockSpec((2, rows, seq), lambda h: (h, 0, 0)),
+            pl.BlockSpec((None, 2 * rows, LANES), lambda h: (h, 0, 0)),
             row_spec,
             kv_spec,
             row_spec,
@@ -179,12 +190,12 @@
         out_specs=[
             row_spec,
             kv_spec,
-            pl.BlockSpec((None, 4, window), lambda h: (h, 0, 0)),
+            pl.BlockSpec((2, None, 2, window), lambda h: (0, h, 0, 0)),
         ],
         out_shape=[
             jax.ShapeDtypeStruct((rows, width), BF),
             jax.ShapeDtypeStruct(key_value.shape, BF),
-            jax.ShapeDtypeStruct((pairs, 4, window), F32),
+            jax.ShapeDtypeStruct((2, pairs, 2, window), F32),
         ],
         compiler_params=pltpu.CompilerParams(vmem_limit_bytes=VMEM_LIMIT),
         cost_estimate=pl.CostEstimate(
@@ -193,7 +204,7 @@
             transcendentals=0,
         ),
         name="attend_back",
-    )(prob, queries, key_value, attended_grad)
+    )(exps, inverse, queries, key_value, attended_grad)
 
 
 def key_value_kernel(place_ref, near_ref, far_ref, gain_ref, wk_ref, wv_ref, normed_ref, kv_ref, *, half):
@@ -246,15 +257,13 @@
     )(place, near, far, gain[None], w_qkv, w_qkv)
 
 
-def normed_grad_kernel(position_ref, dkv_ref, wk_ref, wv_ref, out_ref, *, half):
-    tile = out_ref.shape[0] // half
+def normed_grad_kernel(position_ref, *refs):
+    *block_refs, wk_ref, wv_ref, out_ref = refs
     out = 0.0
     for part, weight_ref in enumerate((wk_ref, wv_ref)):
         rows = []
-        for block in range(tile):
-            source = position_ref[pl.program_id(0) * tile + block]
-            at = pl.ds(pl.multiple_of(source * half, half), half)
-            pairs = [dkv_ref[part, pair, at] for pair in range(dkv_ref.shape[1])]
+        for block_ref in block_refs:
+            pairs = [block_ref[part, pair] for pair in range(block_ref.shape[1])]
             rows.append(jnp.concatenate(pairs, axis=1))
         out += contract_cols(jnp.concatenate(rows, axis=0), weight_ref[...])
     out_ref[...] = out.astype(BF)
@@ -262,19 +271,25 @@
 
 def normed_grads(position, key_value_grad, w_qkv, half):
     width = w_qkv.shape[0]
-    rows = position.shape[0] * half
-    tile = 8 * half
+    pairs = key_value_grad.shape[1]
+    count = position.shape[0]
+    rows = count * half
+    step = 8
+
+    def block_spec(at):
+        return pl.BlockSpec((2, pairs, half, LANES), lambda r, p: (0, 0, p[step * r + at], 0))
+
     return pl.pallas_call(
-        functools.partial(normed_grad_kernel, half=half),
+        normed_grad_kernel,
         grid_spec=pltpu.PrefetchScalarGridSpec(
             num_scalar_prefetch=1,
-            grid=(rows // tile,),
+            grid=(count // step,),
             in_specs=[
-                pl.BlockSpec(key_value_grad.shape, lambda r, p: (0, 0, 0, 0)),
+                *[block_spec(at) for at in range(step)],
                 pl.BlockSpec((width, width), lambda r, p: (0, 1)),
                 pl.BlockSpec((width, width), lambda r, p: (0, 2)),
             ],
-            out_specs=pl.BlockSpec((tile, width), lambda r, p: (r, 0)),
+            out_specs=pl.BlockSpec((step * half, width), lambda r, p: (r, 0)),
         ),
         out_shape=jax.ShapeDtypeStruct((rows, width), BF),
         compiler_params=pltpu.CompilerParams(vmem_limit_bytes=VMEM_LIMIT),
@@ -282,7 +297,7 @@
             flops=4 * rows * width * width, bytes_accessed=8 * rows * width, transcendentals=0
         ),
         name="normed_grads",
-    )(position, key_value_grad, w_qkv, w_qkv)
+    )(position, *([key_value_grad] * step), w_qkv, w_qkv)
 
 
 def weight_grad_kernel(
@@ -293,7 +308,9 @@
     all_normed_ref,
     attended_ref,
     branch_ref,
-    extra_ref,
+    small_ref,
+    hot_ref,
+    diag_ref,
     kept_ref,
     given_ref,
 ):
@@ -329,15 +346,39 @@
 
     @pl.when(step == 4)
     def _():
-        give(extra_ref[...])
+        window = diag_ref.shape[3]
+        bias_grad = 0.0
+        for part in range(2):
+            sums = jnp.concatenate([diag_ref[part, pair] for pair in range(diag_ref.shape[1])], axis=0)
+            bias_grad += lax.dot_general(
+                hot_ref[:, part * window : (part + 1) * window],
+                sums,
+                COLS,
+                precision=HIGHEST,
+                preferred_element_type=F32,
+            )
+        buckets, heads = bias_grad.shape
+        spare = jnp.zeros((buckets, small_ref.shape[1] - heads), F32)
+        bias_rows = jnp.concatenate([bias_grad, spare], axis=1)
+        give(jnp.concatenate([small_ref[...], bias_rows], axis=0))
 
 
 def weight_grads(
-    core, query_grad, normed_one, key_value_grad, all_normed, attended, branch_grad, extra
+    core,
+    query_grad,
+    normed_one,
+    key_value_grad,
+    all_normed,
+    attended,
+    branch_grad,
+    small,
+    bucket_hot,
+    diagonals,
+    spare,
 ):
     rows, width = normed_one.shape
     seq = all_normed.shape[0]
-    total = 4 * width + extra.shape[0]
+    total = 4 * width + small.shape[0] + bucket_hot.shape[0] + spare
     row_spec = pl.BlockSpec((rows, width), lambda t, p: (0, 0))
     out_spec = pl.BlockSpec((width, width // 2), lambda t, p: (t, 0))
     out_shape = jax.ShapeDtypeStruct((total, width // 2), BF)
@@ -355,7 +396,9 @@
                 pl.BlockSpec((seq, width), lambda t, p: (0, 0)),
                 row_spec,
                 row_spec,
-                pl.BlockSpec(extra.shape, lambda t, p: (0, 0)),
+                pl.BlockSpec(small.shape, lambda t, p: (0, 0)),
+                pl.BlockSpec(bucket_hot.shape, lambda t, p: (0, 0)),
+                pl.BlockSpec(diagonals.shape, lambda t, p: (0, 0, 0, 0)),
             ],
             out_specs=[out_spec, out_spec],
         ),
@@ -365,23 +408,32 @@
             flops=4 * seq * width * width, bytes_accessed=10 * seq * width, transcendentals=0
         ),
         name="weight_grads",
-    )(core, query_grad, normed_one, key_value_grad, all_normed, attended, branch_grad, extra)
-
-
-def whole_grad_kernel(core_ref, mine_ref, other_ref, weight_ref, grad_ref, product_ref, out_ref):
+    )(
+        core,
+        query_grad,
+        normed_one,
+        key_value_grad,
+        all_normed,
+        attended,
+        branch_grad,
+        small,
+        bucket_hot,
+        diagonals,
+    )
+
+
+def whole_grad_kernel(side_ref, half_ref, weight_ref, *refs):
+    grad_ref, product_ref, out_ref = refs[-3:]
     step = pl.program_id(0)
-    last = pl.num_programs(0) - out_ref.shape[0] // mine_ref.shape[0]
-    side, tile = mine_ref.shape[1], mine_ref.shape[0]
-    width = 2 * side
-    mine_at = pl.ds(pl.multiple_of(core_ref[0] * side, side), side)
-    other_at = pl.ds(pl.multiple_of(side - core_ref[0] * side, side), side)
+    last = pl.num_programs(0) - 1
+    half = half_ref[...].astype(F32)
 
     @pl.when(step < last)
     def _():
-        grad_ref[mine_at, :] = mine_ref[...].astype(F32).T
-        grad_ref[other_at, :] = other_ref[...].astype(F32).T
-        product = jnp.sum(grad_ref[...] * weight_ref[...].astype(F32), axis=1, keepdims=True)
-        product = jnp.broadcast_to(product, (width, LANES))
+        grad = half.T
+        grad_ref[...] = grad
+        product = jnp.sum(grad * weight_ref[...].astype(F32), axis=1, keepdims=True)
+        product = jnp.broadcast_to(product, product_ref.shape)
 
         @pl.when(step == 0)
         def _():
@@ -391,38 +443,33 @@
         def _():
             product_ref[...] += product
 
-    @pl.when(step >= last)
+    @pl.when(step == last)
     def _():
-        at = pl.ds(pl.multiple_of((step - last) * tile, tile), tile)
-
-        @pl.when(core_ref[0] == 0)
-        def _():
-            out_ref[at, :side] = mine_ref[...].astype(F32)
-            out_ref[at, side:] = other_ref[...].astype(F32)
-
-        @pl.when(core_ref[0] != 0)
-        def _():
-            out_ref[at, :side] = other_ref[...].astype(F32)
-            out_ref[at, side:] = mine_ref[...].astype(F32)
-
-
-def whole_grad(core, mine, other, weight):
+        out_ref[...] = half
+
+
+def whole_grad(side, half_sums, weight, held):
     width, columns = weight.shape
-    side = mine.shape[1]
-    tile = width
-    count = columns // tile
-    half_spec = pl.BlockSpec((tile, side), lambda t, p: (t, 0))
-    whole_spec = pl.BlockSpec((width, tile), lambda t, p: (0, jnp.minimum(t, count - 1)))
+    half = half_sums.shape[1]
+    steps = columns // width + 1
+
+    def tile_map(t, p):
+        return (p[0], jnp.minimum(t, steps - 2))
+
     return pl.pallas_call(
         whole_grad_kernel,
         grid_spec=pltpu.PrefetchScalarGridSpec(
             num_scalar_prefetch=1,
-            grid=(count + width // tile,),
-            in_specs=[half_spec, half_spec, whole_spec],
+            grid=(steps,),
+            in_specs=[
+                pl.BlockSpec((width, half), lambda t, p: (t, 0)),
+                pl.BlockSpec((half, width), tile_map),
+                *[pl.BlockSpec(memory_space=pl.ANY) for _ in held],
+            ],
             out_specs=[
-                whole_spec,
-                pl.BlockSpec((width, LANES), lambda t, p: (0, 0)),
-                pl.BlockSpec((width, width), lambda t, p: (0, 0)),
+                pl.BlockSpec((half, width), tile_map),
+                pl.BlockSpec((half, LANES), lambda t, p: (p[0], 0)),
+                pl.BlockSpec((width, half), lambda t, p: (0, p[0])),
             ],
         ),
         out_shape=[
@@ -430,12 +477,13 @@
             jax.ShapeDtypeStruct((width, LANES), F32),
             jax.ShapeDtypeStruct((width, width), F32),
         ],
+        input_output_aliases={3 + at: at for at in range(len(held))},
         compiler_params=pltpu.CompilerParams(vmem_limit_bytes=VMEM_LIMIT),
         cost_estimate=pl.CostEstimate(
-            flops=2 * width * columns, bytes_accessed=8 * width * columns, transcendentals=0
+            flops=width * columns, bytes_accessed=4 * width * columns, transcendentals=0
         ),
         name="whole_grad",
-    )(core, mine, other, weight)
+    )(side, half_sums, weight, *held)
 
 
 def expert_rows(x_ref, cot_ref):
@@ -444,7 +492,7 @@
     rows_in = x_ref[...].reshape(rows, x_ref.shape[2])
     gate = jnp.sum(rows_in[:, width:].astype(F32), axis=1, keepdims=True)
     slot_grad = (cot_ref[...].reshape(rows, width).astype(F32) * gate).astype(BF)
-    return rows_in[:, :width], slot_grad
+    return rows_in[:, :width], slot_grad, gate
 
 
 def high_and_low(column):
@@ -455,17 +503,62 @@
 
 
 def write_weight_grads(x, slot_grad, activated, pre_grad, grad_ref):
-    grad_in = contract_rows(pre_grad, x).astype(BF)
+    grad_in = contract_rows(x, pre_grad).astype(BF)
     grad_out = contract_rows(activated, slot_grad).astype(BF)
     slices, hidden = grad_ref.shape[0], grad_ref.shape[1] // 2
     for index in range(slices):
-        grad_ref[index, :hidden] = grad_in[index * hidden : (index + 1) * hidden]
+        columns = grad_in[:, index * hidden : (index + 1) * hidden]
+        grad_ref[index, :hidden, :hidden] = columns[:hidden]
+        grad_ref[index, :hidden, hidden:] = columns[hidden:]
         grad_ref[index, hidden:] = grad_out[index * hidden : (index + 1) * hidden]
+
+
+def slice_weights(weight_ref):
+    slices, hidden = weight_ref.shape[0], weight_ref.shape[1] // 2
+    weights = [weight_ref[index] for index in range(slices)]
+    tops = [weight[:hidden] for weight in weights]
+    tops = [jnp.concatenate([top[:, :hidden], top[:, hidden:]], axis=0) for top in tops]
+    weight_out = jnp.concatenate([weight[hidden:] for weight in weights], axis=0)
+    return jnp.concatenate(tops, axis=1), weight_out
+
+
+def cotangent_kernel(cot_ref, weight_ref, units_ref):
+    rows = cot_ref.shape[0] * cot_ref.shape[1]
+    cot = cot_ref[...].reshape(rows, cot_ref.shape[2])
+    slices, hidden = weight_ref.shape[0], weight_ref.shape[1]
+    weight_out = weight_ref[...].reshape(slices * hidden, weight_ref.shape[2])
+    units_ref[...] = contract_cols(cot, weight_out).astype(BF)
+
+
+def cotangent_units(cot_rows, weights):
+    devices, experts, slots, width = cot_rows.shape
+    parts, _, both, _ = weights.shape
+    hidden = both // 2
+    rows = devices * slots
+    slices = 2
+    return pl.pallas_call(
+        cotangent_kernel,
+        grid=(experts, parts // slices),
+        in_specs=[
+            pl.BlockSpec((devices, None, slots, width), lambda e, w: (0, e, 0, 0)),
+            pl.BlockSpec((slices, None, hidden, width), lambda e, w: (w, e, 1, 0)),
+        ],
+        out_specs=pl.BlockSpec((None, rows, slices * hidden), lambda e, w: (e, 0, w)),
+        out_shape=jax.ShapeDtypeStruct((experts, rows, parts * hidden), BF),
+        compiler_params=pltpu.CompilerParams(vmem_limit_bytes=VMEM_LIMIT),
+        cost_estimate=pl.CostEstimate(
+            flops=2 * experts * rows * width * parts * hidden,
+            bytes_accessed=4 * experts * rows * width + 2 * parts * experts * width * hidden,
+            transcendentals=0,
+        ),
+        name="cotangent_units",
+    )(cot_rows, weights)
 
 
 def expert_kernel(
     x_ref,
     cot_ref,
+    units_ref,
     weight_ref,
     dx_ref,
     ret_ref,
@@ -477,19 +570,16 @@
 ):
     part = pl.program_id(1)
     width = cot_ref.shape[-1]
-    x, slot_grad = expert_rows(x_ref, cot_ref)
-    slices, hidden = weight_ref.shape[0], weight_ref.shape[1] // 2
-    weights = [weight_ref[index] for index in range(slices)]
-    weight_in = jnp.concatenate([weight[:hidden] for weight in weights], axis=0)
-    weight_out = jnp.concatenate([weight[hidden:] for weight in weights], axis=0)
-    pre = contract_cols(x, weight_in)
-    act_grad = contract_cols(slot_grad, weight_out)
+    x, slot_grad, gate = expert_rows(x_ref, cot_ref)
+    weight_in, weight_out = slice_weights(weight_ref)
+    pre = jnp.dot(x, weight_in, preferred_element_type=F32)
+    act_grad = units_ref[...].astype(F32) * gate
     cumulative = 0.5 * (1.0 + lax.erf(pre * 0.7071067811865476))
     activated = (pre * cumulative).astype(BF)
     slope = cumulative + pre * (jnp.exp(-0.5 * pre * pre) * 0.3989422804014327)
     pre_grad = (act_grad * slope).astype(BF)
     returned = jnp.dot(activated, weight_out, preferred_element_type=F32)
-    input_grad = jnp.dot(pre_grad, weight_in, preferred_element_type=F32)
+    input_grad = contract_cols(pre_grad, weight_in)
 
     @pl.when(pl.program_id(0) == 0)
     def _():
@@ -523,11 +613,11 @@
 
 
 def expert_grad_kernel(x_ref, cot_ref, act_ref, pre_grad_ref, grad_ref):
-    x, slot_grad = expert_rows(x_ref, cot_ref)
+    x, slot_grad, _ = expert_rows(x_ref, cot_ref)
     write_weight_grads(x, slot_grad, act_ref[...], pre_grad_ref[...], grad_ref)
 
 
-def run_experts(x_rows, cot_rows, weights):
+def run_experts(x_rows, cot_rows, units, weights):
     devices, experts, slots, width = cot_rows.shape
     wide = x_rows.shape[3]
     parts, _, both, _ = weights.shape
@@ -554,6 +644,7 @@
         in_specs=[
             row_spec(wide),
             row_spec(width),
+            pl.BlockSpec((None, rows, slices * hidden), lambda e, w: (e, 0, w)),
             pl.BlockSpec((slices, None, both, width), lambda e, w: (w, e, 0, 0)),
         ],
         out_specs=[
@@ -580,7 +671,7 @@
             transcendentals=2 * experts * rows * parts * hidden,
         ),
         name="experts",
-    )(x_rows, cot_rows, weights)
+    )(x_rows, cot_rows, units, weights)
     weight_grads_of = [first_grad]
     for expert in range(1, experts):
 
@@ -607,6 +698,125 @@
             )(x_rows, cot_rows, activated, pre_grad)
         )
     return input_grad, returned, weight_grads_of
+
+
+def into_experts_kernel(
+    attended_ref,
+    tokens_ref,
+    w_out_ref,
+    gain_ref,
+    w_router_ref,
+    chosen_ref,
+    table_ref,
+    residual_ref,
+    normed_ref,
+    gate_ref,
+    slots_ref,
+):
+    inputs = tokens_ref[...].astype(F32)
+    residual = inputs + jnp.dot(attended_ref[...], w_out_ref[...], preferred_element_type=F32)
+    residual_ref[...] = residual
+    normed = (residual * norm_scale(residual) * gain_ref[...]).astype(BF)
+    normed_ref[...] = normed
+    logits = jnp.dot(normed, w_router_ref[...], preferred_element_type=F32)
+    hots = picked_hots(chosen_ref, logits.shape)
+    first, second = [jnp.sum(hot * logits, axis=1, keepdims=True) for hot in hots]
+    peak = jnp.maximum(first, second)
+    first, second = jnp.exp(first - peak), jnp.exp(second - peak)
+    gates = [first / (first + second), second / (first + second)]
+    lanes = lax.broadcasted_iota(jnp.int32, gate_ref.shape, 1)
+    gate_ref[...] = jnp.where(lanes == 0, gates[0], jnp.where(lanes == 1, gates[1], 0.0))
+    picks = [jnp.concatenate([normed, high_and_low(gate)], axis=1) for gate in gates]
+    slots_ref[...] = contract_rows(table_ref[...], jnp.concatenate(picks, axis=0)).astype(BF)
+
+
+def picked_hots(chosen_ref, shape):
+    ids = lax.broadcasted_iota(jnp.int32, shape, 1)
+    return [jnp.where(chosen_ref[:, pick : pick + 1] == ids, 1.0, 0.0) for pick in range(2)]
+
+
+def into_experts(attended, tokens, w_attn_out, gain, w_router, chosen, table):
+    rows, width = attended.shape
+    return pl.pallas_call(
+        into_experts_kernel,
+        out_shape=[
+            jax.ShapeDtypeStruct((rows, width), F32),
+            jax.ShapeDtypeStruct((rows, width), BF),
+            jax.ShapeDtypeStruct((rows, LANES), F32),
+            jax.ShapeDtypeStruct((table.shape[1], width + LANES), BF),
+        ],
+        compiler_params=pltpu.CompilerParams(vmem_limit_bytes=VMEM_LIMIT),
+        name="into_experts",
+    )(attended, tokens, w_attn_out, gain[None], w_router, chosen, table)
+
+
+def out_of_experts_kernel(
+    grads_ref,
+    table_ref,
+    gate_ref,
+    chosen_ref,
+    normed_ref,
+    residual_ref,
+    cot_ref,
+    gain_ref,
+    w_router_ref,
+    w_out_ref,
+    mixed_ref,
+    branch_ref,
+    attended_grad_ref,
+    small_ref,
+):
+    rows, width = residual_ref.shape
+    table = table_ref[...]
+    grads = jnp.dot(table, grads_ref[...], preferred_element_type=F32)
+    gate_grads = jnp.sum(grads[:, width:], axis=1, keepdims=True)
+    gate_grads = [gate_grads[:rows], gate_grads[rows:]]
+    gates = [gate_ref[:, :1], gate_ref[:, 1:2]]
+    inner = gates[0] * gate_grads[0] + gates[1] * gate_grads[1]
+    hots = picked_hots(chosen_ref, (rows, w_router_ref.shape[1]))
+    logit_grad = sum(
+        hot * (gate * (gate_grad - inner)) for hot, gate, gate_grad in zip(hots, gates, gate_grads)
+    )
+    normed = normed_ref[...].astype(F32)
+    w_router = w_router_ref[...].astype(F32)
+    w_router_grad = lax.dot_general(
+        logit_grad, normed, ROWS, precision=HIGHEST, preferred_element_type=F32
+    )
+    router_back = lax.dot_general(
+        logit_grad, w_router, COLS, precision=HIGHEST, preferred_element_type=F32
+    )
+    normed_grad = grads[:rows, :width] + grads[rows:, :width] + router_back
+    residual = residual_ref[...]
+    norm_part, gain_grad = norm_backward(
+        residual, norm_scale(residual), gain_ref[...], normed_grad
+    )
+    mixed = cot_ref[...].astype(F32) + norm_part
+    mixed_ref[...] = mixed
+    branch = mixed.astype(BF)
+    branch_ref[...] = branch
+    attended_grad_ref[...] = contract_cols(branch, w_out_ref[...]).astype(BF)
+    experts = w_router_grad.shape[0]
+    small_ref[:experts] = w_router_grad
+    tail = small_ref.shape[0] - experts
+    first = lax.broadcasted_iota(jnp.int32, (tail, width), 0) == 0
+    small_ref[experts:] = jnp.where(first, gain_grad[None], 0.0)
+
+
+def out_of_experts(
+    grads, table, gates, chosen, normed, residual, cotangent, gain, w_router, w_attn_out
+):
+    rows, width = residual.shape
+    return pl.pallas_call(
+        out_of_experts_kernel,
+        out_shape=[
+            jax.ShapeDtypeStruct((rows, width), F32),
+            jax.ShapeDtypeStruct((rows, width), BF),
+            jax.ShapeDtypeStruct((rows, width), BF),
+            jax.ShapeDtypeStruct((w_router.shape[1] + 8, width), F32),
+        ],
+        compiler_params=pltpu.CompilerParams(vmem_limit_bytes=VMEM_LIMIT),
+        name="out_of_experts",
+    )(grads, table, gates, chosen, normed, residual, cotangent, gain[None], w_router, w_attn_out)
 
 
 def on_device(
@@ -645,7 +855,9 @@
     far_tokens = lax.ppermute(near_tokens, "core", SWAP)
     near_tokens = near_tokens.reshape(seq // 2, model_width)
     far_tokens = far_tokens.reshape(seq // 2, model_width)
-    weights = jnp.concatenate([w_in.transpose(0, 2, 1), w_out], axis=1)
+    hidden = w_in.shape[2]
+    weights = jnp.concatenate([w_in[:, :hidden], w_in[:, hidden:]], axis=2)
+    weights = jnp.concatenate([weights, w_out], axis=1)
     weights = lax.all_gather(weights, "x", axis=0)
 
     chosen = routes[0].T
@@ -665,12 +877,11 @@
     slot_table = slot_hot.astype(BF)
     token_table = slot_table[:tok_rows] + slot_table[tok_rows:]
 
-    def to_experts(table, rows):
-        slots = contract_rows(table, rows).astype(BF)
-        arrived = exchange(slots.reshape(expert_devices, device_slots, rows.shape[1]), EXPERT_AXES)
-        return arrived.reshape(expert_devices, local_experts, capacity, rows.shape[1])
-
-    cot_rows = to_experts(token_table, cotangent[0])
+    def to_slots(slots):
+        arrived = exchange(slots.reshape(expert_devices, device_slots, -1), EXPERT_AXES)
+        return arrived.reshape(expert_devices, local_experts, capacity, -1)
+
+    cot_rows = to_slots(contract_rows(token_table, cotangent[0]).astype(BF))
 
     ctx_ids = jnp.arange(ctx_count, dtype=jnp.int32)
     my_core = lax.axis_index("core")
@@ -714,23 +925,14 @@
     all_normed, key_value = keys_and_values(
         place, near_tokens, far_tokens, gain_attn, w_qkv, half
     )
-    attended, probabilities = attend(queries, key_value, windows)
-    residual_one = inputs + jnp.dot(attended, w_attn_out, preferred_element_type=F32)
-    scale_two = norm_scale(residual_one)
-    normed_two = (residual_one * scale_two * gain_ffn).astype(BF)
-
-    router_logits = jnp.dot(normed_two, w_router, preferred_element_type=F32)
-    chosen_hot = (chosen[:, :, None] == expert_ids[None, None, :]).astype(F32)
-    picked_logits = jnp.sum(chosen_hot * router_logits[None], axis=2)
-    logit_peak = jnp.max(picked_logits, axis=0, keepdims=True)
-    gate_exp = jnp.exp(picked_logits - logit_peak)
-    gate_weights = (gate_exp / jnp.sum(gate_exp, axis=0, keepdims=True))[:, :, None]
-
-    flat_gate = gate_weights.reshape(2 * tok_rows, 1)
-    gate_lanes = high_and_low(flat_gate)
-    pick_rows = jnp.concatenate([normed_two, normed_two], axis=0)
-    x_rows = to_experts(slot_table, jnp.concatenate([pick_rows, gate_lanes], axis=1))
-    input_grad, returned, parts = run_experts(x_rows, cot_rows, weights)
+    attended, exps, inverse = attend(queries, key_value, windows)
+
+    residual_one, normed_two, gates, slots = into_experts(
+        attended, tokens[0], w_attn_out, gain_ffn, w_router, routes[0], slot_table
+    )
+    x_rows = to_slots(slots)
+    units = cotangent_units(cot_rows, weights)
+    input_grad, returned, parts = run_experts(x_rows, cot_rows, units, weights)
 
     def from_experts(rows):
         rows = exchange(rows.reshape(expert_devices, device_slots, rows.shape[3]), EXPERT_AXES)
@@ -743,39 +945,29 @@
     shares = [
         lax.psum_scatter(part, "x", scatter_dimension=0) for part in (parts[0], *later_parts)
     ]
-    expert_part = jnp.dot(
-        token_table, input_grad[:, :model_width], preferred_element_type=F32
-    )
-    gate_grad = jnp.dot(slot_table, input_grad[:, model_width:], preferred_element_type=F32)
-    gate_grad = jnp.sum(gate_grad.reshape(2, tok_rows, LANES), axis=2, keepdims=True)
     returned = from_experts(returned)
 
-    upstream = cotangent[0].astype(F32)
-    inner_mean = jnp.sum(gate_weights * gate_grad, axis=0, keepdims=True)
-    pick_grad = gate_weights * (gate_grad - inner_mean)
-    logit_grad = jnp.sum(pick_grad * chosen_hot, axis=0)
-    grad_w_router = lax.dot_general(normed_two.astype(F32), logit_grad, ROWS, precision=HIGHEST)
-    router_back = lax.dot_general(logit_grad, w_router.astype(F32), COLS, precision=HIGHEST)
-    normed_two_grad = expert_part + router_back
-    norm_part, grad_gain_ffn = norm_backward(residual_one, scale_two, gain_ffn, normed_two_grad)
-    mixed_grad = upstream + norm_part
-    branch_grad = mixed_grad.astype(BF)
-
-    attended_grad = contract_cols(branch_grad, w_attn_out).astype(BF)
+    mixed_grad, branch_grad, attended_grad, small = out_of_experts(
+        input_grad,
+        slot_table,
+        gates,
+        routes[0],
+        normed_two,
+        residual_one,
+        cotangent[0],
+        gain_ffn,
+        w_router,
+        w_attn_out,
+    )
+
     query_grad, key_value_grad, diagonals = attend_back(
-        probabilities, queries, key_value, attended_grad
+        exps, inverse, queries, key_value, attended_grad
     )
     query_grad, returned = lax.optimization_barrier((query_grad, returned))
-    diagonals = diagonals.reshape(head_count, 2 * window)
-    grad_rel_bias = lax.dot_general(bucket_hot, diagonals, COLS, precision=HIGHEST)
 
     core = jnp.reshape(my_core, (1,)).astype(jnp.int32)
     side = model_width // 2
-    biases = bucket_count * head_count
-    bias_row = jnp.pad(grad_rel_bias.reshape(1, biases), ((0, 0), (0, model_width - biases)))
-    extra = jnp.concatenate([grad_w_router.T, grad_gain_ffn[None], bias_row], axis=0)
-    spare = -(4 * model_width + extra.shape[0]) % (8 * lax.axis_size(CHIPS))
-    extra = jnp.pad(extra, ((0, spare), (0, 0)))
+    spare = -(4 * model_width + small.shape[0] + bucket_count) % (8 * lax.axis_size(CHIPS))
     kept, given = weight_grads(
         core,
         query_grad,
@@ -784,54 +976,50 @@
         all_normed,
         attended,
         branch_grad,
-        extra,
+        small,
+        bucket_hot,
+        diagonals,
+        spare,
     )
     key_value_grad, kept, given, returned = lax.optimization_barrier(
         (key_value_grad, kept, given, returned)
     )
+    share = half_share(kept, given)
     picked = jnp.dot(slot_table, returned, preferred_element_type=F32)
-    mixture = jnp.sum(gate_weights * picked.reshape(2, tok_rows, model_width), axis=0)
+    mixture = gates[:, :1] * picked[:tok_rows] + gates[:, 1:2] * picked[tok_rows:]
     layer_out = (residual_one + mixture).astype(BF)[None]
-    share = half_share(kept, given)
 
     far_grad = normed_grads(positions[blocks // 2 :], key_value_grad, w_qkv, half)
     near_grad = normed_grads(positions[: blocks // 2], key_value_grad, w_qkv, half)
     near_grad = near_grad.astype(F32) + lax.ppermute(far_grad, "core", SWAP).astype(F32)
-    near_grad = near_grad.astype(BF).reshape(2, ctx_count // 4, tok_rows, model_width)
-    share, near_grad, layer_out, shares = lax.optimization_barrier(
-        (share, near_grad, layer_out, shares)
-    )
-    my_ya, my_z = lax.axis_index("ya"), lax.axis_index("z")
-    ring = lax.axis_size("z")
-    along_z = 0.0
-    for hop in range(ring):
-        rows = lax.dynamic_index_in_dim(near_grad, (my_z + hop) % ring, axis=1, keepdims=False)
-        if hop:
-            rows = lax.ppermute(rows, "z", [(at, (at + hop) % ring) for at in range(ring)])
-        along_z = along_z + rows.astype(F32)
-    given = jnp.where(my_ya == 0, along_z[1], along_z[0]).astype(BF)
-    kept = jnp.where(my_ya == 0, along_z[0], along_z[1])
+    near_grad = near_grad.astype(BF).reshape(ctx_count // 2, tok_rows, model_width)
+    query_part = contract_cols(query_grad, w_q)
+    share, near_grad, query_part, layer_out, shares = lax.optimization_barrier(
+        (share, near_grad, query_part, layer_out, shares)
+    )
+
     mine = spread(share, CHIPS).reshape(-1, side)
-    hidden = w_in.shape[2]
-    shares = jnp.stack(shares)
-    grad_w_in = shares[:, :hidden].transpose(0, 2, 1).astype(F32)
-    grad_w_out = shares[:, hidden:].astype(F32)
-    mine, given, grad_w_in, grad_w_out = lax.optimization_barrier(
-        (mine, given, grad_w_in, grad_w_out)
+    shares = jnp.stack(shares).astype(F32)
+    grad_w_in = jnp.concatenate([shares[:, :hidden, :hidden], shares[:, :hidden, hidden:]], axis=1)
+    grad_w_out = shares[:, hidden:]
+    mine, near_grad, grad_w_in, grad_w_out = lax.optimization_barrier(
+        (mine, near_grad, grad_w_in, grad_w_out)
     )
     other = lax.ppermute(mine, "core", SWAP)
-    normed_one_grad = kept + lax.ppermute(given, "ya", SWAP).astype(F32)
-    normed_one_grad = normed_one_grad + contract_cols(query_grad, w_q)
+    row_grads = exchange(near_grad, SAME_CORE)
+    held = whole_grad(core, mine, w_qkv, ())
+    whole = whole_grad(1 - core, other, w_qkv, held)
+    row_grads, sum_w_qkv, products, sum_w_attn_out = lax.optimization_barrier((row_grads, *whole))
+    normed_one_grad = jnp.sum(row_grads.astype(F32), axis=0) + query_part
     input_norm_grad, _ = norm_backward(inputs, scale_one, gain_attn, normed_one_grad)
     grad_tokens = (mixed_grad + input_norm_grad)[None]
-    sum_w_qkv, products, sum_w_attn_out = whole_grad(core, mine, other, w_qkv)
     sum_gain_attn = products[:, 0] / gain_attn
-    small = slice(4 * model_width, 4 * model_width + experts + 2)
-    left = jnp.where(my_core == 0, mine[small], other[small])
-    right = jnp.where(my_core == 0, other[small], mine[small])
+    rows = slice(4 * model_width, 4 * model_width + small.shape[0] + bucket_count)
+    left = jnp.where(my_core == 0, mine[rows], other[rows])
+    right = jnp.where(my_core == 0, other[rows], mine[rows])
     sums = jnp.concatenate([left, right], axis=1).astype(F32)
     sum_w_router, sum_gain_ffn = sums[:experts].T, sums[experts]
-    sum_rel_bias = sums[experts + 1, :biases].reshape(bucket_count, head_count)
+    sum_rel_bias = sums[small.shape[0] :, :head_count]
     return (
         layer_out,
         grad_tokens,

time: 369 us -> 355 us (0.962)
  blocking collectives: 32 us -> 0 us
  Pallas kernels: 101 us -> 117 us
  waiting for transfers between devices: 104 us -> 120 us
  matrix products: 17.8 us -> 7.1 us
  local copies, waits for them, and re-layouts: 21.7 us -> 14.6 us
  starting transfers between devices: 49.9 us -> 56.1 us
    ppermute x4 -> x0, waiting for transfers between devices: 45.1 us -> none  [the longest x3 42.2 us: on_device(): lax.ppermute(rows, 'z', [(at, (at + hop) % ring) for at in range(ring)])]
    all_to_all x6 -> x8, waiting for transfers between devices: 54.1 us -> 99 us  [exchange(): return lax.all_to_all(array, axes, split_axis=0, concat_axis=0, tiled=True)]
    all_to_all x1 -> x0, blocking collectives: 32 us -> none  [exchange(): return lax.all_to_all(array, axes, split_axis=0, concat_axis=0, tiled=True)]
    all_gather x1, waiting for transfers between devices: 0.01 us -> 16.3 us  [on_device(): weights = lax.all_gather(weights, 'x', axis=0)]
    pallas_call x2 -> x5, Pallas kernels: 15.9 us -> 30.5 us  [the longest x2 14.1 us: normed_grads(): pl.pallas_call(normed_grad_kernel, grid_spec=pltpu.PrefetchScalarGridSpec...]
    all_to_all x6 -> x8, starting transfers between devices: 42.5 us -> 51.2 us  [exchange(): return lax.all_to_all(array, axes, split_axis=0, concat_axis=0, tiled=True)]
    dot_general x7 -> x0, matrix products: 6.62 us -> none  [the longest x1 1.99 us: on_device(): jnp.dot(token_table, input_grad[:, :model_width], preferred_element_type=...]
    ppermute x4 -> x0, starting transfers between devices: 5.24 us -> none  [the longest x3 3.3 us: on_device(): lax.ppermute(rows, 'z', [(at, (at + hop) % ring) for at in range(ring)])]
  transfers between devices with their start and end apart: 17 -> 15, of which waited for: 8 -> 9; matrix products, arithmetic and copies ran while one was open for 13% -> 9% of each run, Pallas kernels for 19% -> 28%
where the time goes in v2:
time: 355 us; the launch traced here: 353 us
  waiting for transfers between devices  120 us (34%)
  Pallas kernels  117 us (33%)
  starting transfers between devices  56.1 us (16%)
  other arithmetic  22.8 us (6%)
  between operations  15.4 us (4%)
  local copies, waits for them, and re-layouts  14.6 us (4%)
  matrix products  7.1 us (2%)
    all_to_all x8, waiting for transfers between devices, exchange(): return lax.all_to_all(array, axes, split_axis=0, concat_axis=0, tiled=True)  99 us
    all_to_all x8, starting transfers between devices, exchange(): return lax.all_to_all(array, axes, split_axis=0, concat_axis=0, tiled=True)  51.2 us
    pallas_call x1, Pallas kernels, run_experts(): pl.pallas_call(expert_kernel, grid=(experts, steps), in_specs=[row_spec(w...  18.6 us
    all_gather x1, waiting for transfers between devices, on_device(): weights = lax.all_gather(weights, 'x', axis=0)  16.3 us
    pallas_call x1, Pallas kernels, attend_back(): pl.pallas_call(attend_back_kernel, grid=(pairs,), in_specs=[pl.BlockSpec(...  14.3 us
    pallas_call x2, Pallas kernels, normed_grads(): pl.pallas_call(normed_grad_kernel, grid_spec=pltpu.PrefetchScalarGridSpec...  14.1 us
    pallas_call x1, Pallas kernels, weight_grads(): pl.pallas_call(weight_grad_kernel, grid_spec=pltpu.PrefetchScalarGridSpec...  13.7 us
    pallas_call x2, Pallas kernels, whole_grad(): pl.pallas_call(whole_grad_kernel, grid_spec=pltpu.PrefetchScalarGridSpec(...  11.8 us
  transfers between devices with their start and end apart: 15, of which 9 were waited for; matrix products, arithmetic and copies ran while one was open for 9% of the time, Pallas kernels for 28%

profile of v2, /device:TPU:1, one launch (start us, length us, event | category | flops | bytes accessed | tf_op | source)
XLA Modules:
  0.0 353.3 jit_solution(13344721315379778416)
XLA Ops:
  12.6 8.6 %all-to-all-start = ((bf16[8,128,768]{2,1,0:T(8,128)(2,1)}), bf16[8,128,768]{2,1,0:T(8,128)(2,1)S(1)}, u32[]{:S(2)}, u32[]{:S(2)}) async-start(bf16[8,128,768]{2,1,0:T(8,128)(2,1)} %broadcast_in_dim.112), calls=%async_computation | async-start | bytes 3145728 | tf_op jit(solution)/shard_map/all_to_all | solution.py:53
  25.9 15.8 %all-to-all-done = bf16[8,128,768]{2,1,0:T(8,128)(2,1)S(1)} async-done(((bf16[8,128,768]{2,1,0:T(8,128)(2,1)}), bf16[8,128,768]{2,1,0:T(8,128)(2,1)S(1)}, u32[]{:S(2)}, u32[]{:S(2)}) %all-to-all-start) | async-done | bytes 1572896 | tf_op jit(solution)/shard_map/all_to_all | solution.py:53
  42.8 6.2 %all-to-all-start.2 = ((bf16[32,32,768]{2,1,0:T(8,128)(2,1)}), bf16[32,32,768]{2,1,0:T(8,128)(2,1)S(1)}, u32[]{:S(2)}, u32[]{:S(2)}) async-start(bf16[32,32,768]{2,1,0:T(8,128)(2,1)} %bitcast.64), calls=%async_computation.2 | async-start | bytes 3145728 | tf_op jit(solution)/shard_map/all_to_all | solution.py:53
  55.7 11.1 %keys_and_values.1 = (bf16[2048,768]{1,0:T(8,128)(2,1)}, bf16[2,6,2048,128]{3,2,1,0:T(8,128)(2,1)}) custom-call(s32[32]{0:T(128)} %get-tuple-element.157.place_ref, bf16[1024,768]{1,0:T(8,128)(2,1)} %bitcast.67, bf16[1024,768]{1,0:T(8,128)(2,1)} %bitcast.2.far_ref, f32[1,768]{1,0:T(1,128)} %broadcast_in_dim.113.gain_ref, bf16[768,2304]{1,0:T(8,128)(2,1)} %weight_ref.3, ...), custom_call_target="tpu_custom_call" | custom-call | flops 4831838208 | bytes 12582912 | tf_op jit(solution)/shard_map/keys_and_values/pallas_call | solution.py:231
  66.9 10.8 %attend.1 = (bf16[128,768]{1,0:T(8,128)(2,1)}, bf16[12,128,2048]{2,1,0:T(8,128)(2,1)}, f32[6,256,128]{2,1,0:T(8,128)}) custom-call(bf16[128,768]{1,0:T(8,128)(2,1)} %convolution_convert_fusion.1.q_ref, bf16[2,6,2048,128]{3,2,1,0:T(8,128)(2,1)} %get-tuple-element.62.kv_ref, f32[6,4,2176]{2,1,0:T(4,128)} %reshape.260.window_ref), custom_call_target="tpu_custom_call" | custom-call | flops 1610612736 | bytes 12582912 | tf_op jit(solution)/shard_map/attend/pallas_call | solution.py:120
  81.9 7.3 %all-to-all-start.1 = ((bf16[32,32,896]{2,1,0:T(8,128)(2,1)}), bf16[32,32,896]{2,1,0:T(8,128)(2,1)S(1)}, u32[]{:S(2)}, u32[]{:S(2)}) async-start(bf16[32,32,896]{2,1,0:T(8,128)(2,1)} %bitcast.66), calls=%async_computation.1 | async-start | bytes 3670016 | tf_op jit(solution)/shard_map/all_to_all | solution.py:53
  89.4 16.3 %all-gather.3.cloned.1.call-done = bf16[8,768,768]{2,1,0:T(8,128)(2,1)} async-done(((bf16[2,768,768]{2,1,0:T(8,128)(2,1)}), bf16[8,768,768]{2,1,0:T(8,128)(2,1)}) %all-gather.3.cloned.1.call-update) | async-done | bytes 9437200 | tf_op jit(solution)/shard_map/all_gather | solution.py:861
  105.8 6.8 %cotangent_units.1.units_ref = bf16[2,512,1536]{2,1,0:T(8,128)(2,1)} custom-call(bf16[32,2,16,768]{3,2,1,0:T(8,128)(2,1)} %bitcast.49, bf16[4,2,768,768]{3,2,1,0:T(8,128)(2,1)} %bitcast.56), custom_call_target="tpu_custom_call" | custom-call | flops 2415919104 | bytes 7864320 | tf_op jit(solution)/shard_map/cotangent_units/pallas_call | solution.py:539
  114.5 18.6 %experts.1 = (bf16[32,2,16,896]{3,2,1,0:T(8,128)(2,1)}, bf16[32,2,16,768]{3,2,1,0:T(8,128)(2,1)}, bf16[4,768,768]{2,1,0:T(8,128)(2,1)}, bf16[1,512,1536]{2,1,0:T(8,128)(2,1)}, bf16[1,512,1536]{2,1,0:T(8,128)(2,1)}) custom-call(bf16[32,2,16,896]{3,2,1,0:T(8,128)(2,1)} %bitcast.59, bf16[32,2,16,768]{3,2,1,0:T(8,128)(2,1)} %bitcast.50, ...), custom_call_target="tpu_custom_call" | custom-call | flops 12079595520 | bytes 15728640 | tf_op jit(solution)/shard_map/experts/pallas_call | solution.py:641
  133.1 7.0 %all-to-all-start.3 = ((bf16[32,32,896]{2,1,0:T(8,128)(2,1)}), bf16[32,32,896]{2,1,0:T(8,128)(2,1)S(1)}, u32[]{:S(2)}, u32[]{:S(2)}) async-start(bf16[32,32,896]{2,1,0:T(8,128)(2,1)} %bitcast.65), calls=%async_computation.3 | async-start | bytes 3670016 | tf_op jit(solution)/shard_map/all_to_all | solution.py:53
  140.2 6.3 %expert_grads.1 = bf16[4,768,768]{2,1,0:T(8,128)(2,1)} custom-call(bf16[32,2,16,896]{3,2,1,0:T(8,128)(2,1)} %bitcast.60, bf16[32,2,16,768]{3,2,1,0:T(8,128)(2,1)} %bitcast.51, bf16[1,512,1536]{2,1,0:T(8,128)(2,1)} %get-tuple-element.67.act_ref, bf16[1,512,1536]{2,1,0:T(8,128)(2,1)} %get-tuple-element.68.pre_grad_ref), custom_call_target="tpu_custom_call" | custom-call | flops 2415919104 | bytes 7864320 | tf_op jit(solution)/shard_map/expert_grads/pallas_call | solution.py:685
  146.4 17.8 %all-to-all-done.3 = bf16[32,32,896]{2,1,0:T(8,128)(2,1)S(1)} async-done(((bf16[32,32,896]{2,1,0:T(8,128)(2,1)}), bf16[32,32,896]{2,1,0:T(8,128)(2,1)S(1)}, u32[]{:S(2)}, u32[]{:S(2)}) %all-to-all-start.3) | async-done | bytes 1835040 | tf_op jit(solution)/shard_map/all_to_all | solution.py:53
  165.4 5.9 %all-to-all-start.4 = ((bf16[32,32,768]{2,1,0:T(8,128)(2,1)}), bf16[32,32,768]{2,1,0:T(8,128)(2,1)S(1)}, u32[]{:S(2)}, u32[]{:S(2)}) async-start(bf16[32,32,768]{2,1,0:T(8,128)(2,1)} %bitcast.16), calls=%async_computation.4 | async-start | bytes 3145728 | tf_op jit(solution)/shard_map/all_to_all | solution.py:53
  172.2 5.5 %out_of_experts.1 = (f32[128,768]{1,0:T(8,128)}, bf16[128,768]{1,0:T(8,128)(2,1)}, bf16[128,768]{1,0:T(8,128)(2,1)}, f32[40,768]{1,0:T(8,128)}) custom-call(bf16[1024,896]{1,0:T(8,128)(2,1)} %bitcast.58, bf16[256,1024]{1,0:T(8,128)(2,1)} %copy-done.8, f32[128,128]{1,0:T(8,128)} %get-tuple-element.72.gate_ref, s32[128,2]{1,0:T(8,128)} %bitcast.71, ...), custom_call_target="tpu_custom_call" | custom-call | tf_op jit(solution)/shard_map/out_of_experts/pallas_call | solution.py:809
  177.7 14.3 %attend_back.1 = (bf16[128,768]{1,0:T(8,128)(2,1)}, bf16[2,6,2048,128]{3,2,1,0:T(8,128)(2,1)}, f32[2,6,2,2176]{3,2,1,0:T(2,128)}) custom-call(bf16[12,128,2048]{2,1,0:T(8,128)(2,1)} %get-tuple-element.63.exps_ref, f32[6,256,128]{2,1,0:T(8,128)} %get-tuple-element.64.inverse_ref, bf16[128,768]{1,0:T(8,128)(2,1)} %convolution_convert_fusion.1.q_ref, ...), custom_call_target="tpu_custom_call" | custom-call | flops 3221225472 | bytes 18874368 | tf_op jit(solution)/shard_map/attend_back/pallas_call | solution.py:180
  192.8 13.7 %weight_grads.1 = (bf16[3584,384]{1,0:T(8,128)(2,1)}, bf16[3584,384]{1,0:T(8,128)(2,1)}) custom-call(s32[1]{0:T(128)} %bitcast.15.core_ref.side_ref, bf16[128,768]{1,0:T(8,128)(2,1)} %get-tuple-element.79.dq_ref, bf16[128,768]{1,0:T(8,128)(2,1)} %copy-done.23, ...), custom_call_target="tpu_custom_call" | custom-call | flops 4831838208 | bytes 15728640 | tf_op jit(solution)/shard_map/weight_grads/pallas_call | solution.py:385
  216.8 7.1 %all-to-all-start.5 = ((bf16[64,56,384]{2,1,0:T(8,128)(2,1)}), bf16[64,56,384]{2,1,0:T(8,128)(2,1)S(1)}, u32[]{:S(2)}, u32[]{:S(2)}) async-start(bf16[64,56,384]{2,1,0:T(8,128)(2,1)} %bitcast.55), calls=%async_computation.5 | async-start | bytes 5505024 | tf_op jit(solution)/shard_map/all_to_all | solution.py:53
  224.5 7.0 %normed_grads.3 = bf16[1024,768]{1,0:T(8,128)(2,1)} custom-call(s32[16]{0:T(128)} %get-tuple-element.169.position_ref, bf16[2,6,2048,128]{3,2,1,0:T(8,128)(2,1)} %get-tuple-element.89.dkv_ref.refs_0_.refs_1_.refs_2_.refs_3_.refs_4_.refs_5_.refs_6_.refs_7_, ...), custom_call_target="tpu_custom_call" | custom-call | flops 2415919104 | bytes 6291456 | tf_op jit(solution)/shard_map/normed_grads/pallas_call | solution.py:282
  232.3 7.1 %normed_grads.2 = bf16[1024,768]{1,0:T(8,128)(2,1)} custom-call(s32[16]{0:T(128)} %get-tuple-element.168.position_ref, bf16[2,6,2048,128]{3,2,1,0:T(8,128)(2,1)} %get-tuple-element.89.dkv_ref.refs_0_.refs_1_.refs_2_.refs_3_.refs_4_.refs_5_.refs_6_.refs_7_, ...), custom_call_target="tpu_custom_call" | custom-call | flops 2415919104 | bytes 6291456 | tf_op jit(solution)/shard_map/normed_grads/pallas_call | solution.py:282
  246.0 25.6 %all-to-all-done.5 = bf16[64,56,384]{2,1,0:T(8,128)(2,1)S(1)} async-done(((bf16[64,56,384]{2,1,0:T(8,128)(2,1)}), bf16[64,56,384]{2,1,0:T(8,128)(2,1)S(1)}, u32[]{:S(2)}, u32[]{:S(2)}) %all-to-all-start.5) | async-done | bytes 2752544 | tf_op jit(solution)/shard_map/all_to_all | solution.py:53
  283.7 31.3 %all-to-all-done.6 = bf16[64,56,384]{2,1,0:T(8,128)(2,1)S(1)} async-done(((bf16[64,56,384]{2,1,0:T(8,128)(2,1)}), bf16[64,56,384]{2,1,0:T(8,128)(2,1)S(1)}, u32[]{:S(2)}, u32[]{:S(2)}) %all-to-all-start.6) | async-done | bytes 2752544 | tf_op jit(solution)/shard_map/all_to_all | solution.py:53
  321.6 5.9 %whole_grad.2 = (f32[768,2304]{1,0:T(8,128)}, f32[768,128]{1,0:T(8,128)}, f32[768,768]{1,0:T(8,128)}) custom-call(s32[1]{0:T(128)} %bitcast.15.core_ref.side_ref, bf16[3584,384]{1,0:T(8,128)(2,1)} %bitcast.53, bf16[768,2304]{1,0:T(8,128)(2,1)} %weight_ref.3), custom_call_target="tpu_custom_call" | custom-call | flops 1769472 | bytes 7077888 | tf_op jit(solution)/shard_map/whole_grad/pallas_call | solution.py:459
  327.6 5.9 %whole_grad.3 = (f32[768,2304]{1,0:T(8,128)}, f32[768,128]{1,0:T(8,128)}, f32[768,768]{1,0:T(8,128)}) custom-call(s32[1]{0:T(128)S(6)} %sub.50.side_ref, bf16[3584,384]{1,0:T(8,128)(2,1)} %collective-permute-done.3.half_ref, bf16[768,2304]{1,0:T(8,128)(2,1)} %weight_ref.3, ...), custom_call_target="tpu_custom_call", output_to_operand_aliasing={{0}: (3, {}), {1}: (4, {}), {2}: (5, {})} | custom-call | flops 1769472 | bytes 7077888 | tf_op jit(solution)/shard_map/whole_grad/pallas_call | solution.py:459
  335.7 6.8 %all-to-all-done.7 = bf16[8,128,768]{2,1,0:T(8,128)(2,1)} async-done(((bf16[8,128,768]{2,1,0:T(8,128)(2,1)}), bf16[8,128,768]{2,1,0:T(8,128)(2,1)}, u32[]{:S(2)}, u32[]{:S(2)}) %all-to-all-start.7) | async-done | bytes 1572896 | tf_op jit(solution)/shard_map/all_to_all | solution.py:53
  (137 shorter events, 69.1 us)
Async XLA Ops:
  7.2 42.8 %copy-start = (f32[32,12]{0,1:T(8,128)S(1)}, f32[32,12]{0,1:T(8,128)}, u32[]{:S(2)}) copy-start(f32[32,12]{0,1:T(8,128)} %param.16) | copy-start | bytes 4612
  7.2 98.6 %all-gather.3.cloned.1.call-start = ((), (), s32[]{:S(2)}) async-start(), calls=%async_computation.12 | async-start | bytes 11796480 | tf_op jit(solution)/shard_map/all_gather | solution.py:861
  12.6 29.1 %all-to-all-start = ((bf16[8,128,768]{2,1,0:T(8,128)(2,1)}), bf16[8,128,768]{2,1,0:T(8,128)(2,1)S(1)}, u32[]{:S(2)}, u32[]{:S(2)}) async-start(bf16[8,128,768]{2,1,0:T(8,128)(2,1)} %broadcast_in_dim.112), calls=%async_computation | async-start | bytes 3145728 | tf_op jit(solution)/shard_map/all_to_all | solution.py:53
  23.5 19.3 %copy-start.18 = (s32[1,128,2]{2,1,0:T(8,128)}, s32[1,128,2]{2,1,0:T(8,128)S(1)}, u32[]{:S(2)}) copy-start(s32[1,128,2]{2,1,0:T(8,128)S(1)} %copy.40) | copy-start | bytes 3076
  24.1 18.7 %copy-start.8 = (bf16[256,1024]{1,0:T(8,128)(2,1)}, bf16[256,1024]{1,0:T(8,128)(2,1)S(1)}, u32[]{:S(2)}) copy-start(bf16[256,1024]{1,0:T(8,128)(2,1)S(1)} %fusion.7.table_ref) | copy-start | bytes 1572868
  24.1 25.3 %copy-start.24 = (f32[768]{0:T(1024)S(1)}, f32[768]{0:T(1024)}, u32[]{:S(2)}) copy-start(f32[768]{0:T(1024)} %param.14) | copy-start | bytes 9220
  25.9 25.2 %copy-start.27 = (f32[768]{0:T(1024)S(1)}, f32[768]{0:T(1024)}, u32[]{:S(2)}) copy-start(f32[768]{0:T(1024)} %param.18) | copy-start | bytes 9220
  25.9 25.8 %copy-start.25 = (bf16[768,32]{0,1:T(8,128)(2,1)S(1)}, bf16[768,32]{0,1:T(8,128)(2,1)}, u32[]{:S(2)}) copy-start(bf16[768,32]{0,1:T(8,128)(2,1)} %param.19) | copy-start | bytes 147460
  42.8 39.0 %all-to-all-start.2 = ((bf16[32,32,768]{2,1,0:T(8,128)(2,1)}), bf16[32,32,768]{2,1,0:T(8,128)(2,1)S(1)}, u32[]{:S(2)}, u32[]{:S(2)}) async-start(bf16[32,32,768]{2,1,0:T(8,128)(2,1)} %bitcast.64), calls=%async_computation.2 | async-start | bytes 3145728 | tf_op jit(solution)/shard_map/all_to_all | solution.py:53
  49.0 6.7 %collective-permute-start = (bf16[8,128,768]{2,1,0:T(8,128)(2,1)}, bf16[8,128,768]{2,1,0:T(8,128)(2,1)}, u32[]{:S(2)}, u32[]{:S(2)}) collective-permute-start(bf16[8,128,768]{2,1,0:T(8,128)(2,1)} %copy-done.12), channel_id=1, source_target_pairs={{0,8},{8,0},{1,9},{9,1},{2,10},{10,2},{3,11},{11,3},{4,12},{12,4},... | collective-permute-start | bytes 4718600 | tf_op jit(solution)/shard_map/ppermute | solution.py:855
  53.4 13.5 %copy-start.23 = (bf16[128,768]{1,0:T(8,128)(2,1)}, bf16[128,768]{1,0:T(8,128)(2,1)S(1)}, u32[]{:S(2)}) copy-start(bf16[128,768]{1,0:T(8,128)(2,1)S(1)} %fusion.15.normed_ref) | copy-start | bytes 589828
  81.8 23.9 %copy-start.2 = (bf16[32,32,768]{2,1,0:T(8,128)(2,1)}, bf16[32,32,768]{2,1,0:T(8,128)(2,1)S(1)}, u32[]{:S(2)}) copy-start(bf16[32,32,768]{2,1,0:T(8,128)(2,1)S(1)} %all-to-all-done.2) | copy-start | bytes 4718596
  81.9 31.4 %all-to-all-start.1 = ((bf16[32,32,896]{2,1,0:T(8,128)(2,1)}), bf16[32,32,896]{2,1,0:T(8,128)(2,1)S(1)}, u32[]{:S(2)}, u32[]{:S(2)}) async-start(bf16[32,32,896]{2,1,0:T(8,128)(2,1)} %bitcast.66), calls=%async_computation.1 | async-start | bytes 3670016 | tf_op jit(solution)/shard_map/all_to_all | solution.py:53
  89.2 182.8 %reduce-scatter.3.cloned.1.call-start = ((), (), s32[]{:S(2)}) async-start(), calls=%async_computation.10 | async-start | bytes 5898240 | tf_op jit(solution)/shard_map/reduce_scatter | solution.py:946
  133.1 31.1 %all-to-all-start.3 = ((bf16[32,32,896]{2,1,0:T(8,128)(2,1)}), bf16[32,32,896]{2,1,0:T(8,128)(2,1)S(1)}, u32[]{:S(2)}, u32[]{:S(2)}) async-start(bf16[32,32,896]{2,1,0:T(8,128)(2,1)} %bitcast.65), calls=%async_computation.3 | async-start | bytes 3670016 | tf_op jit(solution)/shard_map/all_to_all | solution.py:53
  140.1 131.9 %reduce-scatter.5.cloned.1.call-start = ((), (), s32[]{:S(2)}) async-start(), calls=%async_computation.11 | async-start | bytes 5898240 | tf_op jit(solution)/shard_map/reduce_scatter | solution.py:946
  165.4 27.4 %all-to-all-start.4 = ((bf16[32,32,768]{2,1,0:T(8,128)(2,1)}), bf16[32,32,768]{2,1,0:T(8,128)(2,1)S(1)}, u32[]{:S(2)}, u32[]{:S(2)}) async-start(bf16[32,32,768]{2,1,0:T(8,128)(2,1)} %bitcast.16), calls=%async_computation.4 | async-start | bytes 3145728 | tf_op jit(solution)/shard_map/all_to_all | solution.py:53
  192.8 13.7 %copy-start.13 = (bf16[32,32,768]{2,1,0:T(8,128)(2,1)}, bf16[32,32,768]{2,1,0:T(8,128)(2,1)S(1)}, u32[]{:S(2)}) copy-start(bf16[32,32,768]{2,1,0:T(8,128)(2,1)S(1)} %all-to-all-done.4) | copy-start | bytes 4718596
  206.5 6.3 %collective-permute-start.1 = (bf16[3584,384]{1,0:T(8,128)(2,1)}, bf16[3584,384]{1,0:T(8,128)(2,1)S(1)}, u32[]{:S(2)}, u32[]{:S(2)}) collective-permute-start(bf16[3584,384]{1,0:T(8,128)(2,1)} %get-tuple-element.88), channel_id=1, source_target_pairs={{0,8},{8,0},{1,9},{9,1},{2,10},{10,2},{3,11},{11,3},{4,12},{12,4},... | collective-permute-start | bytes 8257544 | tf_op jit(solution)/shard_map/ppermute | solution.py:63
  216.8 54.8 %all-to-all-start.5 = ((bf16[64,56,384]{2,1,0:T(8,128)(2,1)}), bf16[64,56,384]{2,1,0:T(8,128)(2,1)S(1)}, u32[]{:S(2)}, u32[]{:S(2)}) async-start(bf16[64,56,384]{2,1,0:T(8,128)(2,1)} %bitcast.55), calls=%async_computation.5 | async-start | bytes 5505024 | tf_op jit(solution)/shard_map/all_to_all | solution.py:53
  231.5 11.5 %collective-permute-start.2 = (bf16[1024,768]{1,0:T(8,128)(2,1)}, bf16[1024,768]{1,0:T(8,128)(2,1)}, u32[]{:S(2)}, u32[]{:S(2)}) collective-permute-start(bf16[1024,768]{1,0:T(8,128)(2,1)} %normed_grads.3), channel_id=1, source_target_pairs={{0,8},{8,0},{1,9},{9,1},{2,10},{10,2},{3,11},{11,3},{4,12},{12,4},... | collective-permute-start | bytes 4718600 | tf_op jit(solution)/shard_map/ppermute | solution.py:994
  273.8 41.2 %all-to-all-start.6 = ((bf16[64,56,384]{2,1,0:T(8,128)(2,1)}), bf16[64,56,384]{2,1,0:T(8,128)(2,1)S(1)}, u32[]{:S(2)}, u32[]{:S(2)}) async-start(bf16[64,56,384]{2,1,0:T(8,128)(2,1)} %broadcast_in_dim.120), calls=%async_computation.8 | async-start | bytes 5505024 | tf_op jit(solution)/shard_map/all_to_all | solution.py:53
  315.0 12.5 %collective-permute-start.3 = (bf16[3584,384]{1,0:T(8,128)(2,1)S(1)}, bf16[3584,384]{1,0:T(8,128)(2,1)}, u32[]{:S(2)}, u32[]{:S(2)}) collective-permute-start(bf16[3584,384]{1,0:T(8,128)(2,1)S(1)} %bitcast.52), channel_id=1, source_target_pairs={{0,8},{8,0},{1,9},{9,1},{2,10},{10,2},{3,11},{11,3},{4,12},{12,4},... | collective-permute-start | bytes 8257544 | tf_op jit(solution)/shard_map/ppermute | solution.py:1008
  317.3 25.2 %all-to-all-start.7 = ((bf16[8,128,768]{2,1,0:T(8,128)(2,1)}), bf16[8,128,768]{2,1,0:T(8,128)(2,1)}, u32[]{:S(2)}, u32[]{:S(2)}) async-start(bf16[8,128,768]{2,1,0:T(8,128)(2,1)} %bitcast.63), calls=%async_computation.9 | async-start | bytes 3145728 | tf_op jit(solution)/shard_map/all_to_all | solution.py:53
  (21 other events, 120.8 us)
Sparse Core Ops, SparseCore 0:
  10.5 95.1 all-gather.2
  133.2 51.3 reduce-scatter.2
  187.0 67.1 reduce-scatter.4

commit v3 on v2

--- a/solution.py
+++ b/solution.py
@@ -492,7 +492,7 @@
     rows_in = x_ref[...].reshape(rows, x_ref.shape[2])
     gate = jnp.sum(rows_in[:, width:].astype(F32), axis=1, keepdims=True)
     slot_grad = (cot_ref[...].reshape(rows, width).astype(F32) * gate).astype(BF)
-    return rows_in[:, :width], slot_grad, gate
+    return rows_in[:, :width], slot_grad
 
 
 def high_and_low(column):
@@ -513,6 +513,29 @@
         grad_ref[index, hidden:] = grad_out[index * hidden : (index + 1) * hidden]
 
 
+def pack_kernel(in_ref, out_ref, packed_ref):
+    hidden = out_ref.shape[0]
+    packed_ref[:hidden, :hidden] = in_ref[:hidden]
+    packed_ref[:hidden, hidden:] = in_ref[hidden:]
+    packed_ref[hidden:] = out_ref[...]
+
+
+def packed_weights(w_in, w_out):
+    experts, width, hidden = w_in.shape
+    return pl.pallas_call(
+        pack_kernel,
+        grid=(experts,),
+        in_specs=[
+            pl.BlockSpec((None, width, hidden), lambda e: (e, 0, 0)),
+            pl.BlockSpec((None, hidden, width), lambda e: (e, 0, 0)),
+        ],
+        out_specs=pl.BlockSpec((None, 2 * hidden, width), lambda e: (e, 0, 0)),
+        out_shape=jax.ShapeDtypeStruct((experts, 2 * hidden, width), BF),
+        compiler_params=pltpu.CompilerParams(vmem_limit_bytes=VMEM_LIMIT),
+        name="packed_weights",
+    )(w_in, w_out)
+
+
 def slice_weights(weight_ref):
     slices, hidden = weight_ref.shape[0], weight_ref.shape[1] // 2
     weights = [weight_ref[index] for index in range(slices)]
@@ -522,43 +545,9 @@
     return jnp.concatenate(tops, axis=1), weight_out
 
 
-def cotangent_kernel(cot_ref, weight_ref, units_ref):
-    rows = cot_ref.shape[0] * cot_ref.shape[1]
-    cot = cot_ref[...].reshape(rows, cot_ref.shape[2])
-    slices, hidden = weight_ref.shape[0], weight_ref.shape[1]
-    weight_out = weight_ref[...].reshape(slices * hidden, weight_ref.shape[2])
-    units_ref[...] = contract_cols(cot, weight_out).astype(BF)
-
-
-def cotangent_units(cot_rows, weights):
-    devices, experts, slots, width = cot_rows.shape
-    parts, _, both, _ = weights.shape
-    hidden = both // 2
-    rows = devices * slots
-    slices = 2
-    return pl.pallas_call(
-        cotangent_kernel,
-        grid=(experts, parts // slices),
-        in_specs=[
-            pl.BlockSpec((devices, None, slots, width), lambda e, w: (0, e, 0, 0)),
-            pl.BlockSpec((slices, None, hidden, width), lambda e, w: (w, e, 1, 0)),
-        ],
-        out_specs=pl.BlockSpec((None, rows, slices * hidden), lambda e, w: (e, 0, w)),
-        out_shape=jax.ShapeDtypeStruct((experts, rows, parts * hidden), BF),
-        compiler_params=pltpu.CompilerParams(vmem_limit_bytes=VMEM_LIMIT),
-        cost_estimate=pl.CostEstimate(
-            flops=2 * experts * rows * width * parts * hidden,
-            bytes_accessed=4 * experts * rows * width + 2 * parts * experts * width * hidden,
-            transcendentals=0,
-        ),
-        name="cotangent_units",
-    )(cot_rows, weights)
-
-
 def expert_kernel(
     x_ref,
     cot_ref,
-    units_ref,
     weight_ref,
     dx_ref,
     ret_ref,
@@ -570,10 +559,10 @@
 ):
     part = pl.program_id(1)
     width = cot_ref.shape[-1]
-    x, slot_grad, gate = expert_rows(x_ref, cot_ref)
+    x, slot_grad = expert_rows(x_ref, cot_ref)
     weight_in, weight_out = slice_weights(weight_ref)
     pre = jnp.dot(x, weight_in, preferred_element_type=F32)
-    act_grad = units_ref[...].astype(F32) * gate
+    act_grad = contract_cols(slot_grad, weight_out)
     cumulative = 0.5 * (1.0 + lax.erf(pre * 0.7071067811865476))
     activated = (pre * cumulative).astype(BF)
     slope = cumulative + pre * (jnp.exp(-0.5 * pre * pre) * 0.3989422804014327)
@@ -613,11 +602,11 @@
 
 
 def expert_grad_kernel(x_ref, cot_ref, act_ref, pre_grad_ref, grad_ref):
-    x, slot_grad, _ = expert_rows(x_ref, cot_ref)
+    x, slot_grad = expert_rows(x_ref, cot_ref)
     write_weight_grads(x, slot_grad, act_ref[...], pre_grad_ref[...], grad_ref)
 
 
-def run_experts(x_rows, cot_rows, units, weights):
+def run_experts(x_rows, cot_rows, weights):
     devices, experts, slots, width = cot_rows.shape
     wide = x_rows.shape[3]
     parts, _, both, _ = weights.shape
@@ -644,7 +633,6 @@
         in_specs=[
             row_spec(wide),
             row_spec(width),
-            pl.BlockSpec((None, rows, slices * hidden), lambda e, w: (e, 0, w)),
             pl.BlockSpec((slices, None, both, width), lambda e, w: (w, e, 0, 0)),
         ],
         out_specs=[
@@ -671,7 +659,7 @@
             transcendentals=2 * experts * rows * parts * hidden,
         ),
         name="experts",
-    )(x_rows, cot_rows, units, weights)
+    )(x_rows, cot_rows, weights)
     weight_grads_of = [first_grad]
     for expert in range(1, experts):
 
@@ -852,13 +840,8 @@
     copies = expert_devices // ctx_count
 
     near_tokens = spread(tokens[0], SAME_CORE)
-    far_tokens = lax.ppermute(near_tokens, "core", SWAP)
-    near_tokens = near_tokens.reshape(seq // 2, model_width)
-    far_tokens = far_tokens.reshape(seq // 2, model_width)
     hidden = w_in.shape[2]
-    weights = jnp.concatenate([w_in[:, :hidden], w_in[:, hidden:]], axis=2)
-    weights = jnp.concatenate([weights, w_out], axis=1)
-    weights = lax.all_gather(weights, "x", axis=0)
+    weights = lax.all_gather(packed_weights(w_in, w_out), "x", axis=0)
 
     chosen = routes[0].T
     expert_ids = jnp.arange(experts, dtype=jnp.int32)
@@ -881,7 +864,7 @@
         arrived = exchange(slots.reshape(expert_devices, device_slots, -1), EXPERT_AXES)
         return arrived.reshape(expert_devices, local_experts, capacity, -1)
 
-    cot_rows = to_slots(contract_rows(token_table, cotangent[0]).astype(BF))
+    cot_slots = contract_rows(token_table, cotangent[0]).astype(BF)
 
     ctx_ids = jnp.arange(ctx_count, dtype=jnp.int32)
     my_core = lax.axis_index("core")
@@ -922,6 +905,12 @@
     normed_one = (inputs * scale_one * gain_attn).astype(BF)
     w_q = w_qkv[:, :model_width]
     queries = jnp.dot(normed_one, w_q, preferred_element_type=F32).astype(BF)
+    near_tokens, queries, windows, place, slot_table, cot_slots = lax.optimization_barrier(
+        (near_tokens, queries, windows, place, slot_table, cot_slots)
+    )
+    cot_rows = to_slots(cot_slots)
+    near_tokens = near_tokens.reshape(seq // 2, model_width)
+    far_tokens = lax.ppermute(near_tokens, "core", SWAP)
     all_normed, key_value = keys_and_values(
         place, near_tokens, far_tokens, gain_attn, w_qkv, half
     )
@@ -931,16 +920,15 @@
         attended, tokens[0], w_attn_out, gain_ffn, w_router, routes[0], slot_table
     )
     x_rows = to_slots(slots)
-    units = cotangent_units(cot_rows, weights)
-    input_grad, returned, parts = run_experts(x_rows, cot_rows, units, weights)
+    input_grad, returned, parts = run_experts(x_rows, cot_rows, weights)
 
     def from_experts(rows):
         rows = exchange(rows.reshape(expert_devices, device_slots, rows.shape[3]), EXPERT_AXES)
         return rows.reshape(expert_devices * device_slots, rows.shape[2])
 
     input_grad = from_experts(input_grad)
-    later_parts, input_grad, returned = lax.optimization_barrier(
-        (parts[1:], input_grad, returned)
+    later_parts, input_grad, returned, bucket_hot = lax.optimization_barrier(
+        (parts[1:], input_grad, returned, bucket_hot)
     )
     shares = [
         lax.psum_scatter(part, "x", scatter_dimension=0) for part in (parts[0], *later_parts)
@@ -1009,10 +997,7 @@
     row_grads = exchange(near_grad, SAME_CORE)
     held = whole_grad(core, mine, w_qkv, ())
     whole = whole_grad(1 - core, other, w_qkv, held)
-    row_grads, sum_w_qkv, products, sum_w_attn_out = lax.optimization_barrier((row_grads, *whole))
-    normed_one_grad = jnp.sum(row_grads.astype(F32), axis=0) + query_part
-    input_norm_grad, _ = norm_backward(inputs, scale_one, gain_attn, normed_one_grad)
-    grad_tokens = (mixed_grad + input_norm_grad)[None]
+    sum_w_qkv, products, sum_w_attn_out = whole
     sum_gain_attn = products[:, 0] / gain_attn
     rows = slice(4 * model_width, 4 * model_width + small.shape[0] + bucket_count)
     left = jnp.where(my_core == 0, mine[rows], other[rows])
@@ -1020,6 +1005,14 @@
     sums = jnp.concatenate([left, right], axis=1).astype(F32)
     sum_w_router, sum_gain_ffn = sums[:experts].T, sums[experts]
     sum_rel_bias = sums[small.shape[0] :, :head_count]
+    row_grads, sum_w_qkv, sum_gain_attn, sum_w_router, sum_gain_ffn, sum_rel_bias = (
+        lax.optimization_barrier(
+            (row_grads, sum_w_qkv, sum_gain_attn, sum_w_router, sum_gain_ffn, sum_rel_bias)
+        )
+    )
+    normed_one_grad = jnp.sum(row_grads.astype(F32), axis=0) + query_part
+    input_norm_grad, _ = norm_backward(inputs, scale_one, gain_attn, normed_one_grad)
+    grad_tokens = (mixed_grad + input_norm_grad)[None]
     return (
         layer_out,
         grad_tokens,

time: 355 us -> 348 us (0.980)
  blocking collectives: 0 us -> 32.1 us
  waiting for transfers between devices: 120 us -> 96.5 us
  starting transfers between devices: 56.1 us -> 46.6 us
    all_to_all x0 -> x1, blocking collectives: none -> 32.1 us  [exchange(): return lax.all_to_all(array, axes, split_axis=0, concat_axis=0, tiled=True)]
    all_gather x1, waiting for transfers between devices: 16.3 us -> 0.01 us  [on_device(): weights = lax.all_gather(packed_weights(w_in, w_out), 'x', axis=0)]
    all_to_all x8 -> x7, starting transfers between devices: 51.2 us -> 40.5 us  [exchange(): return lax.all_to_all(array, axes, split_axis=0, concat_axis=0, tiled=True)]
    all_to_all x8 -> x7, waiting for transfers between devices: 99 us -> 91.5 us  [exchange(): return lax.all_to_all(array, axes, split_axis=0, concat_axis=0, tiled=True)]
    pallas_call x1, Pallas kernels: 6.78 us -> 2.75 us  [packed_weights(): pl.pallas_call(pack_kernel, grid=(experts,), in_specs=[pl.BlockSpec((None...]
  transfers between devices with their start and end apart: 15 -> 14, of which waited for: 9 -> 7; matrix products, arithmetic and copies ran while one was open for 9% -> 9% of each run, Pallas kernels for 28% -> 27%
where the time goes in v3:
time: 348 us; the launch traced here: 346 us
  Pallas kernels  115 us (33%)
  waiting for transfers between devices  96.5 us (28%)
  starting transfers between devices  46.6 us (13%)
  blocking collectives  32.1 us (9%)
  other arithmetic  20.4 us (6%)
  between operations  15.5 us (4%)
  local copies, waits for them, and re-layouts  12.5 us (4%)
  matrix products  7.2 us (2%)
    all_to_all x7, waiting for transfers between devices, exchange(): return lax.all_to_all(array, axes, split_axis=0, concat_axis=0, tiled=True)  91.5 us
    all_to_all x7, starting transfers between devices, exchange(): return lax.all_to_all(array, axes, split_axis=0, concat_axis=0, tiled=True)  40.5 us
    all_to_all x1, blocking collectives, exchange(): return lax.all_to_all(array, axes, split_axis=0, concat_axis=0, tiled=True)  32.1 us
    pallas_call x1, Pallas kernels, run_experts(): pl.pallas_call(expert_kernel, grid=(experts, steps), in_specs=[row_spec(w...  20.5 us
    pallas_call x1, Pallas kernels, attend_back(): pl.pallas_call(attend_back_kernel, grid=(pairs,), in_specs=[pl.BlockSpec(...  14.2 us
    pallas_call x2, Pallas kernels, normed_grads(): pl.pallas_call(normed_grad_kernel, grid_spec=pltpu.PrefetchScalarGridSpec...  14 us
    pallas_call x1, Pallas kernels, weight_grads(): pl.pallas_call(weight_grad_kernel, grid_spec=pltpu.PrefetchScalarGridSpec...  13.6 us
    pallas_call x2, Pallas kernels, whole_grad(): pl.pallas_call(whole_grad_kernel, grid_spec=pltpu.PrefetchScalarGridSpec(...  11.8 us
  transfers between devices with their start and end apart: 14, of which 7 were waited for; matrix products, arithmetic and copies ran while one was open for 9% of the time, Pallas kernels for 27%

profile of v3, /device:TPU:1, one launch (start us, length us, event | category | flops | bytes accessed | tf_op | source)
XLA Modules:
  0.0 346.1 jit_solution(13414994375250527430)
XLA Ops:
  12.2 8.6 %all-to-all-start = ((bf16[8,128,768]{2,1,0:T(8,128)(2,1)}), bf16[8,128,768]{2,1,0:T(8,128)(2,1)S(1)}, u32[]{:S(2)}, u32[]{:S(2)}) async-start(bf16[8,128,768]{2,1,0:T(8,128)(2,1)} %broadcast_in_dim.113), calls=%async_computation | async-start | bytes 3145728 | tf_op jit(solution)/shard_map/all_to_all | solution.py:53
  30.1 11.2 %all-to-all-done = bf16[8,128,768]{2,1,0:T(8,128)(2,1)S(1)} async-done(((bf16[8,128,768]{2,1,0:T(8,128)(2,1)}), bf16[8,128,768]{2,1,0:T(8,128)(2,1)S(1)}, u32[]{:S(2)}, u32[]{:S(2)}) %all-to-all-start) | async-done | bytes 1572896 | tf_op jit(solution)/shard_map/all_to_all | solution.py:53
  42.6 5.0 %all-to-all-start.2 = ((bf16[32,32,768]{2,1,0:T(8,128)(2,1)}), bf16[32,32,768]{2,1,0:T(8,128)(2,1)S(1)}, u32[]{:S(2)}, u32[]{:S(2)}) async-start(bf16[32,32,768]{2,1,0:T(8,128)(2,1)} %bitcast.9), calls=%async_computation.2 | async-start | bytes 3145728 | tf_op jit(solution)/shard_map/all_to_all | solution.py:53
  49.7 11.1 %keys_and_values.1 = (bf16[2048,768]{1,0:T(8,128)(2,1)}, bf16[2,6,2048,128]{3,2,1,0:T(8,128)(2,1)}) custom-call(s32[32]{0:T(128)} %get-tuple-element.72.place_ref, bf16[1024,768]{1,0:T(8,128)(2,1)} %bitcast.65, bf16[1024,768]{1,0:T(8,128)(2,1)} %collective-permute-done.far_ref, f32[1,768]{1,0:T(1,128)} %broadcast_in_dim.122.gain_ref, ...), custom_call_target="tpu_custom_call" | custom-call | flops 4831838208 | bytes 12582912 | tf_op jit(solution)/shard_map/keys_and_values/pallas_call | solution.py:231
  60.8 10.8 %attend.1 = (bf16[128,768]{1,0:T(8,128)(2,1)}, bf16[12,128,2048]{2,1,0:T(8,128)(2,1)}, f32[6,256,128]{2,1,0:T(8,128)}) custom-call(bf16[128,768]{1,0:T(8,128)(2,1)} %convolution_convert_fusion.1.q_ref, bf16[2,6,2048,128]{3,2,1,0:T(8,128)(2,1)} %get-tuple-element.74.kv_ref, f32[6,4,2176]{2,1,0:T(4,128)} %reshape.255.window_ref), custom_call_target="tpu_custom_call" | custom-call | flops 1610612736 | bytes 12582912 | tf_op jit(solution)/shard_map/attend/pallas_call | solution.py:120
  75.7 32.1 %all_to_all.40 = bf16[32,32,896]{2,1,0:T(8,128)(2,1)} all-to-all(bf16[32,32,896]{2,1,0:T(8,128)(2,1)} %bitcast.63), channel_id=1, replica_groups=mesh['ya'=2,'z'=4,'core'=2,'yb'=2,'x'=4] {'ya','z','core','yb'}, dimensions={0} | all-to-all | bytes 3670016 | tf_op jit(solution)/shard_map/all_to_all | solution.py:53
  107.8 20.5 %experts.1 = (bf16[32,2,16,896]{3,2,1,0:T(8,128)(2,1)}, bf16[32,2,16,768]{3,2,1,0:T(8,128)(2,1)}, bf16[4,768,768]{2,1,0:T(8,128)(2,1)}, bf16[1,512,1536]{2,1,0:T(8,128)(2,1)}, bf16[1,512,1536]{2,1,0:T(8,128)(2,1)}) custom-call(bf16[32,2,16,896]{3,2,1,0:T(8,128)(2,1)} %bitcast.54, bf16[32,2,16,768]{3,2,1,0:T(8,128)(2,1)} %bitcast.60, ...), custom_call_target="tpu_custom_call" | custom-call | flops 12079595520 | bytes 15728640 | tf_op jit(solution)/shard_map/experts/pallas_call | solution.py:630
  128.4 5.3 %all-to-all-start.3 = ((bf16[32,32,896]{2,1,0:T(8,128)(2,1)}), bf16[32,32,896]{2,1,0:T(8,128)(2,1)S(1)}, u32[]{:S(2)}, u32[]{:S(2)}) async-start(bf16[32,32,896]{2,1,0:T(8,128)(2,1)} %bitcast.62), calls=%async_computation.3 | async-start | bytes 3670016 | tf_op jit(solution)/shard_map/all_to_all | solution.py:53
  134.6 6.8 %expert_grads.1 = bf16[4,768,768]{2,1,0:T(8,128)(2,1)} custom-call(bf16[32,2,16,896]{3,2,1,0:T(8,128)(2,1)} %bitcast.55, bf16[32,2,16,768]{3,2,1,0:T(8,128)(2,1)} %bitcast.61, bf16[1,512,1536]{2,1,0:T(8,128)(2,1)} %get-tuple-element.82.act_ref, bf16[1,512,1536]{2,1,0:T(8,128)(2,1)} %get-tuple-element.83.pre_grad_ref), custom_call_target="tpu_custom_call" | custom-call | flops 2415919104 | bytes 7864320 | tf_op jit(solution)/shard_map/expert_grads/pallas_call | solution.py:673
  141.4 16.5 %all-to-all-done.3 = bf16[32,32,896]{2,1,0:T(8,128)(2,1)S(1)} async-done(((bf16[32,32,896]{2,1,0:T(8,128)(2,1)}), bf16[32,32,896]{2,1,0:T(8,128)(2,1)S(1)}, u32[]{:S(2)}, u32[]{:S(2)}) %all-to-all-start.3) | async-done | bytes 1835040 | tf_op jit(solution)/shard_map/all_to_all | solution.py:53
  159.1 5.9 %all-to-all-start.4 = ((bf16[32,32,768]{2,1,0:T(8,128)(2,1)}), bf16[32,32,768]{2,1,0:T(8,128)(2,1)S(1)}, u32[]{:S(2)}, u32[]{:S(2)}) async-start(bf16[32,32,768]{2,1,0:T(8,128)(2,1)} %bitcast.15), calls=%async_computation.4 | async-start | bytes 3145728 | tf_op jit(solution)/shard_map/all_to_all | solution.py:53
  165.0 5.5 %out_of_experts.1 = (f32[128,768]{1,0:T(8,128)}, bf16[128,768]{1,0:T(8,128)(2,1)}, bf16[128,768]{1,0:T(8,128)(2,1)}, f32[40,768]{1,0:T(8,128)}) custom-call(bf16[1024,896]{1,0:T(8,128)(2,1)} %bitcast.53, bf16[256,1024]{1,0:T(8,128)(2,1)} %copy-done.3, f32[128,128]{1,0:T(8,128)} %get-tuple-element.87.gate_ref, s32[128,2]{1,0:T(8,128)} %bitcast.68, ...), custom_call_target="tpu_custom_call" | custom-call | tf_op jit(solution)/shard_map/out_of_experts/pallas_call | solution.py:797
  170.4 14.2 %attend_back.1 = (bf16[128,768]{1,0:T(8,128)(2,1)}, bf16[2,6,2048,128]{3,2,1,0:T(8,128)(2,1)}, f32[2,6,2,2176]{3,2,1,0:T(2,128)}) custom-call(bf16[12,128,2048]{2,1,0:T(8,128)(2,1)} %get-tuple-element.76.exps_ref, f32[6,256,128]{2,1,0:T(8,128)} %get-tuple-element.77.inverse_ref, bf16[128,768]{1,0:T(8,128)(2,1)} %convolution_convert_fusion.1.q_ref, ...), custom_call_target="tpu_custom_call" | custom-call | flops 3221225472 | bytes 18874368 | tf_op jit(solution)/shard_map/attend_back/pallas_call | solution.py:180
  186.4 13.6 %weight_grads.1 = (bf16[3584,384]{1,0:T(8,128)(2,1)}, bf16[3584,384]{1,0:T(8,128)(2,1)}) custom-call(s32[1]{0:T(128)} %bitcast.14.core_ref.side_ref, bf16[128,768]{1,0:T(8,128)(2,1)} %get-tuple-element.94.dq_ref, bf16[128,768]{1,0:T(8,128)(2,1)} %copy-done.21, ...), custom_call_target="tpu_custom_call" | custom-call | flops 4831838208 | bytes 15728640 | tf_op jit(solution)/shard_map/weight_grads/pallas_call | solution.py:385
  201.4 4.9 %collective-permute-done.1 = bf16[3584,384]{1,0:T(8,128)(2,1)S(1)} collective-permute-done((bf16[3584,384]{1,0:T(8,128)(2,1)}, bf16[3584,384]{1,0:T(8,128)(2,1)S(1)}, u32[]{:S(2)}, u32[]{:S(2)}) %collective-permute-start.1) | collective-permute-done | bytes 2752544 | tf_op jit(solution)/shard_map/ppermute | solution.py:63
  210.4 6.7 %all-to-all-start.5 = ((bf16[64,56,384]{2,1,0:T(8,128)(2,1)}), bf16[64,56,384]{2,1,0:T(8,128)(2,1)S(1)}, u32[]{:S(2)}, u32[]{:S(2)}) async-start(bf16[64,56,384]{2,1,0:T(8,128)(2,1)} %bitcast.52), calls=%async_computation.5 | async-start | bytes 5505024 | tf_op jit(solution)/shard_map/all_to_all | solution.py:53
  217.6 7.0 %normed_grads.3 = bf16[1024,768]{1,0:T(8,128)(2,1)} custom-call(s32[16]{0:T(128)} %get-tuple-element.185.position_ref, bf16[2,6,2048,128]{3,2,1,0:T(8,128)(2,1)} %get-tuple-element.105.dkv_ref.refs_0_.refs_1_.refs_2_.refs_3_.refs_4_.refs_5_.refs_6_.refs_7_, ...), custom_call_target="tpu_custom_call" | custom-call | flops 2415919104 | bytes 6291456 | tf_op jit(solution)/shard_map/normed_grads/pallas_call | solution.py:282
  225.5 7.0 %normed_grads.2 = bf16[1024,768]{1,0:T(8,128)(2,1)} custom-call(s32[16]{0:T(128)} %get-tuple-element.184.position_ref, bf16[2,6,2048,128]{3,2,1,0:T(8,128)(2,1)} %get-tuple-element.105.dkv_ref.refs_0_.refs_1_.refs_2_.refs_3_.refs_4_.refs_5_.refs_6_.refs_7_, ...), custom_call_target="tpu_custom_call" | custom-call | flops 2415919104 | bytes 6291456 | tf_op jit(solution)/shard_map/normed_grads/pallas_call | solution.py:282
  239.1 26.0 %all-to-all-done.5 = bf16[64,56,384]{2,1,0:T(8,128)(2,1)S(1)} async-done(((bf16[64,56,384]{2,1,0:T(8,128)(2,1)}), bf16[64,56,384]{2,1,0:T(8,128)(2,1)S(1)}, u32[]{:S(2)}, u32[]{:S(2)}) %all-to-all-start.5) | async-done | bytes 2752544 | tf_op jit(solution)/shard_map/all_to_all | solution.py:53
  267.4 4.7 %all-to-all-start.6 = ((bf16[64,56,384]{2,1,0:T(8,128)(2,1)}), bf16[64,56,384]{2,1,0:T(8,128)(2,1)S(1)}, u32[]{:S(2)}, u32[]{:S(2)}) async-start(bf16[64,56,384]{2,1,0:T(8,128)(2,1)} %broadcast_in_dim.126), calls=%async_computation.8 | async-start | bytes 5505024 | tf_op jit(solution)/shard_map/all_to_all | solution.py:53
  277.2 31.0 %all-to-all-done.6 = bf16[64,56,384]{2,1,0:T(8,128)(2,1)S(1)} async-done(((bf16[64,56,384]{2,1,0:T(8,128)(2,1)}), bf16[64,56,384]{2,1,0:T(8,128)(2,1)S(1)}, u32[]{:S(2)}, u32[]{:S(2)}) %all-to-all-start.6) | async-done | bytes 2752544 | tf_op jit(solution)/shard_map/all_to_all | solution.py:53
  315.2 5.9 %whole_grad.2 = (f32[768,2304]{1,0:T(8,128)}, f32[768,128]{1,0:T(8,128)}, f32[768,768]{1,0:T(8,128)}) custom-call(s32[1]{0:T(128)} %bitcast.14.core_ref.side_ref, bf16[3584,384]{1,0:T(8,128)(2,1)} %bitcast.50, bf16[768,2304]{1,0:T(8,128)(2,1)} %weight_ref.3), custom_call_target="tpu_custom_call" | custom-call | flops 1769472 | bytes 7077888 | tf_op jit(solution)/shard_map/whole_grad/pallas_call | solution.py:459
  321.1 5.9 %whole_grad.3 = (f32[768,2304]{1,0:T(8,128)}, f32[768,128]{1,0:T(8,128)}, f32[768,768]{1,0:T(8,128)}) custom-call(s32[1]{0:T(128)S(6)} %sub.50.side_ref, bf16[3584,384]{1,0:T(8,128)(2,1)} %collective-permute-done.3.half_ref, bf16[768,2304]{1,0:T(8,128)(2,1)} %weight_ref.3, ...), custom_call_target="tpu_custom_call", output_to_operand_aliasing={{0}: (3, {}), {1}: (4, {}), {2}: (5, {})} | custom-call | flops 1769472 | bytes 7077888 | tf_op jit(solution)/shard_map/whole_grad/pallas_call | solution.py:459
  331.0 5.1 %all-to-all-done.7 = bf16[8,128,768]{2,1,0:T(8,128)(2,1)} async-done(((bf16[8,128,768]{2,1,0:T(8,128)(2,1)}), bf16[8,128,768]{2,1,0:T(8,128)(2,1)}, u32[]{:S(2)}, u32[]{:S(2)}) %all-to-all-start.7) | async-done | bytes 1572896 | tf_op jit(solution)/shard_map/all_to_all | solution.py:53
  (131 shorter events, 59.2 us)
Async XLA Ops:
  7.2 16.4 %copy-start = (f32[32,12]{0,1:T(8,128)S(1)}, f32[32,12]{0,1:T(8,128)}, u32[]{:S(2)}) copy-start(f32[32,12]{0,1:T(8,128)} %param.16) | copy-start | bytes 4612
  7.2 100.6 %all-gather.3.cloned.1.call-start = ((), (), s32[]{:S(2)}) async-start(), calls=%async_computation.12 | async-start | bytes 11796480 | tf_op jit(solution)/shard_map/all_gather | solution.py:844
  12.2 8.7 %copy-start.26 = (s32[16]{0:T(128)S(1)}, s32[16]{0:T(128)}, u32[]{:S(2)}) copy-start(s32[16]{0:T(128)} %param.23) | copy-start | bytes 196
  12.2 10.6 %copy-start.24 = (s32[2048]{0:T(1024)S(1)}, s32[2048]{0:T(1024)}, u32[]{:S(2)}) copy-start(s32[2048]{0:T(1024)} %param.24) | copy-start | bytes 24580
  12.2 10.8 %copy-start.27 = (s32[1,128,2]{1,2,0:T(2,128)S(1)}, s32[1,128,2]{1,2,0:T(2,128)}, u32[]{:S(2)}) copy-start(s32[1,128,2]{1,2,0:T(2,128)} %param.22) | copy-start | bytes 3076
  12.2 13.2 %copy-start.22 = (f32[768]{0:T(1024)S(1)}, f32[768]{0:T(1024)}, u32[]{:S(2)}) copy-start(f32[768]{0:T(1024)} %param.14) | copy-start | bytes 9220
  12.2 29.1 %all-to-all-start = ((bf16[8,128,768]{2,1,0:T(8,128)(2,1)}), bf16[8,128,768]{2,1,0:T(8,128)(2,1)S(1)}, u32[]{:S(2)}, u32[]{:S(2)}) async-start(bf16[8,128,768]{2,1,0:T(8,128)(2,1)} %broadcast_in_dim.113), calls=%async_computation | async-start | bytes 3145728 | tf_op jit(solution)/shard_map/all_to_all | solution.py:53
  30.1 18.1 %copy-start.25 = (f32[768]{0:T(1024)S(1)}, f32[768]{0:T(1024)}, u32[]{:S(2)}) copy-start(f32[768]{0:T(1024)} %param.18) | copy-start | bytes 9220
  30.1 18.7 %copy-start.23 = (bf16[768,32]{0,1:T(8,128)(2,1)S(1)}, bf16[768,32]{0,1:T(8,128)(2,1)}, u32[]{:S(2)}) copy-start(bf16[768,32]{0,1:T(8,128)(2,1)} %param.19) | copy-start | bytes 147460
  41.3 8.4 %collective-permute-start = (bf16[1024,768]{1,0:T(8,128)(2,1)S(1)}, bf16[1024,768]{1,0:T(8,128)(2,1)}, u32[]{:S(2)}, u32[]{:S(2)}) collective-permute-start(bf16[1024,768]{1,0:T(8,128)(2,1)S(1)} %bitcast.64), channel_id=1, source_target_pairs={{0,8},{8,0},{1,9},{9,1},{2,10},{10,2},{3,11},{11,3},{4,12},{12,4},... | collective-permute-start | bytes 4718600 | tf_op jit(solution)/shard_map/ppermute | solution.py:913
  42.6 33.2 %all-to-all-start.2 = ((bf16[32,32,768]{2,1,0:T(8,128)(2,1)}), bf16[32,32,768]{2,1,0:T(8,128)(2,1)S(1)}, u32[]{:S(2)}, u32[]{:S(2)}) async-start(bf16[32,32,768]{2,1,0:T(8,128)(2,1)} %bitcast.9), calls=%async_computation.2 | async-start | bytes 3145728 | tf_op jit(solution)/shard_map/all_to_all | solution.py:53
  47.6 218.0 %reduce-scatter.3.cloned.1.call-start = ((), (), s32[]{:S(2)}) async-start(), calls=%async_computation.10 | async-start | bytes 5898240 | tf_op jit(solution)/shard_map/reduce_scatter | solution.py:934
  75.7 32.1 %copy-start.10 = (bf16[32,32,768]{2,1,0:T(8,128)(2,1)}, bf16[32,32,768]{2,1,0:T(8,128)(2,1)S(1)}, u32[]{:S(2)}) copy-start(bf16[32,32,768]{2,1,0:T(8,128)(2,1)S(1)} %all-to-all-done.2) | copy-start | bytes 4718596
  128.4 29.5 %all-to-all-start.3 = ((bf16[32,32,896]{2,1,0:T(8,128)(2,1)}), bf16[32,32,896]{2,1,0:T(8,128)(2,1)S(1)}, u32[]{:S(2)}, u32[]{:S(2)}) async-start(bf16[32,32,896]{2,1,0:T(8,128)(2,1)} %bitcast.62), calls=%async_computation.3 | async-start | bytes 3670016 | tf_op jit(solution)/shard_map/all_to_all | solution.py:53
  133.7 131.9 %reduce-scatter.5.cloned.1.call-start = ((), (), s32[]{:S(2)}) async-start(), calls=%async_computation.11 | async-start | bytes 5898240 | tf_op jit(solution)/shard_map/reduce_scatter | solution.py:934
  159.1 27.3 %all-to-all-start.4 = ((bf16[32,32,768]{2,1,0:T(8,128)(2,1)}), bf16[32,32,768]{2,1,0:T(8,128)(2,1)S(1)}, u32[]{:S(2)}, u32[]{:S(2)}) async-start(bf16[32,32,768]{2,1,0:T(8,128)(2,1)} %bitcast.15), calls=%async_computation.4 | async-start | bytes 3145728 | tf_op jit(solution)/shard_map/all_to_all | solution.py:53
  186.4 13.7 %copy-start.8 = (bf16[32,32,768]{2,1,0:T(8,128)(2,1)}, bf16[32,32,768]{2,1,0:T(8,128)(2,1)S(1)}, u32[]{:S(2)}) copy-start(bf16[32,32,768]{2,1,0:T(8,128)(2,1)S(1)} %all-to-all-done.4) | copy-start | bytes 4718596
  200.1 6.3 %collective-permute-start.1 = (bf16[3584,384]{1,0:T(8,128)(2,1)}, bf16[3584,384]{1,0:T(8,128)(2,1)S(1)}, u32[]{:S(2)}, u32[]{:S(2)}) collective-permute-start(bf16[3584,384]{1,0:T(8,128)(2,1)} %get-tuple-element.104), channel_id=1, source_target_pairs={{0,8},{8,0},{1,9},{9,1},{2,10},{10,2},{3,11},{11,3},{4,12},{12,4},... | collective-permute-start | bytes 8257544 | tf_op jit(solution)/shard_map/ppermute | solution.py:63
  210.4 54.8 %all-to-all-start.5 = ((bf16[64,56,384]{2,1,0:T(8,128)(2,1)}), bf16[64,56,384]{2,1,0:T(8,128)(2,1)S(1)}, u32[]{:S(2)}, u32[]{:S(2)}) async-start(bf16[64,56,384]{2,1,0:T(8,128)(2,1)} %bitcast.52), calls=%async_computation.5 | async-start | bytes 5505024 | tf_op jit(solution)/shard_map/all_to_all | solution.py:53
  224.6 11.5 %collective-permute-start.2 = (bf16[1024,768]{1,0:T(8,128)(2,1)}, bf16[1024,768]{1,0:T(8,128)(2,1)}, u32[]{:S(2)}, u32[]{:S(2)}) collective-permute-start(bf16[1024,768]{1,0:T(8,128)(2,1)} %normed_grads.3), channel_id=1, source_target_pairs={{0,8},{8,0},{1,9},{9,1},{2,10},{10,2},{3,11},{11,3},{4,12},{12,4},... | collective-permute-start | bytes 4718600 | tf_op jit(solution)/shard_map/ppermute | solution.py:982
  267.4 40.8 %all-to-all-start.6 = ((bf16[64,56,384]{2,1,0:T(8,128)(2,1)}), bf16[64,56,384]{2,1,0:T(8,128)(2,1)S(1)}, u32[]{:S(2)}, u32[]{:S(2)}) async-start(bf16[64,56,384]{2,1,0:T(8,128)(2,1)} %broadcast_in_dim.126), calls=%async_computation.8 | async-start | bytes 5505024 | tf_op jit(solution)/shard_map/all_to_all | solution.py:53
  308.2 12.9 %collective-permute-start.3 = (bf16[3584,384]{1,0:T(8,128)(2,1)S(1)}, bf16[3584,384]{1,0:T(8,128)(2,1)}, u32[]{:S(2)}, u32[]{:S(2)}) collective-permute-start(bf16[3584,384]{1,0:T(8,128)(2,1)S(1)} %bitcast.49), channel_id=1, source_target_pairs={{0,8},{8,0},{1,9},{9,1},{2,10},{10,2},{3,11},{11,3},{4,12},{12,4},... | collective-permute-start | bytes 8257544 | tf_op jit(solution)/shard_map/ppermute | solution.py:996
  310.9 25.2 %all-to-all-start.7 = ((bf16[8,128,768]{2,1,0:T(8,128)(2,1)}), bf16[8,128,768]{2,1,0:T(8,128)(2,1)}, u32[]{:S(2)}, u32[]{:S(2)}) async-start(bf16[8,128,768]{2,1,0:T(8,128)(2,1)} %bitcast.58), calls=%async_computation.9 | async-start | bytes 3145728 | tf_op jit(solution)/shard_map/all_to_all | solution.py:53
  327.1 10.7 %copy-start.7 = (bf16[1,128,768]{2,1,0:T(8,128)(2,1)S(1)}, bf16[1,128,768]{2,1,0:T(8,128)(2,1)}, u32[]{:S(2)}) copy-start(bf16[1,128,768]{2,1,0:T(8,128)(2,1)} %param.13) | copy-start | bytes 589828
  (18 other events, 79.4 us)
Sparse Core Ops, SparseCore 0:
  10.3 95.1 all-gather.2
  128.5 49.6 reduce-scatter.2
  180.7 68.2 reduce-scatter.4

commit v4 on v3

--- a/solution.py
+++ b/solution.py
@@ -57,12 +57,14 @@
     return exchange(jnp.broadcast_to(array[None], (lax.axis_size(axes), *array.shape)), axes)
 
 
-def half_share(kept, given):
-    rows, columns = kept.shape
-    chips = lax.axis_size(CHIPS)
-    got = lax.ppermute(given, "core", SWAP)
-    half = (kept.astype(F32) + got.astype(F32)).astype(BF).reshape(chips, rows // chips, columns)
-    return jnp.sum(exchange(half, CHIPS).astype(F32), axis=0).astype(BF)
+def chip_share(parts):
+    sums = [(kept.astype(F32) + got.astype(F32)).astype(BF) for kept, got in parts]
+    total = jnp.concatenate(sums, axis=0)
+    for axes in (CHIPS[:-1], CHIPS[-1]):
+        count = lax.axis_size(axes)
+        pieces = total.reshape(count, total.shape[0] // count, total.shape[1])
+        total = jnp.sum(exchange(pieces, axes).astype(F32), axis=0).astype(BF)
+    return total
 
 
 def shear(tiles):
@@ -167,8 +169,8 @@
     score_grad = score_grad.astype(BF)
     query_grad = jnp.dot(score_grad, kv_ref[0], preferred_element_type=F32) * factor
     dq_ref[...] = join_heads(query_grad)
-    dkv_ref[0] = contract_rows(q, score_grad).T.astype(BF)
-    dkv_ref[1] = contract_rows(grad, exps).T.astype(BF)
+    dkv_ref[0] = contract_rows(q, score_grad).astype(BF)
+    dkv_ref[1] = contract_rows(grad, exps).astype(BF)
 
 
 def attend_back(exps, inverse, queries, key_value, attended_grad):
@@ -189,12 +191,12 @@
         ],
         out_specs=[
             row_spec,
-            kv_spec,
+            pl.BlockSpec((2, None, LANES, seq), lambda h: (0, h, 0, 0)),
             pl.BlockSpec((2, None, 2, window), lambda h: (0, h, 0, 0)),
         ],
         out_shape=[
             jax.ShapeDtypeStruct((rows, width), BF),
-            jax.ShapeDtypeStruct(key_value.shape, BF),
+            jax.ShapeDtypeStruct((2, pairs, LANES, seq), BF),
             jax.ShapeDtypeStruct((2, pairs, 2, window), F32),
         ],
         compiler_params=pltpu.CompilerParams(vmem_limit_bytes=VMEM_LIMIT),
@@ -257,55 +259,93 @@
     )(place, near, far, gain[None], w_qkv, w_qkv)
 
 
-def normed_grad_kernel(position_ref, *refs):
-    *block_refs, wk_ref, wv_ref, out_ref = refs
-    out = 0.0
+def normed_grad_kernel(place_ref, dkv_ref, wk_ref, wv_ref, out_ref, *, half):
+    total = 0.0
     for part, weight_ref in enumerate((wk_ref, wv_ref)):
-        rows = []
-        for block_ref in block_refs:
-            pairs = [block_ref[part, pair] for pair in range(block_ref.shape[1])]
-            rows.append(jnp.concatenate(pairs, axis=1))
-        out += contract_cols(jnp.concatenate(rows, axis=0), weight_ref[...])
-    out_ref[...] = out.astype(BF)
-
-
-def normed_grads(position, key_value_grad, w_qkv, half):
+        columns = dkv_ref[part].reshape(weight_ref.shape[1], dkv_ref.shape[3])
+        total += jnp.dot(weight_ref[...], columns, preferred_element_type=F32)
+    total = total.T.astype(BF)
+    step = total.shape[0] // half
+    for block in range(step):
+        target = place_ref[pl.program_id(0) * step + block]
+        at = pl.ds(pl.multiple_of(target * half, half), half)
+        out_ref[at] = total[block * half : (block + 1) * half]
+
+
+def normed_grads(place, key_value_grad, w_qkv, half):
     width = w_qkv.shape[0]
-    pairs = key_value_grad.shape[1]
-    count = position.shape[0]
-    rows = count * half
-    step = 8
-
-    def block_spec(at):
-        return pl.BlockSpec((2, pairs, half, LANES), lambda r, p: (0, 0, p[step * r + at], 0))
-
+    pairs, seq = key_value_grad.shape[1], key_value_grad.shape[3]
+    tile = 8 * half
     return pl.pallas_call(
-        normed_grad_kernel,
+        functools.partial(normed_grad_kernel, half=half),
         grid_spec=pltpu.PrefetchScalarGridSpec(
             num_scalar_prefetch=1,
-            grid=(count // step,),
+            grid=(seq // tile,),
             in_specs=[
-                *[block_spec(at) for at in range(step)],
+                pl.BlockSpec((2, pairs, LANES, tile), lambda r, p: (0, 0, 0, r)),
                 pl.BlockSpec((width, width), lambda r, p: (0, 1)),
                 pl.BlockSpec((width, width), lambda r, p: (0, 2)),
             ],
-            out_specs=pl.BlockSpec((step * half, width), lambda r, p: (r, 0)),
-        ),
-        out_shape=jax.ShapeDtypeStruct((rows, width), BF),
+            out_specs=pl.BlockSpec((seq, width), lambda r, p: (0, 0)),
+        ),
+        out_shape=jax.ShapeDtypeStruct((seq, width), BF),
         compiler_params=pltpu.CompilerParams(vmem_limit_bytes=VMEM_LIMIT),
         cost_estimate=pl.CostEstimate(
-            flops=4 * rows * width * width, bytes_accessed=8 * rows * width, transcendentals=0
+            flops=4 * seq * width * width, bytes_accessed=8 * seq * width, transcendentals=0
         ),
         name="normed_grads",
-    )(position, *([key_value_grad] * step), w_qkv, w_qkv)
+    )(place, key_value_grad, w_qkv, w_qkv)
+
+
+def give_halves(core_ref, total, kept_ref, given_ref):
+    rows, side = total.shape[0], kept_ref.shape[1]
+    left, right = total[:, :side].astype(BF), total[:, side:].astype(BF)
+
+    @pl.when(core_ref[0] == 0)
+    def _():
+        kept_ref[:rows] = left
+        given_ref[:rows] = right
+
+    @pl.when(core_ref[0] != 0)
+    def _():
+        kept_ref[:rows] = right
+        given_ref[:rows] = left
+
+
+def key_value_weight_kernel(core_ref, dkv_ref, all_normed_ref, kept_ref, given_ref):
+    columns = dkv_ref[...].reshape(dkv_ref.shape[0] * LANES, dkv_ref.shape[2])
+    total = jnp.dot(columns, all_normed_ref[...], preferred_element_type=F32)
+    give_halves(core_ref, total, kept_ref, given_ref)
+
+
+def key_value_weight_grads(core, key_value_grad, all_normed):
+    seq, width = all_normed.shape
+    out_spec = pl.BlockSpec((width, width // 2), lambda t, p: (t, 0))
+    out_shape = jax.ShapeDtypeStruct((2 * width, width // 2), BF)
+    return pl.pallas_call(
+        key_value_weight_kernel,
+        grid_spec=pltpu.PrefetchScalarGridSpec(
+            num_scalar_prefetch=1,
+            grid=(2,),
+            in_specs=[
+                pl.BlockSpec((None, width // LANES, LANES, seq), lambda t, p: (t, 0, 0, 0)),
+                pl.BlockSpec((seq, width), lambda t, p: (0, 0)),
+            ],
+            out_specs=[out_spec, out_spec],
+        ),
+        out_shape=[out_shape, out_shape],
+        compiler_params=pltpu.CompilerParams(vmem_limit_bytes=VMEM_LIMIT),
+        cost_estimate=pl.CostEstimate(
+            flops=4 * seq * width * width, bytes_accessed=8 * seq * width, transcendentals=0
+        ),
+        name="key_value_weight_grads",
+    )(core, key_value_grad, all_normed)
 
 
 def weight_grad_kernel(
     core_ref,
     dq_ref,
     normed_ref,
-    dkv_ref,
-    all_normed_ref,
     attended_ref,
     branch_ref,
     small_ref,
@@ -315,36 +355,18 @@
     given_ref,
 ):
     step = pl.program_id(0)
-    side = kept_ref.shape[1]
-
-    def give(total):
-        left, right = total[:, :side].astype(BF), total[:, side:].astype(BF)
-        rows = total.shape[0]
-
-        @pl.when(core_ref[0] == 0)
-        def _():
-            kept_ref[:rows] = left
-            given_ref[:rows] = right
-
-        @pl.when(core_ref[0] != 0)
-        def _():
-            kept_ref[:rows] = right
-            given_ref[:rows] = left
 
     @pl.when(step == 0)
     def _():
-        give(contract_rows(dq_ref[...], normed_ref[...]))
-
-    @pl.when((step == 1) | (step == 2))
-    def _():
-        pairs = [dkv_ref[pair] for pair in range(dkv_ref.shape[0])]
-        give(contract_rows(jnp.concatenate(pairs, axis=1), all_normed_ref[...]))
-
-    @pl.when(step == 3)
-    def _():
-        give(contract_rows(attended_ref[...], branch_ref[...]))
-
-    @pl.when(step == 4)
+        total = contract_rows(dq_ref[...], normed_ref[...])
+        give_halves(core_ref, total, kept_ref, given_ref)
+
+    @pl.when(step == 1)
+    def _():
+        total = contract_rows(attended_ref[...], branch_ref[...])
+        give_halves(core_ref, total, kept_ref, given_ref)
+
+    @pl.when(step == 2)
     def _():
         window = diag_ref.shape[3]
         bias_grad = 0.0
@@ -360,25 +382,14 @@
         buckets, heads = bias_grad.shape
         spare = jnp.zeros((buckets, small_ref.shape[1] - heads), F32)
         bias_rows = jnp.concatenate([bias_grad, spare], axis=1)
-        give(jnp.concatenate([small_ref[...], bias_rows], axis=0))
+        total = jnp.concatenate([small_ref[...], bias_rows], axis=0)
+        give_halves(core_ref, total, kept_ref, given_ref)
 
 
 def weight_grads(
-    core,
-    query_grad,
-    normed_one,
-    key_value_grad,
-    all_normed,
-    attended,
-    branch_grad,
-    small,
-    bucket_hot,
-    diagonals,
-    spare,
+    core, query_grad, normed_one, attended, branch_grad, small, bucket_hot, diagonals, total
 ):
     rows, width = normed_one.shape
-    seq = all_normed.shape[0]
-    total = 4 * width + small.shape[0] + bucket_hot.shape[0] + spare
     row_spec = pl.BlockSpec((rows, width), lambda t, p: (0, 0))
     out_spec = pl.BlockSpec((width, width // 2), lambda t, p: (t, 0))
     out_shape = jax.ShapeDtypeStruct((total, width // 2), BF)
@@ -386,14 +397,10 @@
         weight_grad_kernel,
         grid_spec=pltpu.PrefetchScalarGridSpec(
             num_scalar_prefetch=1,
-            grid=(5,),
+            grid=(3,),
             in_specs=[
                 row_spec,
                 row_spec,
-                pl.BlockSpec(
-                    (None, width // LANES, seq, LANES), lambda t, p: (jnp.clip(t - 1, 0, 1), 0, 0, 0)
-                ),
-                pl.BlockSpec((seq, width), lambda t, p: (0, 0)),
                 row_spec,
                 row_spec,
                 pl.BlockSpec(small.shape, lambda t, p: (0, 0)),
@@ -405,21 +412,10 @@
         out_shape=[out_shape, out_shape],
         compiler_params=pltpu.CompilerParams(vmem_limit_bytes=VMEM_LIMIT),
         cost_estimate=pl.CostEstimate(
-            flops=4 * seq * width * width, bytes_accessed=10 * seq * width, transcendentals=0
+            flops=4 * rows * width * width, bytes_accessed=16 * rows * width, transcendentals=0
         ),
         name="weight_grads",
-    )(
-        core,
-        query_grad,
-        normed_one,
-        key_value_grad,
-        all_normed,
-        attended,
-        branch_grad,
-        small,
-        bucket_hot,
-        diagonals,
-    )
+    )(core, query_grad, normed_one, attended, branch_grad, small, bucket_hot, diagonals)
 
 
 def whole_grad_kernel(side_ref, half_ref, weight_ref, *refs):
@@ -462,7 +458,9 @@
             num_scalar_prefetch=1,
             grid=(steps,),
             in_specs=[
-                pl.BlockSpec((width, half), lambda t, p: (t, 0)),
+                pl.BlockSpec(
+                    (width, half), lambda t, p: (jnp.where(t < steps - 1, (t + 2) % 3, 3), 0)
+                ),
                 pl.BlockSpec((half, width), tile_map),
                 *[pl.BlockSpec(memory_space=pl.ANY) for _ in held],
             ],
@@ -877,15 +875,6 @@
         axis=1,
         dtype=jnp.int32,
     )
-    positions = jnp.sum(
-        jnp.where(
-            2 * (block_ids // 2) == lies[None, :],
-            jnp.where(block_ids % 2 == 0, pair_order[None, :], blocks - 1 - pair_order[None, :]),
-            0,
-        ),
-        axis=1,
-        dtype=jnp.int32,
-    )
     my_pair = jnp.sum(jnp.where(ctx_ids == lax.axis_index(CTX), pair_order, 0))
     reversed_table = jnp.pad(bucket_table[::-1], (0, window - half), constant_values=-1)
     diagonal_bucket = jnp.stack(
@@ -951,35 +940,37 @@
     query_grad, key_value_grad, diagonals = attend_back(
         exps, inverse, queries, key_value, attended_grad
     )
-    query_grad, returned = lax.optimization_barrier((query_grad, returned))
 
     core = jnp.reshape(my_core, (1,)).astype(jnp.int32)
     side = model_width // 2
-    spare = -(4 * model_width + small.shape[0] + bucket_count) % (8 * lax.axis_size(CHIPS))
-    kept, given = weight_grads(
+    used = 4 * model_width + small.shape[0] + bucket_count
+    total = used + -used % (8 * lax.axis_size(CHIPS))
+    kept, given = key_value_weight_grads(core, key_value_grad, all_normed)
+    got = lax.ppermute(given, "core", SWAP)
+    query_grad, returned = lax.optimization_barrier((query_grad, returned))
+    kept_too, given_too = weight_grads(
         core,
         query_grad,
         normed_one,
-        key_value_grad,
-        all_normed,
         attended,
         branch_grad,
         small,
         bucket_hot,
         diagonals,
-        spare,
-    )
-    key_value_grad, kept, given, returned = lax.optimization_barrier(
-        (key_value_grad, kept, given, returned)
-    )
-    share = half_share(kept, given)
+        total - 2 * model_width,
+    )
+    key_value_grad, given_too, returned = lax.optimization_barrier(
+        (key_value_grad, given_too, returned)
+    )
+    got_too = lax.ppermute(given_too, "core", SWAP)
+    share = chip_share(((kept, got), (kept_too, got_too)))
     picked = jnp.dot(slot_table, returned, preferred_element_type=F32)
     mixture = gates[:, :1] * picked[:tok_rows] + gates[:, 1:2] * picked[tok_rows:]
     layer_out = (residual_one + mixture).astype(BF)[None]
 
-    far_grad = normed_grads(positions[blocks // 2 :], key_value_grad, w_qkv, half)
-    near_grad = normed_grads(positions[: blocks // 2], key_value_grad, w_qkv, half)
-    near_grad = near_grad.astype(F32) + lax.ppermute(far_grad, "core", SWAP).astype(F32)
+    all_grads = normed_grads(place, key_value_grad, w_qkv, half)
+    far_grad = lax.ppermute(all_grads[seq // 2 :], "core", SWAP)
+    near_grad = all_grads[: seq // 2].astype(F32) + far_grad.astype(F32)
     near_grad = near_grad.astype(BF).reshape(ctx_count // 2, tok_rows, model_width)
     query_part = contract_cols(query_grad, w_q)
     share, near_grad, query_part, layer_out, shares = lax.optimization_barrier(

time: 348 us -> 348 us (level)
  starting transfers between devices: 46.6 us -> 58 us
  waiting for transfers between devices: 96.5 us -> 85.2 us
    all_to_all x7 -> x8, starting transfers between devices: 40.5 us -> 51.2 us  [exchange(): return lax.all_to_all(array, axes, split_axis=0, concat_axis=0, tiled=True)]
    pallas_call x1, Pallas kernels: 13.6 us -> 5.16 us  [weight_grads(): pl.pallas_call(weight_grad_kernel, grid_spec=pltpu.PrefetchScalarGridSpec...]
    all_to_all x7 -> x8, waiting for transfers between devices: 91.5 us -> 83.4 us  [exchange(): return lax.all_to_all(array, axes, split_axis=0, concat_axis=0, tiled=True)]
    pallas_call x2, Pallas kernels: 14 us -> 19.9 us  [the longest x1 10.5 us: normed_grads(): pl.pallas_call(functools.partial(normed_grad_kernel, half=half), grid_spe...]
  transfers between devices with their start and end apart: 14 -> 16, of which waited for: 7 -> 7; matrix products, arithmetic and copies ran while one was open for 9% -> 10% of each run, Pallas kernels for 27% -> 26%
where the time goes in v4:
time: 348 us; the launch traced here: 346 us
  Pallas kernels  112 us (32%)
  waiting for transfers between devices  85.2 us (24%)
  starting transfers between devices  58 us (17%)
  blocking collectives  32.1 us (9%)
  other arithmetic  21.5 us (6%)
  between operations  15.4 us (4%)
  local copies, waits for them, and re-layouts  14.2 us (4%)
  matrix products  7.22 us (2%)
    all_to_all x8, waiting for transfers between devices, exchange(): return lax.all_to_all(array, axes, split_axis=0, concat_axis=0, tiled=True)  83.4 us
    all_to_all x8, starting transfers between devices, exchange(): return lax.all_to_all(array, axes, split_axis=0, concat_axis=0, tiled=True)  51.2 us
    all_to_all x1, blocking collectives, exchange(): return lax.all_to_all(array, axes, split_axis=0, concat_axis=0, tiled=True)  32.1 us
    pallas_call x1, Pallas kernels, run_experts(): pl.pallas_call(expert_kernel, grid=(experts, steps), in_specs=[row_spec(w...  20.5 us
    pallas_call x1, Pallas kernels, attend_back(): pl.pallas_call(attend_back_kernel, grid=(pairs,), in_specs=[pl.BlockSpec(...  13.3 us
    pallas_call x2, Pallas kernels, whole_grad(): pl.pallas_call(whole_grad_kernel, grid_spec=pltpu.PrefetchScalarGridSpec(...  11.9 us
    pallas_call x1, Pallas kernels, keys_and_values(): pl.pallas_call(functools.partial(key_value_kernel, half=half), grid_spec=...  11.1 us
    pallas_call x1, Pallas kernels, attend(): pl.pallas_call(attend_kernel, grid=(pairs,), in_specs=[pl.BlockSpec((rows...  10.8 us
  transfers between devices with their start and end apart: 16, of which 7 were waited for; matrix products, arithmetic and copies ran while one was open for 10% of the time, Pallas kernels for 26%

profile of v4, /device:TPU:1, one launch (start us, length us, event | category | flops | bytes accessed | tf_op | source)
XLA Modules:
  0.0 345.6 jit_solution(18059676474854547632)
XLA Ops:
  12.2 8.6 %all-to-all-start = ((bf16[8,128,768]{2,1,0:T(8,128)(2,1)}), bf16[8,128,768]{2,1,0:T(8,128)(2,1)S(1)}, u32[]{:S(2)}, u32[]{:S(2)}) async-start(bf16[8,128,768]{2,1,0:T(8,128)(2,1)} %broadcast_in_dim.88), calls=%async_computation | async-start | bytes 3145728 | tf_op jit(solution)/shard_map/all_to_all | solution.py:53
  30.0 11.3 %all-to-all-done = bf16[8,128,768]{2,1,0:T(8,128)(2,1)S(1)} async-done(((bf16[8,128,768]{2,1,0:T(8,128)(2,1)}), bf16[8,128,768]{2,1,0:T(8,128)(2,1)S(1)}, u32[]{:S(2)}, u32[]{:S(2)}) %all-to-all-start) | async-done | bytes 1572896 | tf_op jit(solution)/shard_map/all_to_all | solution.py:53
  42.6 6.1 %all-to-all-start.2 = ((bf16[32,32,768]{2,1,0:T(8,128)(2,1)}), bf16[32,32,768]{2,1,0:T(8,128)(2,1)S(1)}, u32[]{:S(2)}, u32[]{:S(2)}) async-start(bf16[32,32,768]{2,1,0:T(8,128)(2,1)} %bitcast.10), calls=%async_computation.2 | async-start | bytes 3145728 | tf_op jit(solution)/shard_map/all_to_all | solution.py:53
  50.7 11.1 %keys_and_values.1 = (bf16[2048,768]{1,0:T(8,128)(2,1)}, bf16[2,6,2048,128]{3,2,1,0:T(8,128)(2,1)}) custom-call(s32[32]{0:T(128)} %add_reduce_fusion.place_ref, bf16[1024,768]{1,0:T(8,128)(2,1)} %bitcast.66, bf16[1024,768]{1,0:T(8,128)(2,1)} %collective-permute-done.far_ref, f32[1,768]{1,0:T(1,128)} %broadcast_in_dim.97.gain_ref, ...), custom_call_target="tpu_custom_call" | custom-call | flops 4831838208 | bytes 12582912 | tf_op jit(solution)/shard_map/keys_and_values/pallas_call | solution.py:233
  61.7 10.8 %attend.1 = (bf16[128,768]{1,0:T(8,128)(2,1)}, bf16[12,128,2048]{2,1,0:T(8,128)(2,1)}, f32[6,256,128]{2,1,0:T(8,128)}) custom-call(bf16[128,768]{1,0:T(8,128)(2,1)} %convolution_convert_fusion.1.q_ref, bf16[2,6,2048,128]{3,2,1,0:T(8,128)(2,1)} %get-tuple-element.75.kv_ref, f32[6,4,2176]{2,1,0:T(4,128)} %reshape.203.window_ref), custom_call_target="tpu_custom_call" | custom-call | flops 1610612736 | bytes 12582912 | tf_op jit(solution)/shard_map/attend/pallas_call | solution.py:122
  76.7 32.1 %all_to_all.45 = bf16[32,32,896]{2,1,0:T(8,128)(2,1)} all-to-all(bf16[32,32,896]{2,1,0:T(8,128)(2,1)} %bitcast.64), channel_id=1, replica_groups=mesh['ya'=2,'z'=4,'core'=2,'yb'=2,'x'=4] {'ya','z','core','yb'}, dimensions={0} | all-to-all | bytes 3670016 | tf_op jit(solution)/shard_map/all_to_all | solution.py:53
  108.8 20.5 %experts.1 = (bf16[32,2,16,896]{3,2,1,0:T(8,128)(2,1)}, bf16[32,2,16,768]{3,2,1,0:T(8,128)(2,1)}, bf16[4,768,768]{2,1,0:T(8,128)(2,1)}, bf16[1,512,1536]{2,1,0:T(8,128)(2,1)}, bf16[1,512,1536]{2,1,0:T(8,128)(2,1)}) custom-call(bf16[32,2,16,896]{3,2,1,0:T(8,128)(2,1)} %bitcast.55, bf16[32,2,16,768]{3,2,1,0:T(8,128)(2,1)} %bitcast.61, ...), custom_call_target="tpu_custom_call" | custom-call | flops 12079595520 | bytes 15728640 | tf_op jit(solution)/shard_map/experts/pallas_call | solution.py:628
  129.4 5.3 %all-to-all-start.3 = ((bf16[32,32,896]{2,1,0:T(8,128)(2,1)}), bf16[32,32,896]{2,1,0:T(8,128)(2,1)S(1)}, u32[]{:S(2)}, u32[]{:S(2)}) async-start(bf16[32,32,896]{2,1,0:T(8,128)(2,1)} %bitcast.63), calls=%async_computation.3 | async-start | bytes 3670016 | tf_op jit(solution)/shard_map/all_to_all | solution.py:53
  135.5 6.9 %expert_grads.1 = bf16[4,768,768]{2,1,0:T(8,128)(2,1)} custom-call(bf16[32,2,16,896]{3,2,1,0:T(8,128)(2,1)} %bitcast.56, bf16[32,2,16,768]{3,2,1,0:T(8,128)(2,1)} %bitcast.62, bf16[1,512,1536]{2,1,0:T(8,128)(2,1)} %get-tuple-element.83.act_ref, bf16[1,512,1536]{2,1,0:T(8,128)(2,1)} %get-tuple-element.84.pre_grad_ref), custom_call_target="tpu_custom_call" | custom-call | flops 2415919104 | bytes 7864320 | tf_op jit(solution)/shard_map/expert_grads/pallas_call | solution.py:671
  142.4 16.4 %all-to-all-done.3 = bf16[32,32,896]{2,1,0:T(8,128)(2,1)S(1)} async-done(((bf16[32,32,896]{2,1,0:T(8,128)(2,1)}), bf16[32,32,896]{2,1,0:T(8,128)(2,1)S(1)}, u32[]{:S(2)}, u32[]{:S(2)}) %all-to-all-start.3) | async-done | bytes 1835040 | tf_op jit(solution)/shard_map/all_to_all | solution.py:53
  160.1 5.9 %all-to-all-start.4 = ((bf16[32,32,768]{2,1,0:T(8,128)(2,1)}), bf16[32,32,768]{2,1,0:T(8,128)(2,1)S(1)}, u32[]{:S(2)}, u32[]{:S(2)}) async-start(bf16[32,32,768]{2,1,0:T(8,128)(2,1)} %bitcast.15), calls=%async_computation.4 | async-start | bytes 3145728 | tf_op jit(solution)/shard_map/all_to_all | solution.py:53
  165.9 5.5 %out_of_experts.1 = (f32[128,768]{1,0:T(8,128)}, bf16[128,768]{1,0:T(8,128)(2,1)}, bf16[128,768]{1,0:T(8,128)(2,1)}, f32[40,768]{1,0:T(8,128)}) custom-call(bf16[1024,896]{1,0:T(8,128)(2,1)} %bitcast.54, bf16[256,1024]{1,0:T(8,128)(2,1)} %copy-done.3, f32[128,128]{1,0:T(8,128)} %get-tuple-element.88.gate_ref, s32[128,2]{1,0:T(8,128)} %bitcast.69, ...), custom_call_target="tpu_custom_call" | custom-call | tf_op jit(solution)/shard_map/out_of_experts/pallas_call | solution.py:795
  171.4 13.3 %attend_back.1 = (bf16[128,768]{1,0:T(8,128)(2,1)}, bf16[2,6,128,2048]{3,2,1,0:T(8,128)(2,1)}, f32[2,6,2,2176]{3,2,1,0:T(2,128)}) custom-call(bf16[12,128,2048]{2,1,0:T(8,128)(2,1)} %get-tuple-element.77.exps_ref, f32[6,256,128]{2,1,0:T(8,128)} %get-tuple-element.78.inverse_ref, bf16[128,768]{1,0:T(8,128)(2,1)} %convolution_convert_fusion.1.q_ref, ...), custom_call_target="tpu_custom_call" | custom-call | flops 3221225472 | bytes 18874368 | tf_op jit(solution)/shard_map/attend_back/pallas_call | solution.py:182
  184.7 9.4 %key_value_weight_grads.1 = (bf16[1536,384]{1,0:T(8,128)(2,1)}, bf16[1536,384]{1,0:T(8,128)(2,1)}) custom-call(s32[1]{0:T(128)} %bitcast.core_ref.side_ref, bf16[2,6,128,2048]{3,2,1,0:T(8,128)(2,1)} %get-tuple-element.107.dkv_ref, bf16[2048,768]{1,0:T(8,128)(2,1)} %get-tuple-element.93.all_normed_ref), custom_call_target="tpu_custom_call" | custom-call | flops 4831838208 | bytes 12582912 | tf_op jit(solution)/shard_map/key_value_weight_grads/pallas_call | solution.py:325
  194.5 5.2 %weight_grads.1 = (bf16[2048,384]{1,0:T(8,128)(2,1)}, bf16[2048,384]{1,0:T(8,128)(2,1)}) custom-call(s32[1]{0:T(128)} %bitcast.core_ref.side_ref, bf16[128,768]{1,0:T(8,128)(2,1)} %get-tuple-element.98.dq_ref, bf16[128,768]{1,0:T(8,128)(2,1)} %copy-done.20, bf16[128,768]{1,0:T(8,128)(2,1)} %get-tuple-element.79.attended_ref, ...), custom_call_target="tpu_custom_call" | custom-call | flops 301989888 | bytes 1572864 | tf_op jit(solution)/shard_map/weight_grads/pallas_call | solution.py:396
  205.5 6.6 %all-to-all-start.5 = ((bf16[16,224,384]{2,1,0:T(8,128)(2,1)}), bf16[16,224,384]{2,1,0:T(8,128)(2,1)S(1)}, u32[]{:S(2)}, u32[]{:S(2)}) async-start(bf16[16,224,384]{2,1,0:T(8,128)(2,1)} %bitcast.53), calls=%async_computation.5 | async-start | bytes 5505024 | tf_op jit(solution)/shard_map/all_to_all | solution.py:53
  212.2 10.5 %normed_grads.1 = bf16[2048,768]{1,0:T(8,128)(2,1)} custom-call(s32[32]{0:T(128)} %add_reduce_fusion.place_ref, bf16[2,6,128,2048]{3,2,1,0:T(8,128)(2,1)} %get-tuple-element.107.dkv_ref, bf16[768,2304]{1,0:T(8,128)(2,1)} %weight_ref.3, bf16[768,2304]{1,0:T(8,128)(2,1)} %weight_ref.3), custom_call_target="tpu_custom_call" | custom-call | flops 4831838208 | bytes 12582912 | tf_op jit(solution)/shard_map/normed_grads/pallas_call | solution.py:279
  229.6 20.9 %all-to-all-done.5 = bf16[16,224,384]{2,1,0:T(8,128)(2,1)S(1)} async-done(((bf16[16,224,384]{2,1,0:T(8,128)(2,1)}), bf16[16,224,384]{2,1,0:T(8,128)(2,1)S(1)}, u32[]{:S(2)}, u32[]{:S(2)}) %all-to-all-start.5) | async-done | bytes 2752544 | tf_op jit(solution)/shard_map/all_to_all | solution.py:53
  251.6 4.3 %all-to-all-start.6 = ((bf16[4,56,384]{2,1,0:T(8,128)(2,1)}), bf16[4,56,384]{2,1,0:T(8,128)(2,1)S(1)}, u32[]{:S(2)}, u32[]{:S(2)}) async-start(bf16[4,56,384]{2,1,0:T(8,128)(2,1)} %bitcast.18), calls=%async_computation.6 | async-start | bytes 344064 | tf_op jit(solution)/shard_map/all_to_all | solution.py:53
  262.7 10.2 %all-to-all-start.7 = ((bf16[64,56,384]{2,1,0:T(8,128)(2,1)}), bf16[64,56,384]{2,1,0:T(8,128)(2,1)S(1)}, u32[]{:S(2)}, u32[]{:S(2)}) async-start(bf16[64,56,384]{2,1,0:T(8,128)(2,1)} %broadcast_in_dim.100), calls=%async_computation.9 | async-start | bytes 5505024 | tf_op jit(solution)/shard_map/all_to_all | solution.py:53
  278.0 29.3 %all-to-all-done.7 = bf16[64,56,384]{2,1,0:T(8,128)(2,1)S(1)} async-done(((bf16[64,56,384]{2,1,0:T(8,128)(2,1)}), bf16[64,56,384]{2,1,0:T(8,128)(2,1)S(1)}, u32[]{:S(2)}, u32[]{:S(2)}) %all-to-all-start.7) | async-done | bytes 2752544 | tf_op jit(solution)/shard_map/all_to_all | solution.py:53
  311.6 4.3 %all-to-all-start.8 = ((bf16[8,128,768]{2,1,0:T(8,128)(2,1)}), bf16[8,128,768]{2,1,0:T(8,128)(2,1)}, u32[]{:S(2)}, u32[]{:S(2)}) async-start(bf16[8,128,768]{2,1,0:T(8,128)(2,1)} %bitcast.60), calls=%async_computation.10 | async-start | bytes 3145728 | tf_op jit(solution)/shard_map/all_to_all | solution.py:53
  315.9 5.9 %whole_grad.2 = (f32[768,2304]{1,0:T(8,128)}, f32[768,128]{1,0:T(8,128)}, f32[768,768]{1,0:T(8,128)}) custom-call(s32[1]{0:T(128)} %bitcast.core_ref.side_ref, bf16[3584,384]{1,0:T(8,128)(2,1)} %bitcast.51, bf16[768,2304]{1,0:T(8,128)(2,1)} %weight_ref.3), custom_call_target="tpu_custom_call" | custom-call | flops 1769472 | bytes 7077888 | tf_op jit(solution)/shard_map/whole_grad/pallas_call | solution.py:455
  321.9 5.9 %whole_grad.3 = (f32[768,2304]{1,0:T(8,128)}, f32[768,128]{1,0:T(8,128)}, f32[768,768]{1,0:T(8,128)}) custom-call(s32[1]{0:T(128)S(6)} %sub.42.side_ref, bf16[3584,384]{1,0:T(8,128)(2,1)} %collective-permute-done.4.half_ref, bf16[768,2304]{1,0:T(8,128)(2,1)} %weight_ref.3, ...), custom_call_target="tpu_custom_call", output_to_operand_aliasing={{0}: (3, {}), {1}: (4, {}), {2}: (5, {})} | custom-call | flops 1769472 | bytes 7077888 | tf_op jit(solution)/shard_map/whole_grad/pallas_call | solution.py:455
  (138 shorter events, 64.0 us)
Async XLA Ops:
  7.2 16.4 %copy-start = (f32[32,12]{0,1:T(8,128)S(1)}, f32[32,12]{0,1:T(8,128)}, u32[]{:S(2)}) copy-start(f32[32,12]{0,1:T(8,128)} %param.16) | copy-start | bytes 4612
  7.2 101.6 %all-gather.3.cloned.1.call-start = ((), (), s32[]{:S(2)}) async-start(), calls=%async_computation.13 | async-start | bytes 11796480 | tf_op jit(solution)/shard_map/all_gather | solution.py:842
  12.2 8.7 %copy-start.27 = (s32[16]{0:T(128)S(1)}, s32[16]{0:T(128)}, u32[]{:S(2)}) copy-start(s32[16]{0:T(128)} %param.23) | copy-start | bytes 196
  12.2 10.6 %copy-start.25 = (s32[2048]{0:T(1024)S(1)}, s32[2048]{0:T(1024)}, u32[]{:S(2)}) copy-start(s32[2048]{0:T(1024)} %param.24) | copy-start | bytes 24580
  12.2 10.8 %copy-start.28 = (s32[1,128,2]{1,2,0:T(2,128)S(1)}, s32[1,128,2]{1,2,0:T(2,128)}, u32[]{:S(2)}) copy-start(s32[1,128,2]{1,2,0:T(2,128)} %param.22) | copy-start | bytes 3076
  12.2 13.1 %copy-start.23 = (f32[768]{0:T(1024)S(1)}, f32[768]{0:T(1024)}, u32[]{:S(2)}) copy-start(f32[768]{0:T(1024)} %param.14) | copy-start | bytes 9220
  12.2 29.1 %all-to-all-start = ((bf16[8,128,768]{2,1,0:T(8,128)(2,1)}), bf16[8,128,768]{2,1,0:T(8,128)(2,1)S(1)}, u32[]{:S(2)}, u32[]{:S(2)}) async-start(bf16[8,128,768]{2,1,0:T(8,128)(2,1)} %broadcast_in_dim.88), calls=%async_computation | async-start | bytes 3145728 | tf_op jit(solution)/shard_map/all_to_all | solution.py:53
  41.3 9.4 %collective-permute-start = (bf16[1024,768]{1,0:T(8,128)(2,1)S(1)}, bf16[1024,768]{1,0:T(8,128)(2,1)}, u32[]{:S(2)}, u32[]{:S(2)}) collective-permute-start(bf16[1024,768]{1,0:T(8,128)(2,1)S(1)} %bitcast.65), channel_id=1, source_target_pairs={{0,8},{8,0},{1,9},{9,1},{2,10},{10,2},{3,11},{11,3},{4,12},{12,4},... | collective-permute-start | bytes 4718600 | tf_op jit(solution)/shard_map/ppermute | solution.py:902
  42.6 7.3 %copy-start.24 = (bf16[768,32]{0,1:T(8,128)(2,1)S(1)}, bf16[768,32]{0,1:T(8,128)(2,1)}, u32[]{:S(2)}) copy-start(bf16[768,32]{0,1:T(8,128)(2,1)} %param.19) | copy-start | bytes 147460
  42.6 34.1 %all-to-all-start.2 = ((bf16[32,32,768]{2,1,0:T(8,128)(2,1)}), bf16[32,32,768]{2,1,0:T(8,128)(2,1)S(1)}, u32[]{:S(2)}, u32[]{:S(2)}) async-start(bf16[32,32,768]{2,1,0:T(8,128)(2,1)} %bitcast.10), calls=%async_computation.2 | async-start | bytes 3145728 | tf_op jit(solution)/shard_map/all_to_all | solution.py:53
  48.6 212.3 %reduce-scatter.3.cloned.1.call-start = ((), (), s32[]{:S(2)}) async-start(), calls=%async_computation.11 | async-start | bytes 5898240 | tf_op jit(solution)/shard_map/reduce_scatter | solution.py:923
  76.7 32.1 %copy-start.10 = (bf16[32,32,768]{2,1,0:T(8,128)(2,1)}, bf16[32,32,768]{2,1,0:T(8,128)(2,1)S(1)}, u32[]{:S(2)}) copy-start(bf16[32,32,768]{2,1,0:T(8,128)(2,1)S(1)} %all-to-all-done.2) | copy-start | bytes 4718596
  129.4 29.5 %all-to-all-start.3 = ((bf16[32,32,896]{2,1,0:T(8,128)(2,1)}), bf16[32,32,896]{2,1,0:T(8,128)(2,1)S(1)}, u32[]{:S(2)}, u32[]{:S(2)}) async-start(bf16[32,32,896]{2,1,0:T(8,128)(2,1)} %bitcast.63), calls=%async_computation.3 | async-start | bytes 3670016 | tf_op jit(solution)/shard_map/all_to_all | solution.py:53
  134.6 126.3 %reduce-scatter.5.cloned.1.call-start = ((), (), s32[]{:S(2)}) async-start(), calls=%async_computation.12 | async-start | bytes 5898240 | tf_op jit(solution)/shard_map/reduce_scatter | solution.py:923
  160.1 34.4 %all-to-all-start.4 = ((bf16[32,32,768]{2,1,0:T(8,128)(2,1)}), bf16[32,32,768]{2,1,0:T(8,128)(2,1)S(1)}, u32[]{:S(2)}, u32[]{:S(2)}) async-start(bf16[32,32,768]{2,1,0:T(8,128)(2,1)} %bitcast.15), calls=%async_computation.4 | async-start | bytes 3145728 | tf_op jit(solution)/shard_map/all_to_all | solution.py:53
  194.1 5.8 %collective-permute-start.1 = (bf16[1536,384]{1,0:T(8,128)(2,1)}, bf16[1536,384]{1,0:T(8,128)(2,1)}, u32[]{:S(2)}, u32[]{:S(2)}) collective-permute-start(bf16[1536,384]{1,0:T(8,128)(2,1)} %get-tuple-element.95), channel_id=1, source_target_pairs={{0,8},{8,0},{1,9},{9,1},{2,10},{10,2},{3,11},{11,3},{4,12},{12,4},... | collective-permute-start | bytes 3538952 | tf_op jit(solution)/shard_map/ppermute | solution.py:949
  199.6 3.6 %collective-permute-start.2 = (bf16[2048,384]{1,0:T(8,128)(2,1)}, bf16[2048,384]{1,0:T(8,128)(2,1)S(1)}, u32[]{:S(2)}, u32[]{:S(2)}) collective-permute-start(bf16[2048,384]{1,0:T(8,128)(2,1)} %get-tuple-element.106), channel_id=1, source_target_pairs={{0,8},{8,0},{1,9},{9,1},{2,10},{10,2},{3,11},{11,3},{4,12},{12,4},... | collective-permute-start | bytes 4718600 | tf_op jit(solution)/shard_map/ppermute | solution.py:965
  205.5 45.0 %all-to-all-start.5 = ((bf16[16,224,384]{2,1,0:T(8,128)(2,1)}), bf16[16,224,384]{2,1,0:T(8,128)(2,1)S(1)}, u32[]{:S(2)}, u32[]{:S(2)}) async-start(bf16[16,224,384]{2,1,0:T(8,128)(2,1)} %bitcast.53), calls=%async_computation.5 | async-start | bytes 5505024 | tf_op jit(solution)/shard_map/all_to_all | solution.py:53
  225.5 30.3 %collective-permute-start.3 = (bf16[1024,768]{1,0:T(8,128)(2,1)}, bf16[1024,768]{1,0:T(8,128)(2,1)}, u32[]{:S(2)}, u32[]{:S(2)}) collective-permute-start(bf16[1024,768]{1,0:T(8,128)(2,1)} %slice.77), channel_id=1, source_target_pairs={{0,8},{8,0},{1,9},{9,1},{2,10},{10,2},{3,11},{11,3},{4,12},{12,4},... | collective-permute-start | bytes 4718600 | tf_op jit(solution)/shard_map/ppermute | solution.py:972
  251.6 9.3 %all-to-all-start.6 = ((bf16[4,56,384]{2,1,0:T(8,128)(2,1)}), bf16[4,56,384]{2,1,0:T(8,128)(2,1)S(1)}, u32[]{:S(2)}, u32[]{:S(2)}) async-start(bf16[4,56,384]{2,1,0:T(8,128)(2,1)} %bitcast.18), calls=%async_computation.6 | async-start | bytes 344064 | tf_op jit(solution)/shard_map/all_to_all | solution.py:53
  262.7 44.6 %all-to-all-start.7 = ((bf16[64,56,384]{2,1,0:T(8,128)(2,1)}), bf16[64,56,384]{2,1,0:T(8,128)(2,1)S(1)}, u32[]{:S(2)}, u32[]{:S(2)}) async-start(bf16[64,56,384]{2,1,0:T(8,128)(2,1)} %broadcast_in_dim.100), calls=%async_computation.9 | async-start | bytes 5505024 | tf_op jit(solution)/shard_map/all_to_all | solution.py:53
  307.4 14.5 %collective-permute-start.4 = (bf16[3584,384]{1,0:T(8,128)(2,1)S(1)}, bf16[3584,384]{1,0:T(8,128)(2,1)}, u32[]{:S(2)}, u32[]{:S(2)}) collective-permute-start(bf16[3584,384]{1,0:T(8,128)(2,1)S(1)} %bitcast.50), channel_id=1, source_target_pairs={{0,8},{8,0},{1,9},{9,1},{2,10},{10,2},{3,11},{11,3},{4,12},{12,4},... | collective-permute-start | bytes 8257544 | tf_op jit(solution)/shard_map/ppermute | solution.py:987
  311.6 24.0 %all-to-all-start.8 = ((bf16[8,128,768]{2,1,0:T(8,128)(2,1)}), bf16[8,128,768]{2,1,0:T(8,128)(2,1)}, u32[]{:S(2)}, u32[]{:S(2)}) async-start(bf16[8,128,768]{2,1,0:T(8,128)(2,1)} %bitcast.60), calls=%async_computation.10 | async-start | bytes 3145728 | tf_op jit(solution)/shard_map/all_to_all | solution.py:53
  329.0 8.3 %copy-start.7 = (bf16[1,128,768]{2,1,0:T(8,128)(2,1)S(1)}, bf16[1,128,768]{2,1,0:T(8,128)(2,1)}, u32[]{:S(2)}) copy-start(bf16[1,128,768]{2,1,0:T(8,128)(2,1)} %param.13) | copy-start | bytes 589828
  (21 other events, 76.7 us)
Sparse Core Ops, SparseCore 0:
  10.3 95.1 all-gather.2
  129.5 49.4 reduce-scatter.2
  181.4 50.8 reduce-scatter.4

commit v5 on v4

--- a/solution.py
+++ b/solution.py
@@ -549,7 +549,6 @@
     weight_ref,
     dx_ref,
     ret_ref,
-    first_grad_ref,
     act_ref,
     pre_grad_ref,
     ret_sum,
@@ -568,14 +567,8 @@
     returned = jnp.dot(activated, weight_out, preferred_element_type=F32)
     input_grad = contract_cols(pre_grad, weight_in)
 
-    @pl.when(pl.program_id(0) == 0)
-    def _():
-        write_weight_grads(x, slot_grad, activated, pre_grad, first_grad_ref)
-
-    @pl.when(pl.program_id(0) > 0)
-    def _():
-        act_ref[...] = activated
-        pre_grad_ref[...] = pre_grad
+    act_ref[...] = activated
+    pre_grad_ref[...] = pre_grad
 
     @pl.when(part == 0)
     def _():
@@ -616,16 +609,12 @@
     def row_spec(columns):
         return pl.BlockSpec((devices, None, slots, columns), lambda e, w: (0, e, 0, 0))
 
-    later = experts - 1
-    hidden_spec = pl.BlockSpec(
-        (None, rows, slices * hidden),
-        lambda e, w: (jnp.maximum(e - 1, 0), 0, jnp.where(e == 0, 0, w)),
-    )
-    hidden_shape = jax.ShapeDtypeStruct((later, rows, parts * hidden), BF)
+    hidden_spec = pl.BlockSpec((None, rows, slices * hidden), lambda e, w: (e, 0, w))
+    hidden_shape = jax.ShapeDtypeStruct((experts, rows, parts * hidden), BF)
     grad_shape = jax.ShapeDtypeStruct((parts, both, width), BF)
     work = experts * rows * width * parts * hidden
     params = pltpu.CompilerParams(vmem_limit_bytes=VMEM_LIMIT)
-    input_grad, returned, first_grad, activated, pre_grad = pl.pallas_call(
+    input_grad, returned, activated, pre_grad = pl.pallas_call(
         expert_kernel,
         grid=(experts, steps),
         in_specs=[
@@ -636,36 +625,32 @@
         out_specs=[
             row_spec(width + LANES),
             row_spec(width),
-            pl.BlockSpec(
-                (slices, both, width), lambda e, w: (jnp.where(e == 0, w, steps - 1), 0, 0)
-            ),
             hidden_spec,
             hidden_spec,
         ],
         out_shape=[
             jax.ShapeDtypeStruct((devices, experts, slots, width + LANES), BF),
             jax.ShapeDtypeStruct((devices, experts, slots, width), BF),
-            grad_shape,
             hidden_shape,
             hidden_shape,
         ],
         scratch_shapes=[pltpu.VMEM((rows, width), F32), pltpu.VMEM((rows, width), F32)],
         compiler_params=params,
         cost_estimate=pl.CostEstimate(
-            flops=10 * work,
+            flops=8 * work,
             bytes_accessed=8 * experts * rows * width + 4 * parts * experts * width * hidden,
             transcendentals=2 * experts * rows * parts * hidden,
         ),
         name="experts",
     )(x_rows, cot_rows, weights)
-    weight_grads_of = [first_grad]
-    for expert in range(1, experts):
+    weight_grads_of = []
+    for expert in range(experts):
 
         def own_rows(columns, expert=expert):
             return pl.BlockSpec((devices, None, slots, columns), lambda w: (0, expert, 0, 0))
 
         own_hidden = pl.BlockSpec(
-            (None, rows, slices * hidden), lambda w, expert=expert: (expert - 1, 0, w)
+            (None, rows, slices * hidden), lambda w, expert=expert: (expert, 0, w)
         )
         weight_grads_of.append(
             pl.pallas_call(
@@ -916,11 +901,11 @@
         return rows.reshape(expert_devices * device_slots, rows.shape[2])
 
     input_grad = from_experts(input_grad)
-    later_parts, input_grad, returned, bucket_hot = lax.optimization_barrier(
-        (parts[1:], input_grad, returned, bucket_hot)
+    parts, input_grad, returned, bucket_hot = lax.optimization_barrier(
+        (parts, input_grad, returned, bucket_hot)
     )
     shares = [
-        lax.psum_scatter(part, "x", scatter_dimension=0) for part in (parts[0], *later_parts)
+        lax.psum_scatter(part, "x", scatter_dimension=0) for part in parts
     ]
     returned = from_experts(returned)
 

time: 348 us -> 346 us (level)
  waiting for transfers between devices: 85.2 us -> 80.1 us
    all_to_all x8, waiting for transfers between devices: 83.4 us -> 77.7 us  [exchange(): return lax.all_to_all(array, axes, split_axis=0, concat_axis=0, tiled=True)]
    pallas_call x1 -> x2, Pallas kernels: 6.9 us -> 12.5 us  [run_experts(): pl.pallas_call(expert_grad_kernel, grid=(steps,), in_specs=[own_rows(wide...]
    pallas_call x1, Pallas kernels: 20.5 us -> 16.5 us  [run_experts(): pl.pallas_call(expert_kernel, grid=(experts, steps), in_specs=[row_spec(w...]
  transfers between devices with their start and end apart: 16 -> 16, of which waited for: 7 -> 7; matrix products, arithmetic and copies ran while one was open for 10% -> 10% of each run, Pallas kernels for 26% -> 28%
where the time goes in v5:
time: 346 us; the launch traced here: 343 us
  Pallas kernels  114 us (33%)
  waiting for transfers between devices  80.1 us (23%)
  starting transfers between devices  58.4 us (17%)
  blocking collectives  32.1 us (9%)
  other arithmetic  21.4 us (6%)
  between operations  15.4 us (4%)
  local copies, waits for them, and re-layouts  14.2 us (4%)
  matrix products  7.21 us (2%)
    all_to_all x8, waiting for transfers between devices, exchange(): return lax.all_to_all(array, axes, split_axis=0, concat_axis=0, tiled=True)  77.7 us
    all_to_all x8, starting transfers between devices, exchange(): return lax.all_to_all(array, axes, split_axis=0, concat_axis=0, tiled=True)  51.3 us
    all_to_all x1, blocking collectives, exchange(): return lax.all_to_all(array, axes, split_axis=0, concat_axis=0, tiled=True)  32.1 us
    pallas_call x1, Pallas kernels, run_experts(): pl.pallas_call(expert_kernel, grid=(experts, steps), in_specs=[row_spec(w...  16.5 us
    pallas_call x1, Pallas kernels, attend_back(): pl.pallas_call(attend_back_kernel, grid=(pairs,), in_specs=[pl.BlockSpec(...  13.2 us
    pallas_call x2, Pallas kernels, run_experts(): pl.pallas_call(expert_grad_kernel, grid=(steps,), in_specs=[own_rows(wide...  12.5 us
    pallas_call x2, Pallas kernels, whole_grad(): pl.pallas_call(whole_grad_kernel, grid_spec=pltpu.PrefetchScalarGridSpec(...  11.9 us
    pallas_call x1, Pallas kernels, keys_and_values(): pl.pallas_call(functools.partial(key_value_kernel, half=half), grid_spec=...  11.1 us
  transfers between devices with their start and end apart: 16, of which 7 were waited for; matrix products, arithmetic and copies ran while one was open for 10% of the time, Pallas kernels for 28%

profile of v5, /device:TPU:1, one launch (start us, length us, event | category | flops | bytes accessed | tf_op | source)
XLA Modules:
  0.0 343.5 jit_solution(3480442672576273605)
XLA Ops:
  12.2 8.6 %all-to-all-start = ((bf16[8,128,768]{2,1,0:T(8,128)(2,1)}), bf16[8,128,768]{2,1,0:T(8,128)(2,1)S(1)}, u32[]{:S(2)}, u32[]{:S(2)}) async-start(bf16[8,128,768]{2,1,0:T(8,128)(2,1)} %broadcast_in_dim.88), calls=%async_computation | async-start | bytes 3145728 | tf_op jit(solution)/shard_map/all_to_all | solution.py:53
  30.0 11.3 %all-to-all-done = bf16[8,128,768]{2,1,0:T(8,128)(2,1)S(1)} async-done(((bf16[8,128,768]{2,1,0:T(8,128)(2,1)}), bf16[8,128,768]{2,1,0:T(8,128)(2,1)S(1)}, u32[]{:S(2)}, u32[]{:S(2)}) %all-to-all-start) | async-done | bytes 1572896 | tf_op jit(solution)/shard_map/all_to_all | solution.py:53
  42.6 6.1 %all-to-all-start.2 = ((bf16[32,32,768]{2,1,0:T(8,128)(2,1)}), bf16[32,32,768]{2,1,0:T(8,128)(2,1)S(1)}, u32[]{:S(2)}, u32[]{:S(2)}) async-start(bf16[32,32,768]{2,1,0:T(8,128)(2,1)} %bitcast.10), calls=%async_computation.2 | async-start | bytes 3145728 | tf_op jit(solution)/shard_map/all_to_all | solution.py:53
  50.6 11.1 %keys_and_values.1 = (bf16[2048,768]{1,0:T(8,128)(2,1)}, bf16[2,6,2048,128]{3,2,1,0:T(8,128)(2,1)}) custom-call(s32[32]{0:T(128)} %add_reduce_fusion.place_ref, bf16[1024,768]{1,0:T(8,128)(2,1)} %bitcast.68, bf16[1024,768]{1,0:T(8,128)(2,1)} %collective-permute-done.far_ref, f32[1,768]{1,0:T(1,128)} %broadcast_in_dim.97.gain_ref, ...), custom_call_target="tpu_custom_call" | custom-call | flops 4831838208 | bytes 12582912 | tf_op jit(solution)/shard_map/keys_and_values/pallas_call | solution.py:233
  61.7 10.9 %attend.1 = (bf16[128,768]{1,0:T(8,128)(2,1)}, bf16[12,128,2048]{2,1,0:T(8,128)(2,1)}, f32[6,256,128]{2,1,0:T(8,128)}) custom-call(bf16[128,768]{1,0:T(8,128)(2,1)} %convolution_convert_fusion.1.q_ref, bf16[2,6,2048,128]{3,2,1,0:T(8,128)(2,1)} %get-tuple-element.75.kv_ref, f32[6,4,2176]{2,1,0:T(4,128)} %reshape.203.window_ref), custom_call_target="tpu_custom_call" | custom-call | flops 1610612736 | bytes 12582912 | tf_op jit(solution)/shard_map/attend/pallas_call | solution.py:122
  76.7 32.1 %all_to_all.45 = bf16[32,32,896]{2,1,0:T(8,128)(2,1)} all-to-all(bf16[32,32,896]{2,1,0:T(8,128)(2,1)} %bitcast.66), channel_id=1, replica_groups=mesh['ya'=2,'z'=4,'core'=2,'yb'=2,'x'=4] {'ya','z','core','yb'}, dimensions={0} | all-to-all | bytes 3670016 | tf_op jit(solution)/shard_map/all_to_all | solution.py:53
  108.8 16.5 %experts.1 = (bf16[32,2,16,896]{3,2,1,0:T(8,128)(2,1)}, bf16[32,2,16,768]{3,2,1,0:T(8,128)(2,1)}, bf16[2,512,1536]{2,1,0:T(8,128)(2,1)}, bf16[2,512,1536]{2,1,0:T(8,128)(2,1)}) custom-call(bf16[32,2,16,896]{3,2,1,0:T(8,128)(2,1)} %bitcast.50, bf16[32,2,16,768]{3,2,1,0:T(8,128)(2,1)} %bitcast.53, bf16[4,2,768,768]{3,2,1,0:T(8,128)(2,1)} %bitcast.74), custom_call_target="tpu_custom_call" | custom-call | flops 9663676416 | bytes 15728640 | tf_op jit(solution)/shard_map/experts/pallas_call | solution.py:617
  125.3 5.3 %all-to-all-start.3 = ((bf16[32,32,896]{2,1,0:T(8,128)(2,1)}), bf16[32,32,896]{2,1,0:T(8,128)(2,1)S(1)}, u32[]{:S(2)}, u32[]{:S(2)}) async-start(bf16[32,32,896]{2,1,0:T(8,128)(2,1)} %bitcast.65), calls=%async_computation.3 | async-start | bytes 3670016 | tf_op jit(solution)/shard_map/all_to_all | solution.py:53
  131.7 6.2 %expert_grads.2 = bf16[4,768,768]{2,1,0:T(8,128)(2,1)} custom-call(bf16[32,2,16,896]{3,2,1,0:T(8,128)(2,1)} %bitcast.51, bf16[32,2,16,768]{3,2,1,0:T(8,128)(2,1)} %bitcast.54, bf16[2,512,1536]{2,1,0:T(8,128)(2,1)} %get-tuple-element.83.act_ref, bf16[2,512,1536]{2,1,0:T(8,128)(2,1)} %get-tuple-element.84.pre_grad_ref), custom_call_target="tpu_custom_call" | custom-call | flops 2415919104 | bytes 7864320 | tf_op jit(solution)/shard_map/expert_grads/pallas_call | solution.py:656
  137.9 6.2 %expert_grads.3 = bf16[4,768,768]{2,1,0:T(8,128)(2,1)} custom-call(bf16[32,2,16,896]{3,2,1,0:T(8,128)(2,1)} %bitcast.52, bf16[32,2,16,768]{3,2,1,0:T(8,128)(2,1)} %bitcast.55, bf16[2,512,1536]{2,1,0:T(8,128)(2,1)} %get-tuple-element.83.act_ref, bf16[2,512,1536]{2,1,0:T(8,128)(2,1)} %get-tuple-element.84.pre_grad_ref), custom_call_target="tpu_custom_call" | custom-call | flops 2415919104 | bytes 7864320 | tf_op jit(solution)/shard_map/expert_grads/pallas_call | solution.py:656
  144.1 10.6 %all-to-all-done.3 = bf16[32,32,896]{2,1,0:T(8,128)(2,1)S(1)} async-done(((bf16[32,32,896]{2,1,0:T(8,128)(2,1)}), bf16[32,32,896]{2,1,0:T(8,128)(2,1)S(1)}, u32[]{:S(2)}, u32[]{:S(2)}) %all-to-all-start.3) | async-done | bytes 1835040 | tf_op jit(solution)/shard_map/all_to_all | solution.py:53
  156.7 5.9 %all-to-all-start.4 = ((bf16[32,32,768]{2,1,0:T(8,128)(2,1)}), bf16[32,32,768]{2,1,0:T(8,128)(2,1)S(1)}, u32[]{:S(2)}, u32[]{:S(2)}) async-start(bf16[32,32,768]{2,1,0:T(8,128)(2,1)} %bitcast.15), calls=%async_computation.4 | async-start | bytes 3145728 | tf_op jit(solution)/shard_map/all_to_all | solution.py:53
  162.6 6.2 %out_of_experts.1 = (f32[128,768]{1,0:T(8,128)}, bf16[128,768]{1,0:T(8,128)(2,1)}, bf16[128,768]{1,0:T(8,128)(2,1)}, f32[40,768]{1,0:T(8,128)}) custom-call(bf16[1024,896]{1,0:T(8,128)(2,1)} %bitcast.60, bf16[256,1024]{1,0:T(8,128)(2,1)} %copy-done.4, f32[128,128]{1,0:T(8,128)} %get-tuple-element.88.gate_ref, s32[128,2]{1,0:T(8,128)} %bitcast.71, ...), custom_call_target="tpu_custom_call" | custom-call | tf_op jit(solution)/shard_map/out_of_experts/pallas_call | solution.py:780
  168.8 13.2 %attend_back.1 = (bf16[128,768]{1,0:T(8,128)(2,1)}, bf16[2,6,128,2048]{3,2,1,0:T(8,128)(2,1)}, f32[2,6,2,2176]{3,2,1,0:T(2,128)}) custom-call(bf16[12,128,2048]{2,1,0:T(8,128)(2,1)} %get-tuple-element.77.exps_ref, f32[6,256,128]{2,1,0:T(8,128)} %get-tuple-element.78.inverse_ref, bf16[128,768]{1,0:T(8,128)(2,1)} %convolution_convert_fusion.1.q_ref, ...), custom_call_target="tpu_custom_call" | custom-call | flops 3221225472 | bytes 18874368 | tf_op jit(solution)/shard_map/attend_back/pallas_call | solution.py:182
  182.0 9.5 %key_value_weight_grads.1 = (bf16[1536,384]{1,0:T(8,128)(2,1)}, bf16[1536,384]{1,0:T(8,128)(2,1)}) custom-call(s32[1]{0:T(128)} %bitcast.core_ref.side_ref, bf16[2,6,128,2048]{3,2,1,0:T(8,128)(2,1)} %get-tuple-element.107.dkv_ref, bf16[2048,768]{1,0:T(8,128)(2,1)} %get-tuple-element.93.all_normed_ref), custom_call_target="tpu_custom_call" | custom-call | flops 4831838208 | bytes 12582912 | tf_op jit(solution)/shard_map/key_value_weight_grads/pallas_call | solution.py:325
  191.9 5.2 %weight_grads.1 = (bf16[2048,384]{1,0:T(8,128)(2,1)}, bf16[2048,384]{1,0:T(8,128)(2,1)}) custom-call(s32[1]{0:T(128)} %bitcast.core_ref.side_ref, bf16[128,768]{1,0:T(8,128)(2,1)} %get-tuple-element.98.dq_ref, bf16[128,768]{1,0:T(8,128)(2,1)} %copy-done.20, bf16[128,768]{1,0:T(8,128)(2,1)} %get-tuple-element.79.attended_ref, ...), custom_call_target="tpu_custom_call" | custom-call | flops 301989888 | bytes 1572864 | tf_op jit(solution)/shard_map/weight_grads/pallas_call | solution.py:396
  202.9 6.8 %all-to-all-start.5 = ((bf16[16,224,384]{2,1,0:T(8,128)(2,1)}), bf16[16,224,384]{2,1,0:T(8,128)(2,1)S(1)}, u32[]{:S(2)}, u32[]{:S(2)}) async-start(bf16[16,224,384]{2,1,0:T(8,128)(2,1)} %bitcast.59), calls=%async_computation.5 | async-start | bytes 5505024 | tf_op jit(solution)/shard_map/all_to_all | solution.py:53
  209.7 10.7 %normed_grads.1 = bf16[2048,768]{1,0:T(8,128)(2,1)} custom-call(s32[32]{0:T(128)} %add_reduce_fusion.place_ref, bf16[2,6,128,2048]{3,2,1,0:T(8,128)(2,1)} %get-tuple-element.107.dkv_ref, bf16[768,2304]{1,0:T(8,128)(2,1)} %weight_ref.3, bf16[768,2304]{1,0:T(8,128)(2,1)} %weight_ref.3), custom_call_target="tpu_custom_call" | custom-call | flops 4831838208 | bytes 12582912 | tf_op jit(solution)/shard_map/normed_grads/pallas_call | solution.py:279
  227.2 21.1 %all-to-all-done.5 = bf16[16,224,384]{2,1,0:T(8,128)(2,1)S(1)} async-done(((bf16[16,224,384]{2,1,0:T(8,128)(2,1)}), bf16[16,224,384]{2,1,0:T(8,128)(2,1)S(1)}, u32[]{:S(2)}, u32[]{:S(2)}) %all-to-all-start.5) | async-done | bytes 2752544 | tf_op jit(solution)/shard_map/all_to_all | solution.py:53
  249.5 4.8 %all-to-all-start.6 = ((bf16[4,56,384]{2,1,0:T(8,128)(2,1)}), bf16[4,56,384]{2,1,0:T(8,128)(2,1)S(1)}, u32[]{:S(2)}, u32[]{:S(2)}) async-start(bf16[4,56,384]{2,1,0:T(8,128)(2,1)} %bitcast.18), calls=%async_computation.6 | async-start | bytes 344064 | tf_op jit(solution)/shard_map/all_to_all | solution.py:53
  261.2 9.5 %all-to-all-start.7 = ((bf16[64,56,384]{2,1,0:T(8,128)(2,1)}), bf16[64,56,384]{2,1,0:T(8,128)(2,1)S(1)}, u32[]{:S(2)}, u32[]{:S(2)}) async-start(bf16[64,56,384]{2,1,0:T(8,128)(2,1)} %broadcast_in_dim.100), calls=%async_computation.9 | async-start | bytes 5505024 | tf_op jit(solution)/shard_map/all_to_all | solution.py:53
  275.9 29.1 %all-to-all-done.7 = bf16[64,56,384]{2,1,0:T(8,128)(2,1)S(1)} async-done(((bf16[64,56,384]{2,1,0:T(8,128)(2,1)}), bf16[64,56,384]{2,1,0:T(8,128)(2,1)S(1)}, u32[]{:S(2)}, u32[]{:S(2)}) %all-to-all-start.7) | async-done | bytes 2752544 | tf_op jit(solution)/shard_map/all_to_all | solution.py:53
  313.8 5.9 %whole_grad.2 = (f32[768,2304]{1,0:T(8,128)}, f32[768,128]{1,0:T(8,128)}, f32[768,768]{1,0:T(8,128)}) custom-call(s32[1]{0:T(128)} %bitcast.core_ref.side_ref, bf16[3584,384]{1,0:T(8,128)(2,1)} %bitcast.57, bf16[768,2304]{1,0:T(8,128)(2,1)} %weight_ref.3), custom_call_target="tpu_custom_call" | custom-call | flops 1769472 | bytes 7077888 | tf_op jit(solution)/shard_map/whole_grad/pallas_call | solution.py:455
  319.7 5.9 %whole_grad.3 = (f32[768,2304]{1,0:T(8,128)}, f32[768,128]{1,0:T(8,128)}, f32[768,768]{1,0:T(8,128)}) custom-call(s32[1]{0:T(128)S(6)} %sub.42.side_ref, bf16[3584,384]{1,0:T(8,128)(2,1)} %collective-permute-done.4.half_ref, bf16[768,2304]{1,0:T(8,128)(2,1)} %weight_ref.3, ...), custom_call_target="tpu_custom_call", output_to_operand_aliasing={{0}: (3, {}), {1}: (4, {}), {2}: (5, {})} | custom-call | flops 1769472 | bytes 7077888 | tf_op jit(solution)/shard_map/whole_grad/pallas_call | solution.py:455
  (139 shorter events, 69.1 us)
Async XLA Ops:
  7.2 16.4 %copy-start = (f32[32,12]{0,1:T(8,128)S(1)}, f32[32,12]{0,1:T(8,128)}, u32[]{:S(2)}) copy-start(f32[32,12]{0,1:T(8,128)} %param.16) | copy-start | bytes 4612
  7.2 101.6 %all-gather.3.cloned.1.call-start = ((), (), s32[]{:S(2)}) async-start(), calls=%async_computation.13 | async-start | bytes 11796480 | tf_op jit(solution)/shard_map/all_gather | solution.py:827
  12.2 8.7 %copy-start.27 = (s32[16]{0:T(128)S(1)}, s32[16]{0:T(128)}, u32[]{:S(2)}) copy-start(s32[16]{0:T(128)} %param.23) | copy-start | bytes 196
  12.2 10.6 %copy-start.25 = (s32[2048]{0:T(1024)S(1)}, s32[2048]{0:T(1024)}, u32[]{:S(2)}) copy-start(s32[2048]{0:T(1024)} %param.24) | copy-start | bytes 24580
  12.2 10.8 %copy-start.28 = (s32[1,128,2]{1,2,0:T(2,128)S(1)}, s32[1,128,2]{1,2,0:T(2,128)}, u32[]{:S(2)}) copy-start(s32[1,128,2]{1,2,0:T(2,128)} %param.22) | copy-start | bytes 3076
  12.2 13.1 %copy-start.23 = (f32[768]{0:T(1024)S(1)}, f32[768]{0:T(1024)}, u32[]{:S(2)}) copy-start(f32[768]{0:T(1024)} %param.14) | copy-start | bytes 9220
  12.2 29.1 %all-to-all-start = ((bf16[8,128,768]{2,1,0:T(8,128)(2,1)}), bf16[8,128,768]{2,1,0:T(8,128)(2,1)S(1)}, u32[]{:S(2)}, u32[]{:S(2)}) async-start(bf16[8,128,768]{2,1,0:T(8,128)(2,1)} %broadcast_in_dim.88), calls=%async_computation | async-start | bytes 3145728 | tf_op jit(solution)/shard_map/all_to_all | solution.py:53
  41.3 9.3 %collective-permute-start = (bf16[1024,768]{1,0:T(8,128)(2,1)S(1)}, bf16[1024,768]{1,0:T(8,128)(2,1)}, u32[]{:S(2)}, u32[]{:S(2)}) collective-permute-start(bf16[1024,768]{1,0:T(8,128)(2,1)S(1)} %bitcast.67), channel_id=1, source_target_pairs={{0,8},{8,0},{1,9},{9,1},{2,10},{10,2},{3,11},{11,3},{4,12},{12,4},... | collective-permute-start | bytes 4718600 | tf_op jit(solution)/shard_map/ppermute | solution.py:887
  42.6 7.2 %copy-start.24 = (bf16[768,32]{0,1:T(8,128)(2,1)S(1)}, bf16[768,32]{0,1:T(8,128)(2,1)}, u32[]{:S(2)}) copy-start(bf16[768,32]{0,1:T(8,128)(2,1)} %param.19) | copy-start | bytes 147460
  42.6 34.1 %all-to-all-start.2 = ((bf16[32,32,768]{2,1,0:T(8,128)(2,1)}), bf16[32,32,768]{2,1,0:T(8,128)(2,1)S(1)}, u32[]{:S(2)}, u32[]{:S(2)}) async-start(bf16[32,32,768]{2,1,0:T(8,128)(2,1)} %bitcast.10), calls=%async_computation.2 | async-start | bytes 3145728 | tf_op jit(solution)/shard_map/all_to_all | solution.py:53
  76.7 32.1 %copy-start.2 = (bf16[32,32,768]{2,1,0:T(8,128)(2,1)}, bf16[32,32,768]{2,1,0:T(8,128)(2,1)S(1)}, u32[]{:S(2)}) copy-start(bf16[32,32,768]{2,1,0:T(8,128)(2,1)S(1)} %all-to-all-done.2) | copy-start | bytes 4718596
  125.3 29.4 %all-to-all-start.3 = ((bf16[32,32,896]{2,1,0:T(8,128)(2,1)}), bf16[32,32,896]{2,1,0:T(8,128)(2,1)S(1)}, u32[]{:S(2)}, u32[]{:S(2)}) async-start(bf16[32,32,896]{2,1,0:T(8,128)(2,1)} %bitcast.65), calls=%async_computation.3 | async-start | bytes 3670016 | tf_op jit(solution)/shard_map/all_to_all | solution.py:53
  130.6 128.8 %reduce-scatter.3.cloned.1.call-start = ((), (), s32[]{:S(2)}) async-start(), calls=%async_computation.11 | async-start | bytes 5898240 | tf_op jit(solution)/shard_map/reduce_scatter | solution.py:908
  156.0 103.5 %reduce-scatter.5.cloned.1.call-start = ((), (), s32[]{:S(2)}) async-start(), calls=%async_computation.12 | async-start | bytes 5898240 | tf_op jit(solution)/shard_map/reduce_scatter | solution.py:908
  156.7 35.2 %all-to-all-start.4 = ((bf16[32,32,768]{2,1,0:T(8,128)(2,1)}), bf16[32,32,768]{2,1,0:T(8,128)(2,1)S(1)}, u32[]{:S(2)}, u32[]{:S(2)}) async-start(bf16[32,32,768]{2,1,0:T(8,128)(2,1)} %bitcast.15), calls=%async_computation.4 | async-start | bytes 3145728 | tf_op jit(solution)/shard_map/all_to_all | solution.py:53
  191.5 5.8 %collective-permute-start.1 = (bf16[1536,384]{1,0:T(8,128)(2,1)}, bf16[1536,384]{1,0:T(8,128)(2,1)}, u32[]{:S(2)}, u32[]{:S(2)}) collective-permute-start(bf16[1536,384]{1,0:T(8,128)(2,1)} %get-tuple-element.95), channel_id=1, source_target_pairs={{0,8},{8,0},{1,9},{9,1},{2,10},{10,2},{3,11},{11,3},{4,12},{12,4},... | collective-permute-start | bytes 3538952 | tf_op jit(solution)/shard_map/ppermute | solution.py:934
  197.0 3.6 %collective-permute-start.2 = (bf16[2048,384]{1,0:T(8,128)(2,1)}, bf16[2048,384]{1,0:T(8,128)(2,1)S(1)}, u32[]{:S(2)}, u32[]{:S(2)}) collective-permute-start(bf16[2048,384]{1,0:T(8,128)(2,1)} %get-tuple-element.106), channel_id=1, source_target_pairs={{0,8},{8,0},{1,9},{9,1},{2,10},{10,2},{3,11},{11,3},{4,12},{12,4},... | collective-permute-start | bytes 4718600 | tf_op jit(solution)/shard_map/ppermute | solution.py:950
  202.9 45.5 %all-to-all-start.5 = ((bf16[16,224,384]{2,1,0:T(8,128)(2,1)}), bf16[16,224,384]{2,1,0:T(8,128)(2,1)S(1)}, u32[]{:S(2)}, u32[]{:S(2)}) async-start(bf16[16,224,384]{2,1,0:T(8,128)(2,1)} %bitcast.59), calls=%async_computation.5 | async-start | bytes 5505024 | tf_op jit(solution)/shard_map/all_to_all | solution.py:53
  223.3 31.0 %collective-permute-start.3 = (bf16[1024,768]{1,0:T(8,128)(2,1)}, bf16[1024,768]{1,0:T(8,128)(2,1)}, u32[]{:S(2)}, u32[]{:S(2)}) collective-permute-start(bf16[1024,768]{1,0:T(8,128)(2,1)} %slice.77), channel_id=1, source_target_pairs={{0,8},{8,0},{1,9},{9,1},{2,10},{10,2},{3,11},{11,3},{4,12},{12,4},... | collective-permute-start | bytes 4718600 | tf_op jit(solution)/shard_map/ppermute | solution.py:957
  249.5 9.9 %all-to-all-start.6 = ((bf16[4,56,384]{2,1,0:T(8,128)(2,1)}), bf16[4,56,384]{2,1,0:T(8,128)(2,1)S(1)}, u32[]{:S(2)}, u32[]{:S(2)}) async-start(bf16[4,56,384]{2,1,0:T(8,128)(2,1)} %bitcast.18), calls=%async_computation.6 | async-start | bytes 344064 | tf_op jit(solution)/shard_map/all_to_all | solution.py:53
  261.2 43.8 %all-to-all-start.7 = ((bf16[64,56,384]{2,1,0:T(8,128)(2,1)}), bf16[64,56,384]{2,1,0:T(8,128)(2,1)S(1)}, u32[]{:S(2)}, u32[]{:S(2)}) async-start(bf16[64,56,384]{2,1,0:T(8,128)(2,1)} %broadcast_in_dim.100), calls=%async_computation.9 | async-start | bytes 5505024 | tf_op jit(solution)/shard_map/all_to_all | solution.py:53
  305.0 14.7 %collective-permute-start.4 = (bf16[3584,384]{1,0:T(8,128)(2,1)S(1)}, bf16[3584,384]{1,0:T(8,128)(2,1)}, u32[]{:S(2)}, u32[]{:S(2)}) collective-permute-start(bf16[3584,384]{1,0:T(8,128)(2,1)S(1)} %bitcast.56), channel_id=1, source_target_pairs={{0,8},{8,0},{1,9},{9,1},{2,10},{10,2},{3,11},{11,3},{4,12},{12,4},... | collective-permute-start | bytes 8257544 | tf_op jit(solution)/shard_map/ppermute | solution.py:972
  309.5 24.0 %all-to-all-start.8 = ((bf16[8,128,768]{2,1,0:T(8,128)(2,1)}), bf16[8,128,768]{2,1,0:T(8,128)(2,1)}, u32[]{:S(2)}, u32[]{:S(2)}) async-start(bf16[8,128,768]{2,1,0:T(8,128)(2,1)} %bitcast.64), calls=%async_computation.10 | async-start | bytes 3145728 | tf_op jit(solution)/shard_map/all_to_all | solution.py:53
  326.8 8.3 %copy-start.8 = (bf16[1,128,768]{2,1,0:T(8,128)(2,1)S(1)}, bf16[1,128,768]{2,1,0:T(8,128)(2,1)}, u32[]{:S(2)}) copy-start(bf16[1,128,768]{2,1,0:T(8,128)(2,1)} %param.13) | copy-start | bytes 589828
  (21 other events, 76.4 us)
Sparse Core Ops, SparseCore 0:
  10.3 95.1 all-gather.2
  154.9 50.5 reduce-scatter.2
  207.9 50.7 reduce-scatter.4
